TPU v7x, 32 devices: a whole 2x2x4 slice. The times are simulated.
32 devices in a mesh: pairs: 2 (over y), gx: 4 (over z), gy: 2 (over x), gz: 2 (over core).
Axes of the slice: x: 2, y: 2, z: 4, core: 2. Of those that a mesh axis runs over, the one named last changes fastest.
Arguments:
- sections: bfloat16 [2, 2048, 2048], P('gz', ('pairs', 'gy'), 'gx'), parts along dimension 1, may hold values from -16 to 16
- fine_offsets: int32 [4], P('pairs'), parts along dimension 0, may hold values from 0 to 31
- coarse_offset: int32 [2], P('pairs'), parts along dimension 0, may hold values from 0 to 63
- tissue_mask: int32 [64, 64], P(('pairs', 'gy'), 'gx'), parts along dimension 0, may hold values 0 or 1
Outputs:
- flow: float32 [2, 2, 64, 32], P(None, 'gz', ('pairs', 'gy'), 'gx'), parts along dimension 2
There are 2 independent parts, one for each index of `pairs`. A program takes and returns all parts, laid end to end along the dimension named above; each array names one. Nothing has to cross between parts.
All inputs are finite; a program needn't handle non-finite values. No bound on the sum of `tissue_mask` on one device may be relied on, other than what follows from the above.
Results may differ from a plain program's by a relative error of at most 0.00075.
Values may be sent and summed in bfloat16 or wider, within the bound.
No kernel may reach another device: no remote copies, remote signals or barrier semaphores. Data moves between devices by JAX's collectives and lax.ppermute only.
A program may use at most 64 MiB of HBM per device.

v0:
```python
import math

import jax
import jax.numpy as jnp
import numpy as np
from jax import lax
from jax.experimental import pallas as pl
from jax.experimental.pallas import tpu as pltpu
from jax.sharding import PartitionSpec as P

P_SIZE = 64
HALF = P_SIZE // 2
STRIDE = 32
DOWN = 8
LANES = 128
GROUP = LANES // HALF
SHARPNESS = 12.0
SCALE = SHARPNESS / float(P_SIZE) ** 4 * math.log2(math.e)

f32 = jnp.float32
bf16 = jnp.bfloat16


def basis_table():
    y = np.arange(P_SIZE)
    k = np.arange(HALF)
    angle = 2.0 * np.pi * (k[:, None] * y[None, :] % P_SIZE) / P_SIZE
    sines = np.sin(angle)
    sines[0] = np.cos(np.pi * y)
    return np.stack([np.cos(angle), sines])


def split_table(table):
    high = table.astype(jnp.bfloat16)
    low = (table - high.astype(np.float64)).astype(jnp.bfloat16)
    return high, low


def forward_columns_table():
    table = basis_table()
    halves = []
    for order in ((0, 1), (1, 0)):
        out = np.zeros((2, P_SIZE, 2, 2, HALF))
        for place, kind in enumerate(order):
            for patch in range(2):
                out[patch, :, place, patch, :] = table[kind].T
        halves.append(out.reshape(2 * P_SIZE, LANES))
    high_even, low_even = split_table(halves[0])
    high_odd, low_odd = split_table(halves[1])
    return np.concatenate([high_even, low_even, high_odd, low_odd], axis=1)


def inverse_columns_table():
    table = basis_table()
    out = np.zeros((2, GROUP, HALF, GROUP, P_SIZE))
    for patch in range(GROUP):
        out[:, patch, :, patch, :] = table
    return np.concatenate(split_table(out.reshape(2 * LANES, GROUP * P_SIZE)), axis=1)


def stacked_table(matrix):
    high, low = split_table(matrix)
    return np.block([[high, high], [low, np.zeros_like(low)]])


def forward_rows_table():
    return stacked_table(basis_table().reshape(P_SIZE, P_SIZE))


def inverse_rows_table():
    return stacked_table(basis_table().reshape(P_SIZE, P_SIZE).T)


def cosine_of_turns(turns):
    square = (turns * (2.0 * math.pi)) ** 2
    total = jnp.full_like(square, 1.0 / math.factorial(20))
    for n in range(9, -1, -1):
        total = total * square + (-1.0) ** n / math.factorial(2 * n)
    return total


def sine_of_turns(turns):
    angle = turns * (2.0 * math.pi)
    square = angle * angle
    total = jnp.full_like(square, -1.0 / math.factorial(19))
    for n in range(8, -1, -1):
        total = total * square + (-1.0) ** n / math.factorial(2 * n + 1)
    return total * angle


def nearest(turns):
    return turns - jnp.round(turns)


def basis_values(frequency, kind, place):
    nyquist = (kind == 1) & (frequency == 0)
    number = jnp.where(nyquist, HALF, frequency)
    quarter = jnp.where((kind == 1) & (frequency != 0), P_SIZE // 4, 0)
    step = (number * place - quarter) & (P_SIZE - 1)
    step = jnp.where(step > HALF, P_SIZE - step, step)
    flip = step > P_SIZE // 4
    step = jnp.where(flip, HALF - step, step)
    square = (step.astype(f32) * (2.0 * math.pi / P_SIZE)) ** 2
    total = jnp.full_like(square, 1.0 / math.factorial(12))
    for n in range(5, -1, -1):
        total = total * square + (-1.0) ** n / math.factorial(2 * n)
    return jnp.where(flip, -total, total)


def iota(shape, axis):
    return lax.broadcasted_iota(jnp.int32, shape, axis)


def split(values):
    high = values.astype(bf16)
    return high, (values - high.astype(f32)).astype(bf16)


def matmul(left, right):
    return jnp.dot(left, right, preferred_element_type=f32)


def add_row_halves(values):
    half = values.shape[0] // 2
    return values[:half] + values[half:]


def first_lane(shape):
    return iota(shape, 1) % HALF == 0


def half_spectra(cc, cs, sc, ss, first):
    shape = cc.shape
    l0 = first_lane(shape)
    if not first:
        return (
            cc - jnp.where(l0, 0.0, ss),
            sc + jnp.where(l0, 0.0, cs),
            jnp.where(l0, cs, cc + ss),
            jnp.where(l0, ss, sc - cs),
        )
    r0 = iota(shape, 0) == 0
    either = l0 | r0
    return (
        cc - jnp.where(either, 0.0, ss),
        jnp.where(r0, 0.0, sc) + jnp.where(l0, 0.0, cs),
        jnp.where(l0, cs, jnp.where(r0, sc, cc + ss)),
        jnp.where(either, ss, sc - cs),
    )


def cross_spectra(own, other, sign, first):
    a = half_spectra(*own, first)
    b = half_spectra(*other, first)
    out = []
    for r, i in ((0, 1), (2, 3)):
        out.append(b[r] * a[r] + b[i] * a[i])
        out.append(sign * (b[r] * a[i] - b[i] * a[r]))
    if first:
        shape = own[0].shape
        corner = first_lane(shape) & (iota(shape, 0) == 0)
        out = [jnp.where(corner, x * y, o) for x, y, o in zip(own, other, out)]
    return out


def coefficients(g, t, first):
    gpr, gpi, gmr, gmi = g
    tpr, tpi, tmr, tmi = t
    shape = gpr.shape
    l0 = first_lane(shape)
    hpr = gpr * tpr - gpi * tpi
    hpi = gpr * tpi + gpi * tpr
    hmr = gmr * tmr - gmi * tmi
    hmi = gmr * tmi + gmi * tmr
    if not first:
        return (
            hpr + jnp.where(l0, 0.0, hmr),
            jnp.where(l0, hmr, hmi - hpi),
            -hpi - jnp.where(l0, 0.0, hmi),
            jnp.where(l0, -hmi, hmr - hpr),
        )
    r0 = iota(shape, 0) == 0
    either = l0 | r0
    corner = l0 & r0
    out = (
        hpr + jnp.where(either, 0.0, hmr),
        jnp.where(l0, hmr, jnp.where(r0, 0.0, hmi) - hpi),
        jnp.where(r0, hmr, -hpi - jnp.where(l0, 0.0, hmi)),
        jnp.where(either, -hmi, hmr - hpr),
    )
    return [jnp.where(corner, x * y, o) for x, y, o in zip(g, t, out)]


def signed(number):
    return jnp.where(number >= HALF, number - P_SIZE, number).astype(f32)


def column_sums(logits):
    largest = jnp.max(logits, axis=0, keepdims=True)
    weights = jnp.exp2(logits - largest)
    rows = signed(iota((P_SIZE, 1), 0))
    return largest, jnp.sum(weights, axis=0, keepdims=True), jnp.sum(weights * rows, axis=0, keepdims=True)


def patch_peak(largest, total, moment, patch):
    window = slice(patch * P_SIZE, (patch + 1) * P_SIZE)
    top = largest[:, window]
    peak = jnp.max(top, axis=1, keepdims=True)
    factor = jnp.exp2(top - peak)
    weight = factor * total[:, window]
    columns = signed(iota((1, P_SIZE), 1))
    bottom = jnp.sum(weight, axis=1, keepdims=True)
    along_rows = jnp.sum(factor * moment[:, window], axis=1, keepdims=True)
    along_columns = jnp.sum(weight * columns, axis=1, keepdims=True)
    return along_rows / bottom, along_columns / bottom


ROW_PARTS = ((0, 8, True), (8, HALF, False))


def quads(block, group):
    lane = group * 2 * LANES
    top, bottom = block[:HALF], block[HALF:]
    return (
        top[:, lane : lane + LANES],
        top[:, lane + LANES : lane + 2 * LANES],
        bottom[:, lane : lane + LANES],
        bottom[:, lane + LANES : lane + 2 * LANES],
    )


def shrink_kernel(tile_ref, out_ref):
    rows, width = tile_ref.shape
    columns = width // DOWN
    pick = (iota((width, columns), 0) // DOWN == iota((width, columns), 1)).astype(bf16)
    sums = matmul(tile_ref[...], pick)
    out_ref[...] = (jnp.sum(sums.reshape(rows // DOWN, DOWN, columns), axis=1) / DOWN).astype(bf16)


def forward_kernel(
    offsets_ref,
    columns_ref,
    own_ref,
    own_low_ref,
    own_right_ref,
    other_ref,
    other_low_ref,
    other_right_ref,
    out_ref,
    image,
    weights,
    stacked,
):
    rows, width = own_ref.shape
    tall = rows + P_SIZE
    blocks = tall // STRIDE
    supers = width // (GROUP * P_SIZE)
    side = lax.axis_index("gz")
    row_offset = offsets_ref[0]
    column_offset = offsets_ref[1]
    for s, (main, low, right) in enumerate(
        ((own_ref, own_low_ref, own_right_ref), (other_ref, other_low_ref, other_right_ref))
    ):
        image[s, :rows, :width] = main[...]
        image[s, rows:, :width] = low[...]
        image[s, :, width:] = jnp.zeros((tall, LANES), bf16)
        image[s, :, width : width + P_SIZE] = right[...]
    padded = jnp.concatenate(
        [columns_ref[...].astype(f32), jnp.zeros((2 * P_SIZE, 4 * LANES), f32)], axis=0
    )
    for t in range(2):
        shift = column_offset + STRIDE * ((t + side) % 2)
        weights[t] = pltpu.roll(padded, shift, axis=0).astype(bf16)
    left = iota((tall, LANES), 1) < P_SIZE
    for s in range(2):
        for t in range(2):
            for g in range(supers):
                lane = g * 2 * LANES
                a = matmul(image[s, :, lane : lane + 2 * LANES], weights[t, :, : 2 * LANES])
                b = matmul(image[s, :, lane + LANES : lane + 3 * LANES], weights[t, :, 2 * LANES :])
                a = a[:, :LANES] + a[:, LANES:]
                b = b[:, :LANES] + b[:, LANES:]
                for part, value in enumerate(
                    (jnp.where(left, a, b), pltpu.roll(jnp.where(left, b, a), P_SIZE, axis=1))
                ):
                    high, low = split(value)
                    at = slice(lane + part * LANES, lane + (part + 1) * LANES)
                    for n in range(blocks):
                        block = slice(n * STRIDE, (n + 1) * STRIDE)
                        stacked[s, t, 2 * n * STRIDE : (2 * n + 1) * STRIDE, at] = high[block]
                        stacked[s, t, (2 * n + 1) * STRIDE : (2 * n + 2) * STRIDE, at] = low[block]
    shape = (P_SIZE, 6 * STRIDE)
    number = iota(shape, 0)
    lane = iota(shape, 1)
    place = lane // P_SIZE * STRIDE + lane % STRIDE - row_offset
    values = jnp.where(
        (place >= 0) & (place < P_SIZE), basis_values(number % HALF, number // HALF, place), 0.0
    )
    high, low = split(values)
    is_low = lane % P_SIZE >= STRIDE
    left_rows = jnp.concatenate([high, jnp.where(is_low, 0.0, low.astype(f32)).astype(bf16)], axis=0)
    sign = jnp.where(side == 0, 1.0, -1.0).astype(f32)
    for i in range(rows // STRIDE):
        spectra = []
        for s in range(2):
            window = stacked[s, i % 2, 2 * STRIDE * i : 2 * STRIDE * (i + 3), :]
            spectra.append(add_row_halves(matmul(left_rows, window)))
        for g in range(supers):
            lane = g * 2 * LANES
            own = quads(spectra[0], g)
            other = quads(spectra[1], g)
            for begin, end, first in ROW_PARTS:
                out = cross_spectra(
                    [x[begin:end] for x in own], [x[begin:end] for x in other], sign, first
                )
                out_ref[i, begin:end, lane : lane + LANES] = out[0]
                out_ref[i, begin:end, lane + LANES : lane + 2 * LANES] = out[1]
                out_ref[i, HALF + begin : HALF + end, lane : lane + LANES] = out[2]
                out_ref[i, HALF + begin : HALF + end, lane + LANES : lane + 2 * LANES] = out[3]


def inverse_columns(high, low, table_ref):
    table_high = table_ref[:, : 2 * LANES]
    table_low = table_ref[:, 2 * LANES :]
    return matmul(high, table_high) + matmul(high, table_low) + matmul(low, table_high)


def coarse_peaks(offset, pieces, sources, forward_rows_ref, inverse_ref, inverse_rows_ref, table, sign):
    count = len(pieces)
    supers = count // GROUP
    wide = supers * 2 * LANES
    shape = (P_SIZE, wide)
    lane = iota(shape, 1)
    patch = lane // (2 * LANES) * GROUP + lane % LANES // HALF
    place = iota(shape, 0) - offset - patch * P_SIZE
    for j in range(count):
        here = place + j * P_SIZE
        values = jnp.where(
            (here >= 0) & (here < P_SIZE),
            basis_values(lane % HALF, lane % (2 * LANES) // LANES, here),
            0.0,
        )
        high, low = split(values)
        table[j, :, :wide] = high
        table[j, :, wide:] = low
    strips = jnp.zeros((2 * P_SIZE, wide), f32)
    for piece, source in zip(pieces, sources):
        product = matmul(piece[...], table[source])
        strips = strips + (product[:, :wide] + product[:, wide:])
    spectra = []
    for s in range(2):
        high, low = split(strips[s * P_SIZE : (s + 1) * P_SIZE])
        stack = jnp.concatenate([high, low], axis=0)
        spectra.append(add_row_halves(matmul(forward_rows_ref[...], stack)))
    peaks = []
    for g in range(supers):
        own = quads(spectra[0], g)
        other = quads(spectra[1], g)
        parts = []
        for begin, end, first in ROW_PARTS:
            shape = (end - begin, LANES)
            values = cross_spectra([x[begin:end] for x in own], [x[begin:end] for x in other], sign, first)
            corner = first_lane(shape) & (iota(shape, 0) == 0) & first
            turn = [
                jnp.where(corner, SCALE, c).astype(f32)
                for c in (2.0 * SCALE, 0.0, 2.0 * SCALE, 0.0)
            ]
            parts.append(coefficients(values, turn, first))
        cc, cs, sc, ss = (jnp.concatenate([a, b], axis=0) for a, b in zip(*parts))
        block = jnp.concatenate(
            [jnp.concatenate([cc, cs], axis=1), jnp.concatenate([sc, ss], axis=1)], axis=0
        )
        high, low = split(block)
        high, low = split(inverse_columns(high, low, inverse_ref))
        stack = jnp.concatenate([high, low], axis=0)
        sums = column_sums(add_row_halves(matmul(inverse_rows_ref[...], stack)))
        peaks += [patch_peak(*sums, n) for n in range(GROUP)]
    return peaks


def peak_kernel(
    offsets_ref,
    coarse_offset_ref,
    mask_ref,
    forward_rows_ref,
    inverse_ref,
    inverse_rows_ref,
    spectra_ref,
    *refs,
):
    pieces, (out_ref, table, turns, high_ref, low_ref, stacked) = refs[:-6], refs[-6:]
    bands, _, wide = spectra_ref.shape
    supers = wide // (2 * LANES)
    per_row = supers * GROUP
    side = lax.axis_index("gz")
    place = lax.axis_index("gx")
    count = len(pieces)
    sign = jnp.where(side == 0, 1.0, -1.0).astype(f32)
    sources = [exchange_source(place, step, count) for step in range(count)]
    column_offset = offsets_ref[1]
    coarse_offset = coarse_offset_ref[0]
    peaks = coarse_peaks(
        coarse_offset, pieces, sources, forward_rows_ref, inverse_ref, inverse_rows_ref, table, sign
    )
    blended = []
    for axis in range(2):
        values = [peak[axis] for peak in peaks]
        mean = sum(values[1:], values[0]) / count
        blended.append([(0.5 * DOWN) * (value + mean) for value in values])

    def prior(column):
        centre = (place * (2 * per_row) + column) * STRIDE + column_offset + P_SIZE // 2
        pick = jnp.clip((centre // DOWN - coarse_offset) // P_SIZE, 0, count - 1)
        out = []
        for values in blended:
            chosen = jnp.broadcast_to(values[0], column.shape)
            for j in range(1, count):
                chosen = jnp.where(pick == j, values[j], chosen)
            out.append(chosen)
        return out

    shape = (HALF, LANES)
    frequency_y = iota(shape, 0).astype(f32) / P_SIZE
    l0 = first_lane(shape)
    r0 = iota(shape, 0) == 0
    lane_row = iota((1, LANES), 1)
    frequency_x = (lane_row % HALF).astype(f32) / P_SIZE
    for t in range(2):
        for g in range(supers):
            column = 2 * (g * GROUP + lane_row // HALF) + (t + side) % 2
            dy, dx = (value - P_SIZE * jnp.round(value / P_SIZE) for value in prior(column))
            turn_y = nearest(frequency_y * dy)
            turn_x = nearest(frequency_x * dx)
            cy, sy = cosine_of_turns(turn_y), sine_of_turns(turn_y)
            cx, sx = cosine_of_turns(turn_x), sine_of_turns(turn_x)
            half_y = cosine_of_turns(nearest(0.5 * dy))
            half_x = cosine_of_turns(nearest(0.5 * dx))
            half_both = cosine_of_turns(nearest(0.5 * (dy + dx)))
            plus_real = cy * cx - sy * sx
            plus_imaginary = sy * cx + cy * sx
            minus_real = cy * cx + sy * sx
            minus_imaginary = sy * cx - cy * sx
            minus_real = jnp.where(l0, cy * half_x, jnp.where(r0, cx * half_y, minus_real))
            minus_imaginary = jnp.where(l0, sy * half_x, jnp.where(r0, sx * half_y, minus_imaginary))
            corner = l0 & r0
            turn = (plus_real, plus_imaginary, minus_real, minus_imaginary)
            ends = (1.0, half_x, half_y, half_both)
            for n in range(4):
                turns[t, g, n] = SCALE * jnp.where(corner, ends[n], 2.0 * turn[n])
    for i in range(bands):
        block = spectra_ref[i]
        for g in range(supers):
            lane = g * 2 * LANES
            values = quads(block, g)
            for begin, end, first in ROW_PARTS:
                parts = coefficients(
                    [x[begin:end] for x in values],
                    [turns[i % 2, g, n, begin:end] for n in range(4)],
                    first,
                )
                stacked[begin:end, lane : lane + LANES] = parts[0]
                stacked[begin:end, lane + LANES : lane + 2 * LANES] = parts[1]
                stacked[HALF + begin : HALF + end, lane : lane + LANES] = parts[2]
                stacked[HALF + begin : HALF + end, lane + LANES : lane + 2 * LANES] = parts[3]
        high, low = split(stacked[...])
        high_ref[i * P_SIZE : (i + 1) * P_SIZE] = high
        low_ref[i * P_SIZE : (i + 1) * P_SIZE] = low
    for g in range(supers):
        at = slice(g * 2 * LANES, (g + 1) * 2 * LANES)
        high, low = split(inverse_columns(high_ref[:, at], low_ref[:, at], inverse_ref))
        high_ref[:, at] = high
        low_ref[:, at] = low
    sums = []
    for i in range(bands):
        rows = slice(i * P_SIZE, (i + 1) * P_SIZE)
        stack = jnp.concatenate([high_ref[rows], low_ref[rows]], axis=0)
        sums.append(column_sums(add_row_halves(matmul(inverse_rows_ref[...], stack))))
    sums = [jnp.concatenate(parts, axis=0) for parts in zip(*sums)]
    shape = (bands, per_row)
    lane = iota(shape, 1)
    parity = (iota(shape, 0) + side) % 2
    found = [jnp.zeros(shape, f32) for _ in range(2)]
    for m in range(per_row):
        peak = patch_peak(*sums, m)
        found = [jnp.where(lane == m, p, x) for p, x in zip(peak, found)]
    shape = (2 * per_row, per_row)
    columns = iota(shape, 0) - 2 * iota(shape, 1)
    mask = mask_ref[...].astype(f32).astype(bf16)
    masks = [matmul(mask, (columns == n).astype(bf16)) for n in range(2)]
    chosen = jnp.where(parity == 0, masks[0], masks[1])
    base = prior(2 * lane + parity)
    for axis in range(2):
        out_ref[axis] = base[axis] + chosen * found[axis]


def exchange_source(place, step, count):
    if count & (count - 1) == 0:
        return place ^ step
    return lax.rem(place + count - step, count)


def exchanged(value, axis, step):
    count = lax.axis_size(axis)
    if count & (count - 1) == 0:
        pairs = [(i, i ^ step) for i in range(count)]
    else:
        pairs = [(i, (i + step) % count) for i in range(count)]
    return lax.ppermute(value, axis, pairs)


def from_next(value, axis):
    count = lax.axis_size(axis)
    return lax.ppermute(value, axis, [(i, i - 1) for i in range(1, count)])


def swapped(value):
    return lax.ppermute(value, "gz", [(0, 1), (1, 0)])


VMEM = pl.BlockSpec(memory_space=pltpu.VMEM)
SMEM = pl.BlockSpec(memory_space=pltpu.SMEM)


def params(mebibytes):
    return pltpu.CompilerParams(vmem_limit_bytes=mebibytes * 2**20)


def local(sections, fine_offsets, coarse_offset, tissue_mask):
    own = sections[0]
    rows, width = own.shape
    bands = rows // STRIDE
    per_row = width // P_SIZE
    tall = rows + P_SIZE
    count = lax.axis_size("gx")
    assert rows == DOWN * P_SIZE and width == DOWN * P_SIZE and count % GROUP == 0
    wide = 2 * width // 2
    supers = width // (2 * LANES)
    coarse_wide = count // GROUP * 2 * LANES
    own_low = from_next(own[:P_SIZE], "gy")
    own_right = from_next(jnp.concatenate([own[:, :P_SIZE], own_low[:, :P_SIZE]], axis=0), "gx")
    other = swapped(own)
    other_low = swapped(own_low)
    other_right = swapped(own_right)
    coarse = pl.pallas_call(
        shrink_kernel,
        out_shape=jax.ShapeDtypeStruct((rows // DOWN, width // DOWN), bf16),
        in_specs=[VMEM],
        out_specs=VMEM,
        compiler_params=params(16),
    )(own)
    both = jnp.concatenate([coarse, swapped(coarse)], axis=0)
    pieces = [both] + [exchanged(both, "gx", step) for step in range(1, count)]
    spectra = pl.pallas_call(
        forward_kernel,
        out_shape=jax.ShapeDtypeStruct((bands, P_SIZE, wide), f32),
        in_specs=[SMEM] + [VMEM] * 7,
        out_specs=VMEM,
        scratch_shapes=[
            pltpu.VMEM((2, tall, width + LANES), bf16),
            pltpu.VMEM((2, 2 * LANES, 4 * LANES), bf16),
            pltpu.VMEM((2, 2, 2 * tall, wide), bf16),
        ],
        compiler_params=params(32),
    )(
        fine_offsets,
        jnp.asarray(forward_columns_table()),
        own,
        own_low,
        own_right,
        other,
        other_low,
        other_right,
    )
    flow = pl.pallas_call(
        peak_kernel,
        out_shape=jax.ShapeDtypeStruct((2, bands, per_row), f32),
        in_specs=[SMEM, SMEM] + [VMEM] * (5 + count),
        out_specs=VMEM,
        scratch_shapes=[
            pltpu.VMEM((count, P_SIZE, 2 * coarse_wide), bf16),
            pltpu.VMEM((2, supers, 4, HALF, LANES), f32),
            pltpu.VMEM((bands * P_SIZE, wide), bf16),
            pltpu.VMEM((bands * P_SIZE, wide), bf16),
            pltpu.VMEM((P_SIZE, wide), f32),
        ],
        compiler_params=params(40),
    )(
        fine_offsets,
        coarse_offset,
        tissue_mask,
        jnp.asarray(forward_rows_table()),
        jnp.asarray(inverse_columns_table()),
        jnp.asarray(inverse_rows_table()),
        spectra,
        *pieces,
    )
    return flow.reshape(2, 1, bands, per_row)


def solution(mesh):
    placed = (P("gz", ("pairs", "gy"), "gx"), P("pairs"), P("pairs"), P(("pairs", "gy"), "gx"))
    return jax.shard_map(
        local,
        mesh=mesh,
        in_specs=placed,
        out_specs=P(None, "gz", ("pairs", "gy"), "gx"),
        check_vma=False,
    )
```

profile of v0, /device:TPU:0, one launch (start us, length us, event | category | flops | bytes accessed | tf_op | source)
XLA Modules:
  0.0 33.0 jit_solution(15008299144249707892)
XLA Ops:
  0.0 0.5 %collective-permute-start.2 = (bf16[512,512]{1,0:T(8,128)(2,1)}, bf16[512,512]{1,0:T(8,128)(2,1)S(1)}, u32[]{:S(2)}, u32[]{:S(2)}) collective-permute-start(bf16[512,512]{1,0:T(8,128)(2,1)} %bitcast.4), channel_id=1, source_target_pairs={{0,1},{1,0},{2,3},{3,2},{4,5},{5,4},{6,7},{7,6},{8,9},{9,8},{10,11... | collective-permute-start | bytes 1572872 | tf_op jit(solution)/shard_map/ppermute | solution.py:517
  0.5 0.8 %slice_bitcast_fusion = bf16[64,512]{1,0:T(8,128)(2,1)S(1)} fusion(bf16[1,512,512]{2,1,0:T(8,128)(2,1)} %param.8), kind=kLoop, calls=%fused_computation.1 | loop fusion | bytes 131072 | tf_op jit(solution)/shard_map/slice | solution.py:539
  1.3 1.3 %collective-permute-start = (bf16[64,512]{1,0:T(8,128)(2,1)S(1)}, bf16[64,512]{1,0:T(8,128)(2,1)S(1)}, u32[]{:S(2)}, u32[]{:S(2)}) collective-permute-start(bf16[64,512]{1,0:T(8,128)(2,1)S(1)} %slice_bitcast_fusion), channel_id=1, source_target_pairs={{2,0},{3,1},{6,4},{7,5},{10,8},{11,9},{14,12},{15,13},{18,16},{19,... | collective-permute-start | bytes 196616 | tf_op jit(solution)/shard_map/ppermute | solution.py:513
  2.6 0.9 %slice.16 = bf16[512,64]{1,0:T(8,128)(2,1)S(1)} slice(bf16[512,512]{1,0:T(8,128)(2,1)} %bitcast.5), slice={[0:512], [0:64]} | slice | bytes 131072 | tf_op jit(solution)/shard_map/slice | solution.py:540
  3.5 4.3 %collective-permute-done.own_low_ref = bf16[64,512]{1,0:T(8,128)(2,1)S(1)} collective-permute-done((bf16[64,512]{1,0:T(8,128)(2,1)S(1)}, bf16[64,512]{1,0:T(8,128)(2,1)S(1)}, u32[]{:S(2)}, u32[]{:S(2)}) %collective-permute-start) | collective-permute-done | bytes 65568 | tf_op jit(solution)/shard_map/ppermute | solution.py:513
  7.9 1.3 %collective-permute-start.1 = (bf16[576,64]{1,0:T(8,128)(2,1)S(1)}, bf16[576,64]{1,0:T(8,128)(2,1)S(1)}, u32[]{:S(2)}, u32[]{:S(2)}) collective-permute-start(bf16[576,64]{1,0:T(8,128)(2,1)S(1)} %pad_maximum_fusion), channel_id=1, source_target_pairs={{4,0},{8,4},{12,8},{5,1},{9,5},{13,9},{6,2},{10,6},{14,10},{7,3},{... | collective-permute-start | bytes 221192 | tf_op jit(solution)/shard_map/ppermute | solution.py:513
  9.2 0.0 copy-start
  9.2 1.0 %copy-done = bf16[1,512,512]{2,1,0:T(8,128)(2,1)S(1)} copy-done((bf16[1,512,512]{2,1,0:T(8,128)(2,1)S(1)}, bf16[1,512,512]{2,1,0:T(8,128)(2,1)}, u32[]{:S(2)}) %copy-start) | copy-done | bytes 524312
  10.2 0.0 copy-start.2
  10.2 0.0 copy-start.4
  10.2 0.0 copy-start.5
  10.2 0.0 copy-start.6
  10.2 0.0 copy-start.8
  10.2 0.3 shard_map.83
  10.5 0.1 collective-permute-start.5
  10.6 0.5 %collective-permute-start.3 = (bf16[64,512]{1,0:T(8,128)(2,1)S(1)}, bf16[64,512]{1,0:T(8,128)(2,1)S(1)}, u32[]{:S(2)}, u32[]{:S(2)}) collective-permute-start(bf16[64,512]{1,0:T(8,128)(2,1)S(1)} %collective-permute-done.own_low_ref), channel_id=1, source_target_pairs={{0,1},{1,0},{2,3},{3,2},{4,5},{5,4},{6,7},{7,6},{8,9},{9,8},{10,11... | collective-permute-start | bytes 196616 | tf_op jit(solution)/shard_map/ppermute | solution.py:517
  11.1 4.8 %collective-permute-done.1.own_right_ref = bf16[576,64]{1,0:T(8,128)(2,1)S(1)} collective-permute-done((bf16[576,64]{1,0:T(8,128)(2,1)S(1)}, bf16[576,64]{1,0:T(8,128)(2,1)S(1)}, u32[]{:S(2)}, u32[]{:S(2)}) %collective-permute-start.1) | collective-permute-done | bytes 73760 | tf_op jit(solution)/shard_map/ppermute | solution.py:513
  15.9 0.0 collective-permute-start.4
  15.9 0.0 collective-permute-done.5
  16.0 1.8 %collective-permute-start.6 = (bf16[128,64]{1,0:T(8,128)(2,1)S(1)}, bf16[128,64]{1,0:T(8,128)(2,1)S(1)}, u32[]{:S(2)}, u32[]{:S(2)}) collective-permute-start(bf16[128,64]{1,0:T(8,128)(2,1)S(1)} %pad_maximum_fusion.1.refs_0_), channel_id=1, source_target_pairs={{0,4},{4,0},{8,12},{12,8},{1,5},{5,1},{9,13},{13,9},{2,6},{6,2},{1... | collective-permute-start | bytes 49160 | tf_op jit(solution)/shard_map/ppermute | solution.py:508
  17.8 1.1 %collective-permute-start.7 = (bf16[128,64]{1,0:T(8,128)(2,1)S(1)}, bf16[128,64]{1,0:T(8,128)(2,1)S(1)}, u32[]{:S(2)}, u32[]{:S(2)}) collective-permute-start(bf16[128,64]{1,0:T(8,128)(2,1)S(1)} %pad_maximum_fusion.1.refs_0_), channel_id=1, source_target_pairs={{0,8},{4,12},{8,0},{12,4},{1,9},{5,13},{9,1},{13,5},{2,10},{6,14},... | collective-permute-start | bytes 49160 | tf_op jit(solution)/shard_map/ppermute | solution.py:508
  18.8 0.0 collective-permute-done.3.other_low_ref
  18.9 1.6 %collective-permute-start.8 = (bf16[128,64]{1,0:T(8,128)(2,1)S(1)}, bf16[128,64]{1,0:T(8,128)(2,1)S(1)}, u32[]{:S(2)}, u32[]{:S(2)}) collective-permute-start(bf16[128,64]{1,0:T(8,128)(2,1)S(1)} %pad_maximum_fusion.1.refs_0_), channel_id=1, source_target_pairs={{0,12},{4,8},{8,4},{12,0},{1,13},{5,9},{9,5},{13,1},{2,14},{6,10},... | collective-permute-start | bytes 49160 | tf_op jit(solution)/shard_map/ppermute | solution.py:508
  21.1 0.0 collective-permute-done.4.other_right_ref
  21.1 0.0 collective-permute-done.2.other_ref
  21.1 0.0 copy-start.1
  21.1 1.0 %copy-done.1 = bf16[1,512,512]{2,1,0:T(8,128)(2,1)S(1)} copy-done((bf16[1,512,512]{2,1,0:T(8,128)(2,1)S(1)}, bf16[1,512,512]{2,1,0:T(8,128)(2,1)}, u32[]{:S(2)}) %copy-start.1) | copy-done | bytes 524312
  22.1 0.0 copy-start.3
  22.1 0.9 %copy-done.3 = bf16[128,512]{1,0:T(8,128)(2,1)S(1)} copy-done((bf16[128,512]{1,0:T(8,128)(2,1)S(1)}, bf16[128,512]{1,0:T(8,128)(2,1)}, u32[]{:S(2)}) %copy-start.3) | copy-done | bytes 131096
  23.0 0.0 copy-start.7
  23.0 0.7 %copy-done.7 = s32[2]{0:T(128)S(1)} copy-done((s32[2]{0:T(128)S(1)}, s32[2]{0:T(128)}, u32[]{:S(2)}) %copy-start.7) | copy-done | bytes 32
  23.7 3.8 %shard_map.82.spectra_ref = f32[16,64,512]{2,1,0:T(8,128)S(1)} custom-call(s32[2]{0:T(128)S(1)} %copy-done.7, bf16[128,512]{1,0:T(8,128)(2,1)S(1)} %copy-done.3, bf16[512,512]{1,0:T(8,128)(2,1)S(1)} %bitcast.7, bf16[64,512]{1,0:T(8,128)(2,1)S(1)} %collective-permute-done.own_low_ref, bf16[576,64]{1,0:T(8,128)(2,1)S(1)} %collective-permute-done.1.own_right_ref, ...), custom_call_target="tpu_custom_call" | custom-call | tf_op jit(solution)/shard_map/pallas_call | solution.py:553
  27.5 0.0 collective-permute-done.6.refs_1_
  27.5 0.0 collective-permute-done.7.refs_2_
  27.5 0.0 collective-permute-done.8.refs_3_
  27.5 0.0 copy-done.2
  27.5 0.0 copy-done.4
  27.5 0.0 copy-done.5
  27.5 0.0 copy-done.6
  27.6 0.0 copy-done.8
  27.6 4.7 %shard_map.84 = f32[2,16,8]{2,1,0:T(8,128)S(1)} custom-call(s32[2]{0:T(128)S(1)} %copy-done.8, s32[1]{0:T(128)S(6)} %copy.10.coarse_offset_ref, s32[16,16]{1,0:T(8,128)S(1)} %copy-done.6, bf16[128,128]{1,0:T(8,128)(2,1)S(1)} %copy-done.5, bf16[256,512]{1,0:T(8,128)(2,1)S(1)} %copy-done.2, bf16[128,128]{1,0:T(8,128)(2,1)S(1)} %copy-done.4, ...), custom_call_target="tpu_custom_call" | custom-call | tf_op jit(solution)/shard_map/pallas_call | solution.py:574
  32.3 0.7 %copy.9 = f32[2,1,16,8]{2,3,1,0:T(8,128)} copy(f32[2,1,16,8]{3,2,0,1:T(8,128)S(1)} %bitcast.8) | data formatting | bytes 2048 | tf_op jit(solution)/shard_map/reshape | solution.py:597
  (3 shorter events, 0.0 us)
Async XLA Ops:
  0.0 21.1 %collective-permute-start.2 = (bf16[512,512]{1,0:T(8,128)(2,1)}, bf16[512,512]{1,0:T(8,128)(2,1)S(1)}, u32[]{:S(2)}, u32[]{:S(2)}) collective-permute-start(bf16[512,512]{1,0:T(8,128)(2,1)} %bitcast.4), channel_id=1, source_target_pairs={{0,1},{1,0},{2,3},{3,2},{4,5},{5,4},{6,7},{7,6},{8,9},{9,8},{10,11... | collective-permute-start | bytes 1572872 | tf_op jit(solution)/shard_map/ppermute | solution.py:517
  1.3 6.5 %collective-permute-start = (bf16[64,512]{1,0:T(8,128)(2,1)S(1)}, bf16[64,512]{1,0:T(8,128)(2,1)S(1)}, u32[]{:S(2)}, u32[]{:S(2)}) collective-permute-start(bf16[64,512]{1,0:T(8,128)(2,1)S(1)} %slice_bitcast_fusion), channel_id=1, source_target_pairs={{2,0},{3,1},{6,4},{7,5},{10,8},{11,9},{14,12},{15,13},{18,16},{19,... | collective-permute-start | bytes 196616 | tf_op jit(solution)/shard_map/ppermute | solution.py:513
  7.9 8.1 %collective-permute-start.1 = (bf16[576,64]{1,0:T(8,128)(2,1)S(1)}, bf16[576,64]{1,0:T(8,128)(2,1)S(1)}, u32[]{:S(2)}, u32[]{:S(2)}) collective-permute-start(bf16[576,64]{1,0:T(8,128)(2,1)S(1)} %pad_maximum_fusion), channel_id=1, source_target_pairs={{4,0},{8,4},{12,8},{5,1},{9,5},{13,9},{6,2},{10,6},{14,10},{7,3},{... | collective-permute-start | bytes 221192 | tf_op jit(solution)/shard_map/ppermute | solution.py:513
  9.2 1.0 %copy-start = (bf16[1,512,512]{2,1,0:T(8,128)(2,1)S(1)}, bf16[1,512,512]{2,1,0:T(8,128)(2,1)}, u32[]{:S(2)}) copy-start(bf16[1,512,512]{2,1,0:T(8,128)(2,1)} %param.8) | copy-start | bytes 1572868
  10.2 17.3 %copy-start.2 = (bf16[256,512]{1,0:T(8,128)(2,1)S(1)}, bf16[256,512]{1,0:T(8,128)(2,1)}, u32[]{:S(2)}) copy-start(bf16[256,512]{1,0:T(8,128)(2,1)} %constant.10.clone.inverse_ref) | copy-start | bytes 786436
  10.2 17.3 %copy-start.4 = (bf16[128,128]{1,0:T(8,128)(2,1)S(1)}, bf16[128,128]{1,0:T(8,128)(2,1)}, u32[]{:S(2)}) copy-start(bf16[128,128]{1,0:T(8,128)(2,1)} %constant.11.clone.inverse_rows_ref) | copy-start | bytes 98308
  10.2 17.3 %copy-start.5 = (bf16[128,128]{1,0:T(8,128)(2,1)S(1)}, bf16[128,128]{1,0:T(8,128)(2,1)}, u32[]{:S(2)}) copy-start(bf16[128,128]{1,0:T(8,128)(2,1)} %constant.9.clone.forward_rows_ref) | copy-start | bytes 98308
  10.2 17.3 %copy-start.6 = (s32[16,16]{1,0:T(8,128)S(1)}, s32[16,16]{1,0:T(8,128)}, u32[]{:S(2)}) copy-start(s32[16,16]{1,0:T(8,128)} %mask_ref.1) | copy-start | bytes 3076
  10.2 17.4 %copy-start.8 = (s32[2]{0:T(128)S(1)}, s32[2]{0:T(128)}, u32[]{:S(2)}) copy-start(s32[2]{0:T(128)} %offsets_ref.3) | copy-start | bytes 28
  10.5 5.4 %collective-permute-start.5 = (bf16[64,64]{1,0:T(8,128)(2,1)S(1)}, bf16[64,64]{1,0:T(8,128)(2,1)S(1)}, u32[]{:S(2)}, u32[]{:S(2)}) collective-permute-start(bf16[64,64]{1,0:T(8,128)(2,1)S(1)} %shard_map.83), channel_id=1, source_target_pairs={{0,1},{1,0},{2,3},{3,2},{4,5},{5,4},{6,7},{7,6},{8,9},{9,8},{10,11... | collective-permute-start | bytes 24584 | tf_op jit(solution)/shard_map/ppermute | solution.py:517
  10.6 8.2 %collective-permute-start.3 = (bf16[64,512]{1,0:T(8,128)(2,1)S(1)}, bf16[64,512]{1,0:T(8,128)(2,1)S(1)}, u32[]{:S(2)}, u32[]{:S(2)}) collective-permute-start(bf16[64,512]{1,0:T(8,128)(2,1)S(1)} %collective-permute-done.own_low_ref), channel_id=1, source_target_pairs={{0,1},{1,0},{2,3},{3,2},{4,5},{5,4},{6,7},{7,6},{8,9},{9,8},{10,11... | collective-permute-start | bytes 196616 | tf_op jit(solution)/shard_map/ppermute | solution.py:517
  15.9 5.1 %collective-permute-start.4 = (bf16[576,64]{1,0:T(8,128)(2,1)S(1)}, bf16[576,64]{1,0:T(8,128)(2,1)S(1)}, u32[]{:S(2)}, u32[]{:S(2)}) collective-permute-start(bf16[576,64]{1,0:T(8,128)(2,1)S(1)} %collective-permute-done.1.own_right_ref), channel_id=1, source_target_pairs={{0,1},{1,0},{2,3},{3,2},{4,5},{5,4},{6,7},{7,6},{8,9},{9,8},{10,11... | collective-permute-start | bytes 221192 | tf_op jit(solution)/shard_map/ppermute | solution.py:517
  16.0 11.5 %collective-permute-start.6 = (bf16[128,64]{1,0:T(8,128)(2,1)S(1)}, bf16[128,64]{1,0:T(8,128)(2,1)S(1)}, u32[]{:S(2)}, u32[]{:S(2)}) collective-permute-start(bf16[128,64]{1,0:T(8,128)(2,1)S(1)} %pad_maximum_fusion.1.refs_0_), channel_id=1, source_target_pairs={{0,4},{4,0},{8,12},{12,8},{1,5},{5,1},{9,13},{13,9},{2,6},{6,2},{1... | collective-permute-start | bytes 49160 | tf_op jit(solution)/shard_map/ppermute | solution.py:508
  17.8 9.7 %collective-permute-start.7 = (bf16[128,64]{1,0:T(8,128)(2,1)S(1)}, bf16[128,64]{1,0:T(8,128)(2,1)S(1)}, u32[]{:S(2)}, u32[]{:S(2)}) collective-permute-start(bf16[128,64]{1,0:T(8,128)(2,1)S(1)} %pad_maximum_fusion.1.refs_0_), channel_id=1, source_target_pairs={{0,8},{4,12},{8,0},{12,4},{1,9},{5,13},{9,1},{13,5},{2,10},{6,14},... | collective-permute-start | bytes 49160 | tf_op jit(solution)/shard_map/ppermute | solution.py:508
  18.9 8.7 %collective-permute-start.8 = (bf16[128,64]{1,0:T(8,128)(2,1)S(1)}, bf16[128,64]{1,0:T(8,128)(2,1)S(1)}, u32[]{:S(2)}, u32[]{:S(2)}) collective-permute-start(bf16[128,64]{1,0:T(8,128)(2,1)S(1)} %pad_maximum_fusion.1.refs_0_), channel_id=1, source_target_pairs={{0,12},{4,8},{8,4},{12,0},{1,13},{5,9},{9,5},{13,1},{2,14},{6,10},... | collective-permute-start | bytes 49160 | tf_op jit(solution)/shard_map/ppermute | solution.py:508
  21.1 1.0 %copy-start.1 = (bf16[1,512,512]{2,1,0:T(8,128)(2,1)S(1)}, bf16[1,512,512]{2,1,0:T(8,128)(2,1)}, u32[]{:S(2)}) copy-start(bf16[1,512,512]{2,1,0:T(8,128)(2,1)} %param.8) | copy-start | bytes 1572868
  22.1 0.9 %copy-start.3 = (bf16[128,512]{1,0:T(8,128)(2,1)S(1)}, bf16[128,512]{1,0:T(8,128)(2,1)}, u32[]{:S(2)}) copy-start(bf16[128,512]{1,0:T(8,128)(2,1)} %constant.8.clone.columns_ref) | copy-start | bytes 393220
  23.0 0.7 %copy-start.7 = (s32[2]{0:T(128)S(1)}, s32[2]{0:T(128)}, u32[]{:S(2)}) copy-start(s32[2]{0:T(128)} %offsets_ref.3) | copy-start | bytes 28
where the time goes:
time: 33.3 us; the launch traced here: 33 us
  waiting for transfers between devices  9.15 us (27%)
  Pallas kernels  8.82 us (26%)
  starting transfers between devices  8.05 us (24%)
  local copies, waits for them, and re-layouts  6.08 us (18%)
  between operations  0.83 us (2%)
    ppermute x2, waiting for transfers between devices, from_next(): return lax.ppermute(value, axis, [(i, i - 1) for i in range(1, count)])  9.13 us
    pallas_call x1, Pallas kernels, local(): pl.pallas_call(peak_kernel, out_shape=jax.ShapeDtypeStruct((2, bands, per...  4.72 us
    ppermute x3, starting transfers between devices, exchanged(): return lax.ppermute(value, axis, pairs)  4.45 us
    pallas_call x1, Pallas kernels, local(): pl.pallas_call(forward_kernel, out_shape=jax.ShapeDtypeStruct((bands, P_S...  3.79 us
    unnamed x18, local copies, waits for them, and re-layouts  3.65 us
    ppermute x2, starting transfers between devices, from_next(): return lax.ppermute(value, axis, [(i, i - 1) for i in range(1, count)])  2.57 us
    ppermute x4, starting transfers between devices, swapped(): return lax.ppermute(value, 'gz', [(0, 1), (1, 0)])  1.02 us
    slice x1, local copies, waits for them, and re-layouts, local(): own[:, :P_SIZE]  0.92 us
  transfers between devices with their start and end apart: 9, of which 2 were waited for; matrix products, arithmetic and copies ran while one was open for 5% of the time, Pallas kernels for 12%

commit v1 on v0

--- a/solution.py
+++ b/solution.py
@@ -2,7 +2,6 @@
 
 import jax
 import jax.numpy as jnp
-import numpy as np
 from jax import lax
 from jax.experimental import pallas as pl
 from jax.experimental.pallas import tpu as pltpu
@@ -19,56 +18,6 @@
 
 f32 = jnp.float32
 bf16 = jnp.bfloat16
-
-
-def basis_table():
-    y = np.arange(P_SIZE)
-    k = np.arange(HALF)
-    angle = 2.0 * np.pi * (k[:, None] * y[None, :] % P_SIZE) / P_SIZE
-    sines = np.sin(angle)
-    sines[0] = np.cos(np.pi * y)
-    return np.stack([np.cos(angle), sines])
-
-
-def split_table(table):
-    high = table.astype(jnp.bfloat16)
-    low = (table - high.astype(np.float64)).astype(jnp.bfloat16)
-    return high, low
-
-
-def forward_columns_table():
-    table = basis_table()
-    halves = []
-    for order in ((0, 1), (1, 0)):
-        out = np.zeros((2, P_SIZE, 2, 2, HALF))
-        for place, kind in enumerate(order):
-            for patch in range(2):
-                out[patch, :, place, patch, :] = table[kind].T
-        halves.append(out.reshape(2 * P_SIZE, LANES))
-    high_even, low_even = split_table(halves[0])
-    high_odd, low_odd = split_table(halves[1])
-    return np.concatenate([high_even, low_even, high_odd, low_odd], axis=1)
-
-
-def inverse_columns_table():
-    table = basis_table()
-    out = np.zeros((2, GROUP, HALF, GROUP, P_SIZE))
-    for patch in range(GROUP):
-        out[:, patch, :, patch, :] = table
-    return np.concatenate(split_table(out.reshape(2 * LANES, GROUP * P_SIZE)), axis=1)
-
-
-def stacked_table(matrix):
-    high, low = split_table(matrix)
-    return np.block([[high, high], [low, np.zeros_like(low)]])
-
-
-def forward_rows_table():
-    return stacked_table(basis_table().reshape(P_SIZE, P_SIZE))
-
-
-def inverse_rows_table():
-    return stacked_table(basis_table().reshape(P_SIZE, P_SIZE).T)
 
 
 def cosine_of_turns(turns):
@@ -229,48 +178,143 @@
     )
 
 
-def shrink_kernel(tile_ref, out_ref):
+def unpack(packed):
+    wide = packed.astype(f32)
+    return jnp.concatenate([wide, pltpu.roll(wide, P_SIZE, axis=1)], axis=0).astype(bf16)
+
+
+def prepare_kernel(tile_ref, out_ref, low_ref, packed_ref, sem):
     rows, width = tile_ref.shape
     columns = width // DOWN
-    pick = (iota((width, columns), 0) // DOWN == iota((width, columns), 1)).astype(bf16)
-    sums = matmul(tile_ref[...], pick)
-    out_ref[...] = (jnp.sum(sums.reshape(rows // DOWN, DOWN, columns), axis=1) / DOWN).astype(bf16)
-
-
-def forward_kernel(
+    copy = pltpu.make_async_copy(tile_ref, out_ref, sem)
+    copy.start()
+    pick = (iota((width, LANES), 0) // DOWN == iota((width, LANES), 1) % columns).astype(bf16)
+    left = iota((columns // 2, LANES), 1) < P_SIZE
+    copy.wait()
+    sums = matmul(out_ref[...], pick)
+    coarse = jnp.sum(sums.reshape(rows // DOWN, DOWN, LANES), axis=1) / DOWN
+    half = coarse.shape[0] // 2
+    packed_ref[:half] = jnp.where(left, coarse[:half], coarse[half:]).astype(bf16)
+    low_ref[...] = out_ref[:P_SIZE]
+    edge = out_ref[:, :LANES].astype(f32)
+    half_rows = rows // 2
+    left = iota((half_rows, LANES), 1) < P_SIZE
+    edge = jnp.where(left, edge[:half_rows], pltpu.roll(edge[half_rows:], P_SIZE, axis=1))
+    packed_ref[half:] = edge.astype(bf16)
+
+
+def tables_kernel(
+    offsets_hbm,
+    coarse_offset_hbm,
+    mask_hbm,
+    weights_ref,
+    rows_ref,
+    picks_ref,
+    chosen_ref,
+    mask_out_ref,
+    forward_rows_ref,
+    inverse_ref,
+    inverse_rows_ref,
     offsets_ref,
-    columns_ref,
-    own_ref,
-    own_low_ref,
-    own_right_ref,
-    other_ref,
-    other_low_ref,
-    other_right_ref,
-    out_ref,
-    image,
-    weights,
-    stacked,
+    coarse_offset_ref,
+    mask_ref,
+    sems,
 ):
-    rows, width = own_ref.shape
-    tall = rows + P_SIZE
-    blocks = tall // STRIDE
-    supers = width // (GROUP * P_SIZE)
+    copies = [
+        pltpu.make_async_copy(source, target, sems.at[n])
+        for n, (source, target) in enumerate(
+            (
+                (offsets_hbm, offsets_ref),
+                (coarse_offset_hbm, coarse_offset_ref),
+                (mask_hbm, mask_ref),
+            )
+        )
+    ]
+    for copy in copies:
+        copy.start()
+    count = lax.axis_size("gx")
+    bands, per_row = chosen_ref.shape
+    supers = per_row // GROUP
     side = lax.axis_index("gz")
+    gx_place = lax.axis_index("gx")
+    shape = (2 * P_SIZE, LANES)
+    lane = iota(shape, 1)
+    row = iota(shape, 0)
+    values = jnp.where(
+        row // P_SIZE == lane % P_SIZE // HALF,
+        basis_values(lane % HALF, lane // P_SIZE, row % P_SIZE),
+        0.0,
+    )
+    padded = jnp.concatenate([values, jnp.zeros((2 * P_SIZE, LANES), f32)], axis=0)
+    shape = (P_SIZE, LANES)
+    row = iota(shape, 0)
+    lane = iota(shape, 1)
+    basis = basis_values(row % HALF, row // HALF, lane % P_SIZE)
+    high, low = split(basis)
+    forward_rows_ref[:P_SIZE] = high
+    forward_rows_ref[P_SIZE:] = jnp.where(lane < P_SIZE, low.astype(f32), 0.0).astype(bf16)
+    wide_high = jnp.concatenate([high.astype(f32)] * 2, axis=1)
+    wide_low = jnp.concatenate([low.astype(f32)] * 2, axis=1)
+    for kind in range(2):
+        rows = slice(kind * HALF, (kind + 1) * HALF)
+        for patch in range(GROUP):
+            mine = iota((HALF, GROUP * P_SIZE), 1) // P_SIZE == patch
+            at = (kind * GROUP + patch) * HALF
+            for part, value in enumerate((wide_high, wide_low)):
+                inverse_ref[at : at + HALF, part * 2 * LANES : (part + 1) * 2 * LANES] = jnp.where(
+                    mine, value[rows], 0.0
+                ).astype(bf16)
+    high, low = split(basis_values(lane % HALF, lane % P_SIZE // HALF, row))
+    inverse_rows_ref[:P_SIZE] = high
+    inverse_rows_ref[P_SIZE:] = jnp.where(lane < P_SIZE, low.astype(f32), 0.0).astype(bf16)
+    for copy in copies:
+        copy.wait()
     row_offset = offsets_ref[0]
     column_offset = offsets_ref[1]
-    for s, (main, low, right) in enumerate(
-        ((own_ref, own_low_ref, own_right_ref), (other_ref, other_low_ref, other_right_ref))
-    ):
-        image[s, :rows, :width] = main[...]
-        image[s, rows:, :width] = low[...]
-        image[s, :, width:] = jnp.zeros((tall, LANES), bf16)
-        image[s, :, width : width + P_SIZE] = right[...]
-    padded = jnp.concatenate(
-        [columns_ref[...].astype(f32), jnp.zeros((2 * P_SIZE, 4 * LANES), f32)], axis=0
-    )
+    coarse_offset = coarse_offset_ref[0]
+    shifts = [column_offset + STRIDE * ((t + side) % 2) for t in range(2)] + [coarse_offset]
+    for t, shift in enumerate(shifts):
+        moved = pltpu.roll(padded, shift, axis=0)
+        for part, value in enumerate(split(moved)):
+            weights_ref[t, :, part * LANES : (part + 1) * LANES] = value
+            value = pltpu.roll(value.astype(f32), P_SIZE, axis=1).astype(bf16)
+            weights_ref[t, :, (part + 2) * LANES : (part + 3) * LANES] = value
+    shape = (P_SIZE, 6 * STRIDE)
+    number = iota(shape, 0)
+    lane = iota(shape, 1)
+    place = lane // P_SIZE * STRIDE + lane % STRIDE - row_offset
+    values = jnp.where(
+        (place >= 0) & (place < P_SIZE), basis_values(number % HALF, number // HALF, place), 0.0
+    )
+    high, low = split(values)
+    is_low = lane % P_SIZE >= STRIDE
+    rows_ref[:P_SIZE] = high
+    rows_ref[P_SIZE:] = jnp.where(is_low, 0.0, low.astype(f32)).astype(bf16)
+    def pick(column):
+        centre = (gx_place * (2 * per_row) + column) * STRIDE + column_offset + P_SIZE // 2
+        return jnp.clip((centre // DOWN - coarse_offset) // P_SIZE, 0, count - 1)
+
+    lane_row = iota((1, LANES), 1)
     for t in range(2):
-        shift = column_offset + STRIDE * ((t + side) % 2)
-        weights[t] = pltpu.roll(padded, shift, axis=0).astype(bf16)
+        for g in range(supers):
+            column = 2 * (g * GROUP + lane_row // HALF) + (t + side) % 2
+            picks_ref[t, g] = jnp.broadcast_to(pick(column), (8, LANES))
+    shape = (bands, per_row)
+    parity = (iota(shape, 0) + side) % 2
+    chosen_ref[...] = pick(2 * iota(shape, 1) + parity)
+    shape = (2 * per_row, per_row)
+    columns = iota(shape, 0) - 2 * iota(shape, 1)
+    mask = mask_ref[...].astype(f32).astype(bf16)
+    masks = [matmul(mask, (columns == n).astype(bf16)) for n in range(2)]
+    mask_out_ref[...] = jnp.where(parity == 0, masks[0], masks[1])
+
+
+def forward_bands(image, stacked, weights, left_rows, first_band, out_ref):
+    bands = out_ref.shape[0]
+    tall = image.shape[1]
+    wide = out_ref.shape[2]
+    blocks = tall // STRIDE
+    supers = wide // (2 * LANES)
     left = iota((tall, LANES), 1) < P_SIZE
     for s in range(2):
         for t in range(2):
@@ -289,21 +333,11 @@
                         block = slice(n * STRIDE, (n + 1) * STRIDE)
                         stacked[s, t, 2 * n * STRIDE : (2 * n + 1) * STRIDE, at] = high[block]
                         stacked[s, t, (2 * n + 1) * STRIDE : (2 * n + 2) * STRIDE, at] = low[block]
-    shape = (P_SIZE, 6 * STRIDE)
-    number = iota(shape, 0)
-    lane = iota(shape, 1)
-    place = lane // P_SIZE * STRIDE + lane % STRIDE - row_offset
-    values = jnp.where(
-        (place >= 0) & (place < P_SIZE), basis_values(number % HALF, number // HALF, place), 0.0
-    )
-    high, low = split(values)
-    is_low = lane % P_SIZE >= STRIDE
-    left_rows = jnp.concatenate([high, jnp.where(is_low, 0.0, low.astype(f32)).astype(bf16)], axis=0)
-    sign = jnp.where(side == 0, 1.0, -1.0).astype(f32)
-    for i in range(rows // STRIDE):
+    sign = jnp.where(lax.axis_index("gz") == 0, 1.0, -1.0).astype(f32)
+    for i in range(bands):
         spectra = []
         for s in range(2):
-            window = stacked[s, i % 2, 2 * STRIDE * i : 2 * STRIDE * (i + 3), :]
+            window = stacked[s, (first_band + i) % 2, 2 * STRIDE * i : 2 * STRIDE * (i + 3), :]
             spectra.append(add_row_halves(matmul(left_rows, window)))
         for g in range(supers):
             lane = g * 2 * LANES
@@ -319,34 +353,83 @@
                 out_ref[i, HALF + begin : HALF + end, lane + LANES : lane + 2 * LANES] = out[3]
 
 
+def is_last(axis):
+    return lax.axis_index(axis) == lax.axis_size(axis) - 1
+
+
+def upper_kernel(
+    weights, left_rows_ref, own_ref, own_right_ref, other_ref, other_right_ref, out_ref, image, stacked
+):
+    width = own_ref.shape[1]
+    for s, (main, right) in enumerate(((own_ref, own_right_ref), (other_ref, other_right_ref))):
+        image[s, :, :width] = main[...]
+        image[s, :, width:] = unpack(right[...])
+
+    @pl.when(is_last("gx"))
+    def _():
+        image[:, :, width:] = jnp.zeros((2, image.shape[1], LANES), bf16)
+
+    forward_bands(image, stacked, weights, left_rows_ref[...], 0, out_ref)
+
+
+def lower_kernel(
+    weights,
+    left_rows_ref,
+    own_ref,
+    own_right_ref,
+    own_low_ref,
+    other_ref,
+    other_right_ref,
+    other_low_ref,
+    out_ref,
+    image,
+    stacked,
+):
+    rows, width = own_ref.shape
+    for s, (main, right, low) in enumerate(
+        ((own_ref, own_right_ref, own_low_ref), (other_ref, other_right_ref, other_low_ref))
+    ):
+        image[s, :P_SIZE, :width] = main[rows - P_SIZE :]
+        edge = right[rows // 2 - P_SIZE :].astype(f32)
+        image[s, :P_SIZE, width:] = pltpu.roll(edge, P_SIZE, axis=1).astype(bf16)
+        image[s, P_SIZE:] = low[...]
+
+    @pl.when(is_last("gx"))
+    def _():
+        image[:, :, width:] = jnp.zeros((2, 2 * P_SIZE, LANES), bf16)
+
+    @pl.when(is_last("gy"))
+    def _():
+        image[:, P_SIZE:, :] = jnp.zeros((2, P_SIZE, width + LANES), bf16)
+
+    forward_bands(
+        image, stacked, weights, left_rows_ref[...], rows // STRIDE - out_ref.shape[0], out_ref
+    )
+
+
 def inverse_columns(high, low, table_ref):
     table_high = table_ref[:, : 2 * LANES]
     table_low = table_ref[:, 2 * LANES :]
     return matmul(high, table_high) + matmul(high, table_low) + matmul(low, table_high)
 
 
-def coarse_peaks(offset, pieces, sources, forward_rows_ref, inverse_ref, inverse_rows_ref, table, sign):
-    count = len(pieces)
-    supers = count // GROUP
-    wide = supers * 2 * LANES
-    shape = (P_SIZE, wide)
-    lane = iota(shape, 1)
-    patch = lane // (2 * LANES) * GROUP + lane % LANES // HALF
-    place = iota(shape, 0) - offset - patch * P_SIZE
-    for j in range(count):
-        here = place + j * P_SIZE
-        values = jnp.where(
-            (here >= 0) & (here < P_SIZE),
-            basis_values(lane % HALF, lane % (2 * LANES) // LANES, here),
-            0.0,
+def coarse_peaks(strip, forward_rows_ref, inverse_ref, inverse_rows_ref, weights, sign):
+    supers = len(strip) * 2 // GROUP
+    left = iota((2 * P_SIZE, LANES), 1) < P_SIZE
+    strip = strip + [jnp.zeros_like(strip[0])]
+    columns = []
+    for g in range(supers):
+        a, b = (
+            matmul(
+                jnp.concatenate(strip[2 * g + n : 2 * g + n + 2], axis=1),
+                weights[:, 2 * n * LANES : 2 * (n + 1) * LANES],
+            )
+            for n in range(2)
         )
-        high, low = split(values)
-        table[j, :, :wide] = high
-        table[j, :, wide:] = low
-    strips = jnp.zeros((2 * P_SIZE, wide), f32)
-    for piece, source in zip(pieces, sources):
-        product = matmul(piece[...], table[source])
-        strips = strips + (product[:, :wide] + product[:, wide:])
+        a = a[:, :LANES] + a[:, LANES:]
+        b = b[:, :LANES] + b[:, LANES:]
+        columns += [jnp.where(left, a, b), pltpu.roll(jnp.where(left, b, a), P_SIZE, axis=1)]
+    strips = jnp.concatenate(columns, axis=1)
     spectra = []
     for s in range(2):
         high, low = split(strips[s * P_SIZE : (s + 1) * P_SIZE])
@@ -378,29 +461,36 @@
     return peaks
 
 
-def peak_kernel(
-    offsets_ref,
-    coarse_offset_ref,
-    mask_ref,
+def turn_kernel(
     forward_rows_ref,
     inverse_ref,
     inverse_rows_ref,
-    spectra_ref,
-    *refs,
+    weights,
+    picks_ref,
+    chosen_ref,
+    own_part_ref,
+    other_part_ref,
+    turns,
+    base_ref,
+    ordered,
 ):
-    pieces, (out_ref, table, turns, high_ref, low_ref, stacked) = refs[:-6], refs[-6:]
-    bands, _, wide = spectra_ref.shape
-    supers = wide // (2 * LANES)
-    per_row = supers * GROUP
+    count = ordered.shape[0]
+    supers = turns.shape[1]
     side = lax.axis_index("gz")
     place = lax.axis_index("gx")
-    count = len(pieces)
     sign = jnp.where(side == 0, 1.0, -1.0).astype(f32)
-    sources = [exchange_source(place, step, count) for step in range(count)]
-    column_offset = offsets_ref[1]
-    coarse_offset = coarse_offset_ref[0]
+    for step in range(count):
+        for part, ref in enumerate((own_part_ref, other_part_ref)):
+            tile = ref[step * HALF : (step + 1) * HALF].astype(f32)
+            tile = jnp.concatenate([tile, pltpu.roll(tile, P_SIZE, axis=1)], axis=0)
+            ordered[place ^ step, part * P_SIZE : (part + 1) * P_SIZE] = tile
+    left = iota((2 * P_SIZE, LANES), 1) < P_SIZE
+    strip = []
+    for j in range(0, count, 2):
+        both = jnp.where(left, ordered[j], pltpu.roll(ordered[j + 1], P_SIZE, axis=1))
+        strip.append(both.astype(bf16))
     peaks = coarse_peaks(
-        coarse_offset, pieces, sources, forward_rows_ref, inverse_ref, inverse_rows_ref, table, sign
+        strip, forward_rows_ref, inverse_ref, inverse_rows_ref, weights.at[2], sign
     )
     blended = []
     for axis in range(2):
@@ -408,12 +498,10 @@
         mean = sum(values[1:], values[0]) / count
         blended.append([(0.5 * DOWN) * (value + mean) for value in values])
 
-    def prior(column):
-        centre = (place * (2 * per_row) + column) * STRIDE + column_offset + P_SIZE // 2
-        pick = jnp.clip((centre // DOWN - coarse_offset) // P_SIZE, 0, count - 1)
+    def prior(pick):
         out = []
         for values in blended:
-            chosen = jnp.broadcast_to(values[0], column.shape)
+            chosen = jnp.broadcast_to(values[0], pick.shape)
             for j in range(1, count):
                 chosen = jnp.where(pick == j, values[j], chosen)
             out.append(chosen)
@@ -427,8 +515,9 @@
     frequency_x = (lane_row % HALF).astype(f32) / P_SIZE
     for t in range(2):
         for g in range(supers):
-            column = 2 * (g * GROUP + lane_row // HALF) + (t + side) % 2
-            dy, dx = (value - P_SIZE * jnp.round(value / P_SIZE) for value in prior(column))
+            dy, dx = (
+                value - P_SIZE * jnp.round(value / P_SIZE) for value in prior(picks_ref[t, g, :1])
+            )
             turn_y = nearest(frequency_y * dy)
             turn_x = nearest(frequency_x * dx)
             cy, sy = cosine_of_turns(turn_y), sine_of_turns(turn_y)
@@ -447,8 +536,32 @@
             ends = (1.0, half_x, half_y, half_both)
             for n in range(4):
                 turns[t, g, n] = SCALE * jnp.where(corner, ends[n], 2.0 * turn[n])
+    base = prior(chosen_ref[...])
+    for axis in range(2):
+        base_ref[axis] = base[axis]
+
+
+def peak_kernel(
+    inverse_ref,
+    inverse_rows_ref,
+    mask_ref,
+    base_ref,
+    turns,
+    upper_ref,
+    lower_ref,
+    out_ref,
+    high_ref,
+    low_ref,
+    stacked,
+):
+    _, _, wide = upper_ref.shape
+    supers = wide // (2 * LANES)
+    per_row = supers * GROUP
+    refs = [upper_ref.at[i] for i in range(upper_ref.shape[0])]
+    refs += [lower_ref.at[i] for i in range(lower_ref.shape[0])]
+    bands = len(refs)
     for i in range(bands):
-        block = spectra_ref[i]
+        block = refs[i][...]
         for g in range(supers):
             lane = g * 2 * LANES
             values = quads(block, g)
@@ -476,41 +589,22 @@
         stack = jnp.concatenate([high_ref[rows], low_ref[rows]], axis=0)
         sums.append(column_sums(add_row_halves(matmul(inverse_rows_ref[...], stack))))
     sums = [jnp.concatenate(parts, axis=0) for parts in zip(*sums)]
-    shape = (bands, per_row)
-    lane = iota(shape, 1)
-    parity = (iota(shape, 0) + side) % 2
-    found = [jnp.zeros(shape, f32) for _ in range(2)]
+    lane = iota((bands, LANES), 1)
+    found = [jnp.zeros((bands, LANES), f32) for _ in range(2)]
     for m in range(per_row):
         peak = patch_peak(*sums, m)
         found = [jnp.where(lane == m, p, x) for p, x in zip(peak, found)]
-    shape = (2 * per_row, per_row)
-    columns = iota(shape, 0) - 2 * iota(shape, 1)
-    mask = mask_ref[...].astype(f32).astype(bf16)
-    masks = [matmul(mask, (columns == n).astype(bf16)) for n in range(2)]
-    chosen = jnp.where(parity == 0, masks[0], masks[1])
-    base = prior(2 * lane + parity)
     for axis in range(2):
-        out_ref[axis] = base[axis] + chosen * found[axis]
-
-
-def exchange_source(place, step, count):
-    if count & (count - 1) == 0:
-        return place ^ step
-    return lax.rem(place + count - step, count)
+        flow = base_ref[axis] + mask_ref[...] * found[axis][:, :per_row]
+        out_ref[axis, 0] = jnp.transpose(flow)
 
 
 def exchanged(value, axis, step):
-    count = lax.axis_size(axis)
-    if count & (count - 1) == 0:
-        pairs = [(i, i ^ step) for i in range(count)]
-    else:
-        pairs = [(i, (i + step) % count) for i in range(count)]
-    return lax.ppermute(value, axis, pairs)
-
-
-def from_next(value, axis):
-    count = lax.axis_size(axis)
-    return lax.ppermute(value, axis, [(i, i - 1) for i in range(1, count)])
+    return lax.ppermute(value, axis, [(i, i ^ step) for i in range(lax.axis_size(axis))])
+
+
+def from_later(value, axis, step):
+    return lax.ppermute(value, axis, [(i, i - step) for i in range(step, lax.axis_size(axis))])
 
 
 def swapped(value):
@@ -519,6 +613,12 @@
 
 VMEM = pl.BlockSpec(memory_space=pltpu.VMEM)
 SMEM = pl.BlockSpec(memory_space=pltpu.SMEM)
+
+
+def cost(microseconds):
+    return pl.CostEstimate(
+        flops=0, bytes_accessed=int(microseconds * 3.0e6), transcendentals=0
+    )
 
 
 def params(mebibytes):
@@ -530,71 +630,132 @@
     rows, width = own.shape
     bands = rows // STRIDE
     per_row = width // P_SIZE
-    tall = rows + P_SIZE
     count = lax.axis_size("gx")
-    assert rows == DOWN * P_SIZE and width == DOWN * P_SIZE and count % GROUP == 0
-    wide = 2 * width // 2
+    assert rows == DOWN * P_SIZE and width == DOWN * P_SIZE
+    assert count % GROUP == 0 and count & (count - 1) == 0
+    wide = width
     supers = width // (2 * LANES)
-    coarse_wide = count // GROUP * 2 * LANES
-    own_low = from_next(own[:P_SIZE], "gy")
-    own_right = from_next(jnp.concatenate([own[:, :P_SIZE], own_low[:, :P_SIZE]], axis=0), "gx")
     other = swapped(own)
-    other_low = swapped(own_low)
-    other_right = swapped(own_right)
-    coarse = pl.pallas_call(
-        shrink_kernel,
-        out_shape=jax.ShapeDtypeStruct((rows // DOWN, width // DOWN), bf16),
-        in_specs=[VMEM],
-        out_specs=VMEM,
+    own_tile, own_edge, packed = pl.pallas_call(
+        prepare_kernel,
+        out_shape=(
+            jax.ShapeDtypeStruct((rows, width), bf16),
+            jax.ShapeDtypeStruct((P_SIZE, width), bf16),
+            jax.ShapeDtypeStruct((HALF + rows // 2, LANES), bf16),
+        ),
+        in_specs=[pl.BlockSpec(memory_space=pl.ANY)],
+        out_specs=(VMEM,) * 3,
+        scratch_shapes=[pltpu.SemaphoreType.DMA],
         compiler_params=params(16),
     )(own)
-    both = jnp.concatenate([coarse, swapped(coarse)], axis=0)
-    pieces = [both] + [exchanged(both, "gx", step) for step in range(1, count)]
-    spectra = pl.pallas_call(
-        forward_kernel,
-        out_shape=jax.ShapeDtypeStruct((bands, P_SIZE, wide), f32),
-        in_specs=[SMEM] + [VMEM] * 7,
+    tables = pl.pallas_call(
+        tables_kernel,
+        out_shape=(
+            jax.ShapeDtypeStruct((3, 2 * LANES, 4 * LANES), bf16),
+            jax.ShapeDtypeStruct((2 * P_SIZE, 6 * STRIDE), bf16),
+            jax.ShapeDtypeStruct((2, supers, 8, LANES), jnp.int32),
+            jax.ShapeDtypeStruct((bands, per_row), jnp.int32),
+            jax.ShapeDtypeStruct((bands, per_row), f32),
+            jax.ShapeDtypeStruct((2 * P_SIZE, LANES), bf16),
+            jax.ShapeDtypeStruct((2 * LANES, 4 * LANES), bf16),
+            jax.ShapeDtypeStruct((2 * P_SIZE, LANES), bf16),
+        ),
+        in_specs=[pl.BlockSpec(memory_space=pltpu.HBM)] * 3,
+        out_specs=(VMEM,) * 8,
+        scratch_shapes=[
+            pltpu.SMEM(fine_offsets.shape, jnp.int32),
+            pltpu.SMEM(coarse_offset.shape, jnp.int32),
+            pltpu.VMEM(tissue_mask.shape, jnp.int32),
+            pltpu.SemaphoreType.DMA((3,)),
+        ],
+        compiler_params=params(16),
+        cost_estimate=cost(1.5),
+    )(fine_offsets, coarse_offset, tissue_mask)
+    got_even = exchanged(packed, "gx", 1)
+    got_odd = lax.ppermute(packed[HALF:], "gx", [(i + 1, i) for i in range(1, count - 1, 2)])
+    steps = [packed[:HALF], got_even[:HALF]]
+    right = jnp.where(lax.axis_index("gx") % 2 == 0, got_even[HALF:], got_odd)
+    tiles = jnp.concatenate(steps, axis=0)
+    step = 2
+    while step < count:
+        tiles = jnp.concatenate([tiles, exchanged(tiles, "gx", step)], axis=0)
+        step *= 2
+    weights, left_rows, picks, chosen, mask, forward_rows, inverse, inverse_rows = tables
+    low_payload = jnp.concatenate([own_edge, right[:P_SIZE]], axis=1)
+    low_payload, weights = lax.optimization_barrier((low_payload, weights))
+    own_low = from_later(low_payload, "gy", 1)
+    other_right = swapped(right)
+    other_tiles = swapped(tiles)
+    other_low = swapped(own_low)
+    low_bands = P_SIZE // STRIDE
+    upper = pl.pallas_call(
+        upper_kernel,
+        out_shape=jax.ShapeDtypeStruct((bands - low_bands, P_SIZE, wide), f32),
+        in_specs=[VMEM] * 6,
         out_specs=VMEM,
         scratch_shapes=[
-            pltpu.VMEM((2, tall, width + LANES), bf16),
-            pltpu.VMEM((2, 2 * LANES, 4 * LANES), bf16),
-            pltpu.VMEM((2, 2, 2 * tall, wide), bf16),
+            pltpu.VMEM((2, rows, width + LANES), bf16),
+            pltpu.VMEM((2, 2, 2 * rows, wide), bf16),
         ],
         compiler_params=params(32),
+        cost_estimate=cost(2.6),
+    )(weights, left_rows, own_tile, right, other, other_right)
+    other_tiles, upper = lax.optimization_barrier((other_tiles, upper))
+    turns, base = pl.pallas_call(
+        turn_kernel,
+        out_shape=(
+            jax.ShapeDtypeStruct((2, supers, 4, HALF, LANES), f32),
+            jax.ShapeDtypeStruct((2, bands, per_row), f32),
+        ),
+        in_specs=[VMEM] * 8,
+        out_specs=(VMEM,) * 2,
+        scratch_shapes=[pltpu.VMEM((count, 2 * P_SIZE, LANES), f32)],
+        compiler_params=params(32),
+        cost_estimate=cost(1.2),
     )(
-        fine_offsets,
-        jnp.asarray(forward_columns_table()),
-        own,
-        own_low,
-        own_right,
-        other,
-        other_low,
-        other_right,
-    )
+        forward_rows,
+        inverse,
+        inverse_rows,
+        weights,
+        picks,
+        chosen,
+        tiles,
+        other_tiles,
+    )
+    lower = pl.pallas_call(
+        lower_kernel,
+        out_shape=jax.ShapeDtypeStruct((low_bands, P_SIZE, wide), f32),
+        in_specs=[VMEM] * 8,
+        out_specs=VMEM,
+        scratch_shapes=[
+            pltpu.VMEM((2, 2 * P_SIZE, width + LANES), bf16),
+            pltpu.VMEM((2, 2, 4 * P_SIZE, wide), bf16),
+        ],
+        compiler_params=params(32),
+        cost_estimate=cost(0.6),
+    )(weights, left_rows, own_tile, right, own_low, other, other_right, other_low)
     flow = pl.pallas_call(
         peak_kernel,
-        out_shape=jax.ShapeDtypeStruct((2, bands, per_row), f32),
-        in_specs=[SMEM, SMEM] + [VMEM] * (5 + count),
+        out_shape=jax.ShapeDtypeStruct((2, 1, per_row, bands), f32),
+        in_specs=[VMEM] * 7,
         out_specs=VMEM,
         scratch_shapes=[
-            pltpu.VMEM((count, P_SIZE, 2 * coarse_wide), bf16),
-            pltpu.VMEM((2, supers, 4, HALF, LANES), f32),
             pltpu.VMEM((bands * P_SIZE, wide), bf16),
             pltpu.VMEM((bands * P_SIZE, wide), bf16),
             pltpu.VMEM((P_SIZE, wide), f32),
         ],
         compiler_params=params(40),
+        cost_estimate=cost(3.5),
     )(
-        fine_offsets,
-        coarse_offset,
-        tissue_mask,
-        jnp.asarray(forward_rows_table()),
-        jnp.asarray(inverse_columns_table()),
-        jnp.asarray(inverse_rows_table()),
-        spectra,
-        *pieces,
-    )
-    return flow.reshape(2, 1, bands, per_row)
+        inverse,
+        inverse_rows,
+        mask,
+        base,
+        turns,
+        upper,
+        lower,
+    )
+    return jnp.swapaxes(flow, 2, 3)
 
 
 def solution(mesh):

time: 33.3 us -> 24.1 us (0.72)
  the two profiles are of different devices: /device:TPU:0 before, /device:TPU:11 now
where the time goes in v1:
time: 24.1 us; the launch traced here: 23.8 us
  starting transfers between devices  11.5 us (48%)
  Pallas kernels  10 us (41%)
  local copies, waits for them, and re-layouts  1.36 us (6%)
  between operations  0.77 us (3%)
    ppermute x4, starting transfers between devices, swapped(): return lax.ppermute(value, 'gz', [(0, 1), (1, 0)])  6.16 us
    pallas_call x1, Pallas kernels, local(): pl.pallas_call(peak_kernel, out_shape=jax.ShapeDtypeStruct((2, 1, per_row...  2.96 us
    pallas_call x1, Pallas kernels, local(): pl.pallas_call(upper_kernel, out_shape=jax.ShapeDtypeStruct((bands - low_...  2.6 us
    ppermute x1, starting transfers between devices, from_later(): lax.ppermute(value, axis, [(i, i - step) for i in range(step, lax.axis_si...  2.16 us
    ppermute x2, starting transfers between devices, exchanged(): lax.ppermute(value, axis, [(i, i ^ step) for i in range(lax.axis_size(axi...  1.9 us
    pallas_call x1, Pallas kernels, local(): pl.pallas_call(turn_kernel, out_shape=(jax.ShapeDtypeStruct((2, supers, 4...  1.38 us
    unnamed x4, local copies, waits for them, and re-layouts  1.35 us
    pallas_call x1, Pallas kernels, local(): pl.pallas_call(prepare_kernel, out_shape=(jax.ShapeDtypeStruct((rows, wid...  1.34 us
  transfers between devices with their start and end apart: 8, of which 1 were waited for; matrix products, arithmetic and copies ran while one was open for 0% of the time, Pallas kernels for 21%

profile of v1, /device:TPU:11, one launch (start us, length us, event | category | flops | bytes accessed | tf_op | source)
XLA Modules:
  0.0 23.8 jit_solution(15301434019250541354)
XLA Ops:
  0.0 1.3 %shard_map.47 = (bf16[512,512]{1,0:T(8,128)(2,1)S(1)}, bf16[64,512]{1,0:T(8,128)(2,1)S(1)}, bf16[288,128]{1,0:T(8,128)(2,1)S(1)}) custom-call(bf16[512,512]{1,0:T(8,128)(2,1)} %bitcast.tile_ref), custom_call_target="tpu_custom_call" | custom-call | tf_op jit(solution)/shard_map/pallas_call | solution.py:639
  1.4 0.2 collective-permute-start
  1.6 1.3 %collective-permute-start.1 = (bf16[256,128]{1,0:T(8,128)(2,1)S(1)}, bf16[256,128]{1,0:T(8,128)(2,1)S(1)}, u32[]{:S(2)}, u32[]{:S(2)}) collective-permute-start(bf16[256,128]{1,0:T(8,128)(2,1)S(1)} %slice.16), channel_id=1, source_target_pairs={{8,4},{9,5},{10,6},{11,7},{24,20},{25,21},{26,22},{27,23}} | collective-permute-start | bytes 196616 | tf_op jit(solution)/shard_map/ppermute | solution.py:675
  2.9 1.0 %collective-permute-start.4 = (bf16[512,512]{1,0:T(8,128)(2,1)}, bf16[512,512]{1,0:T(8,128)(2,1)S(1)}, u32[]{:S(2)}, u32[]{:S(2)}) collective-permute-start(bf16[512,512]{1,0:T(8,128)(2,1)} %bitcast.tile_ref), channel_id=1, source_target_pairs={{0,1},{1,0},{2,3},{3,2},{4,5},{5,4},{6,7},{7,6},{8,9},{9,8},{10,11... | collective-permute-start | bytes 1572872 | tf_op jit(solution)/shard_map/ppermute | solution.py:611
  4.5 0.0 copy-start
  4.6 0.7 %copy-done = s32[16,16]{1,0:T(8,128)S(1)} copy-done((s32[16,16]{1,0:T(8,128)S(1)}, s32[16,16]{1,0:T(8,128)}, u32[]{:S(2)}) %copy-start) | copy-done | bytes 1048
  5.2 0.0 copy-start.1
  5.2 0.7 %copy-done.1 = s32[2]{0:T(128)S(1)} copy-done((s32[2]{0:T(128)S(1)}, s32[2]{0:T(128)}, u32[]{:S(2)}) %copy-start.1) | copy-done | bytes 32
  5.9 0.9 %shard_map.46 = (bf16[3,256,512]{2,1,0:T(8,128)(2,1)S(1)}, bf16[128,192]{1,0:T(8,128)(2,1)S(1)}, s32[2,2,8,128]{3,2,1,0:T(8,128)S(1)}, s32[16,8]{1,0:T(8,128)S(1...) custom-call(s32[2]{0:T(128)S(1)} %copy-done.1, ...), custom_call_target="tpu_custom_call" | custom-call | bytes 4500000 | tf_op jit(solution)/shard_map/pallas_call | solution.py:651
  6.8 0.1 collective-permute-done.1
  6.9 0.0 collective-permute-done
  7.0 2.2 %collective-permute-start.6 = (bf16[64,640]{1,0:T(8,128)(2,1)S(1)}, bf16[64,640]{1,0:T(8,128)(2,1)S(1)}, u32[]{:S(2)}, u32[]{:S(2)}) collective-permute-start(bf16[64,640]{1,0:T(8,128)(2,1)S(1)} %pad_maximum_fusion), channel_id=1, source_target_pairs={{2,0},{3,1},{6,4},{7,5},{10,8},{11,9},{14,12},{15,13},{18,16},{19,... | collective-permute-start | bytes 245768 | tf_op jit(solution)/shard_map/ppermute | solution.py:607
  9.2 1.7 %collective-permute-start.2 = (bf16[64,128]{1,0:T(8,128)(2,1)S(1)}, bf16[64,128]{1,0:T(8,128)(2,1)S(1)}, u32[]{:S(2)}, u32[]{:S(2)}) collective-permute-start(bf16[64,128]{1,0:T(8,128)(2,1)S(1)} %pad_maximum_fusion.2), channel_id=1, source_target_pairs={{0,8},{4,12},{8,0},{12,4},{1,9},{5,13},{9,1},{13,5},{2,10},{6,14},... | collective-permute-start | bytes 49160 | tf_op jit(solution)/shard_map/ppermute | solution.py:603
  10.8 0.8 %collective-permute-start.5 = (bf16[256,128]{1,0:T(8,128)(2,1)S(1)}, bf16[256,128]{1,0:T(8,128)(2,1)S(1)}, u32[]{:S(2)}, u32[]{:S(2)}) collective-permute-start(bf16[256,128]{1,0:T(8,128)(2,1)S(1)} %slice_select_fusion.own_right_ref), channel_id=1, source_target_pairs={{0,1},{1,0},{2,3},{3,2},{4,5},{5,4},{6,7},{7,6},{8,9},{9,8},{10,11... | collective-permute-start | bytes 196616 | tf_op jit(solution)/shard_map/ppermute | solution.py:611
  11.6 0.0 collective-permute-done.6.own_low_ref
  11.6 1.7 %collective-permute-start.7 = (bf16[64,640]{1,0:T(8,128)(2,1)S(1)}, bf16[64,640]{1,0:T(8,128)(2,1)S(1)}, u32[]{:S(2)}, u32[]{:S(2)}) collective-permute-start(bf16[64,640]{1,0:T(8,128)(2,1)S(1)} %collective-permute-done.6.own_low_ref), channel_id=1, source_target_pairs={{0,1},{1,0},{2,3},{3,2},{4,5},{5,4},{6,7},{7,6},{8,9},{9,8},{10,11... | collective-permute-start | bytes 245768 | tf_op jit(solution)/shard_map/ppermute | solution.py:611
  13.3 0.0 collective-permute-done.2
  13.3 2.7 %collective-permute-start.3 = (bf16[128,128]{1,0:T(8,128)(2,1)S(1)}, bf16[128,128]{1,0:T(8,128)(2,1)S(1)}, u32[]{:S(2)}, u32[]{:S(2)}) collective-permute-start(bf16[128,128]{1,0:T(8,128)(2,1)S(1)} %pad_maximum_fusion.1.own_part_ref), channel_id=1, source_target_pairs={{0,1},{1,0},{2,3},{3,2},{4,5},{5,4},{6,7},{7,6},{8,9},{9,8},{10,11... | collective-permute-start | bytes 98312 | tf_op jit(solution)/shard_map/ppermute | solution.py:611
  16.0 0.0 collective-permute-done.5.other_right_ref
  16.0 0.0 collective-permute-done.4.other_ref
  16.0 2.6 %shard_map.48.upper_ref = f32[14,64,512]{2,1,0:T(8,128)S(1)} custom-call(bf16[3,256,512]{2,1,0:T(8,128)(2,1)S(1)} %get-tuple-element.29.weights, bf16[128,192]{1,0:T(8,128)(2,1)S(1)} %get-tuple-element.32.left_rows_ref, bf16[512,512]{1,0:T(8,128)(2,1)S(1)} %get-tuple-element.33.own_ref, bf16[256,128]{1,0:T(8,128)(2,1)S(1)} %slice_select_fusion.own_right_ref, ...), custom_call_target="tpu_custom_call" | custom-call | bytes 7800000 | tf_op jit(solution)/shard_map/pallas_call | solution.py:691
  18.6 0.0 collective-permute-done.3.other_part_ref
  18.6 1.4 %shard_map.49 = (f32[2,2,4,32,128]{4,3,2,1,0:T(8,128)S(1)}, f32[2,16,8]{2,1,0:T(8,128)S(1)}) custom-call(bf16[128,128]{1,0:T(8,128)(2,1)S(1)} %get-tuple-element.25.forward_rows_ref, bf16[256,512]{1,0:T(8,128)(2,1)S(1)} %get-tuple-element.22.inverse_ref, bf16[128,128]{1,0:T(8,128)(2,1)S(1)} %get-tuple-element.23.inverse_rows_ref, ...), custom_call_target="tpu_custom_call" | custom-call | bytes 3600000 | tf_op jit(solution)/shard_map/pallas_call | solution.py:704
  20.0 0.0 collective-permute-done.7.other_low_ref
  20.0 0.8 %shard_map.50.lower_ref = f32[2,64,512]{2,1,0:T(8,128)S(1)} custom-call(bf16[3,256,512]{2,1,0:T(8,128)(2,1)S(1)} %get-tuple-element.29.weights, bf16[128,192]{1,0:T(8,128)(2,1)S(1)} %get-tuple-element.32.left_rows_ref, bf16[512,512]{1,0:T(8,128)(2,1)S(1)} %get-tuple-element.33.own_ref, bf16[256,128]{1,0:T(8,128)(2,1)S(1)} %slice_select_fusion.own_right_ref, ...), custom_call_target="tpu_custom_call" | custom-call | bytes 1800000 | tf_op jit(solution)/shard_map/pallas_call | solution.py:725
  20.9 3.0 %shard_map.51 = f32[2,1,8,16]{3,2,1,0:T(8,128)} custom-call(bf16[256,512]{1,0:T(8,128)(2,1)S(1)} %get-tuple-element.22.inverse_ref, bf16[128,128]{1,0:T(8,128)(2,1)S(1)} %get-tuple-element.23.inverse_rows_ref, f32[16,8]{1,0:T(8,128)S(1)} %get-tuple-element.24.mask_ref, f32[2,16,8]{2,1,0:T(8,128)S(1)} %get-tuple-element.35.base_ref, ...), custom_call_target="tpu_custom_call" | custom-call | bytes 10500000 | tf_op jit(solution)/shard_map/pallas_call | solution.py:737
  (8 shorter events, 0.0 us)
Async XLA Ops:
  1.4 5.6 %collective-permute-start = (bf16[288,128]{1,0:T(8,128)(2,1)S(1)}, bf16[288,128]{1,0:T(8,128)(2,1)S(1)}, u32[]{:S(2)}, u32[]{:S(2)}) collective-permute-start(bf16[288,128]{1,0:T(8,128)(2,1)S(1)} %get-tuple-element.27), channel_id=1, source_target_pairs={{0,4},{4,0},{8,12},{12,8},{1,5},{5,1},{9,13},{13,9},{2,6},{6,2},{1... | collective-permute-start | bytes 221192 | tf_op jit(solution)/shard_map/ppermute | solution.py:603
  1.6 5.4 %collective-permute-start.1 = (bf16[256,128]{1,0:T(8,128)(2,1)S(1)}, bf16[256,128]{1,0:T(8,128)(2,1)S(1)}, u32[]{:S(2)}, u32[]{:S(2)}) collective-permute-start(bf16[256,128]{1,0:T(8,128)(2,1)S(1)} %slice.16), channel_id=1, source_target_pairs={{8,4},{9,5},{10,6},{11,7},{24,20},{25,21},{26,22},{27,23}} | collective-permute-start | bytes 196616 | tf_op jit(solution)/shard_map/ppermute | solution.py:675
  2.9 13.1 %collective-permute-start.4 = (bf16[512,512]{1,0:T(8,128)(2,1)}, bf16[512,512]{1,0:T(8,128)(2,1)S(1)}, u32[]{:S(2)}, u32[]{:S(2)}) collective-permute-start(bf16[512,512]{1,0:T(8,128)(2,1)} %bitcast.tile_ref), channel_id=1, source_target_pairs={{0,1},{1,0},{2,3},{3,2},{4,5},{5,4},{6,7},{7,6},{8,9},{9,8},{10,11... | collective-permute-start | bytes 1572872 | tf_op jit(solution)/shard_map/ppermute | solution.py:611
  4.5 0.7 %copy-start = (s32[16,16]{1,0:T(8,128)S(1)}, s32[16,16]{1,0:T(8,128)}, u32[]{:S(2)}) copy-start(s32[16,16]{1,0:T(8,128)} %mask_hbm.1) | copy-start | bytes 3076
  5.2 0.7 %copy-start.1 = (s32[2]{0:T(128)S(1)}, s32[2]{0:T(128)}, u32[]{:S(2)}) copy-start(s32[2]{0:T(128)} %offsets_hbm.1) | copy-start | bytes 28
  7.0 4.6 %collective-permute-start.6 = (bf16[64,640]{1,0:T(8,128)(2,1)S(1)}, bf16[64,640]{1,0:T(8,128)(2,1)S(1)}, u32[]{:S(2)}, u32[]{:S(2)}) collective-permute-start(bf16[64,640]{1,0:T(8,128)(2,1)S(1)} %pad_maximum_fusion), channel_id=1, source_target_pairs={{2,0},{3,1},{6,4},{7,5},{10,8},{11,9},{14,12},{15,13},{18,16},{19,... | collective-permute-start | bytes 245768 | tf_op jit(solution)/shard_map/ppermute | solution.py:607
  9.2 4.1 %collective-permute-start.2 = (bf16[64,128]{1,0:T(8,128)(2,1)S(1)}, bf16[64,128]{1,0:T(8,128)(2,1)S(1)}, u32[]{:S(2)}, u32[]{:S(2)}) collective-permute-start(bf16[64,128]{1,0:T(8,128)(2,1)S(1)} %pad_maximum_fusion.2), channel_id=1, source_target_pairs={{0,8},{4,12},{8,0},{12,4},{1,9},{5,13},{9,1},{13,5},{2,10},{6,14},... | collective-permute-start | bytes 49160 | tf_op jit(solution)/shard_map/ppermute | solution.py:603
  10.8 5.2 %collective-permute-start.5 = (bf16[256,128]{1,0:T(8,128)(2,1)S(1)}, bf16[256,128]{1,0:T(8,128)(2,1)S(1)}, u32[]{:S(2)}, u32[]{:S(2)}) collective-permute-start(bf16[256,128]{1,0:T(8,128)(2,1)S(1)} %slice_select_fusion.own_right_ref), channel_id=1, source_target_pairs={{0,1},{1,0},{2,3},{3,2},{4,5},{5,4},{6,7},{7,6},{8,9},{9,8},{10,11... | collective-permute-start | bytes 196616 | tf_op jit(solution)/shard_map/ppermute | solution.py:611
  11.6 8.4 %collective-permute-start.7 = (bf16[64,640]{1,0:T(8,128)(2,1)S(1)}, bf16[64,640]{1,0:T(8,128)(2,1)S(1)}, u32[]{:S(2)}, u32[]{:S(2)}) collective-permute-start(bf16[64,640]{1,0:T(8,128)(2,1)S(1)} %collective-permute-done.6.own_low_ref), channel_id=1, source_target_pairs={{0,1},{1,0},{2,3},{3,2},{4,5},{5,4},{6,7},{7,6},{8,9},{9,8},{10,11... | collective-permute-start | bytes 245768 | tf_op jit(solution)/shard_map/ppermute | solution.py:611
  13.3 5.3 %collective-permute-start.3 = (bf16[128,128]{1,0:T(8,128)(2,1)S(1)}, bf16[128,128]{1,0:T(8,128)(2,1)S(1)}, u32[]{:S(2)}, u32[]{:S(2)}) collective-permute-start(bf16[128,128]{1,0:T(8,128)(2,1)S(1)} %pad_maximum_fusion.1.own_part_ref), channel_id=1, source_target_pairs={{0,1},{1,0},{2,3},{3,2},{4,5},{5,4},{6,7},{7,6},{8,9},{9,8},{10,11... | collective-permute-start | bytes 98312 | tf_op jit(solution)/shard_map/ppermute | solution.py:611

commit v2 on v1

--- a/solution.py
+++ b/solution.py
@@ -1,3 +1,4 @@
+import functools
 import math
 
 import jax
@@ -14,6 +15,7 @@
 LANES = 128
 GROUP = LANES // HALF
 SHARPNESS = 12.0
+PARTS = 1
 SCALE = SHARPNESS / float(P_SIZE) ** 4 * math.log2(math.e)
 
 f32 = jnp.float32
@@ -186,13 +188,20 @@
 def prepare_kernel(tile_ref, out_ref, low_ref, packed_ref, sem):
     rows, width = tile_ref.shape
     columns = width // DOWN
-    copy = pltpu.make_async_copy(tile_ref, out_ref, sem)
-    copy.start()
+    chunk = rows // PARTS
+    copies = []
+    for n in range(PARTS):
+        at = pl.ds(n * chunk, chunk)
+        copies.append(pltpu.make_async_copy(tile_ref.at[at], out_ref.at[at], sem.at[n]))
+        copies[-1].start()
     pick = (iota((width, LANES), 0) // DOWN == iota((width, LANES), 1) % columns).astype(bf16)
     left = iota((columns // 2, LANES), 1) < P_SIZE
-    copy.wait()
-    sums = matmul(out_ref[...], pick)
-    coarse = jnp.sum(sums.reshape(rows // DOWN, DOWN, LANES), axis=1) / DOWN
+    sums = []
+    for n in range(PARTS):
+        copies[n].wait()
+        part = matmul(out_ref[n * chunk : (n + 1) * chunk], pick)
+        sums.append(jnp.sum(part.reshape(chunk // DOWN, DOWN, LANES), axis=1))
+    coarse = jnp.concatenate(sums, axis=0) / DOWN
     half = coarse.shape[0] // 2
     packed_ref[:half] = jnp.where(left, coarse[:half], coarse[half:]).astype(bf16)
     low_ref[...] = out_ref[:P_SIZE]
@@ -204,34 +213,19 @@
 
 
 def tables_kernel(
-    offsets_hbm,
-    coarse_offset_hbm,
-    mask_hbm,
+    offsets_in,
     weights_ref,
     rows_ref,
     picks_ref,
     chosen_ref,
-    mask_out_ref,
     forward_rows_ref,
     inverse_ref,
     inverse_rows_ref,
     offsets_ref,
-    coarse_offset_ref,
-    mask_ref,
-    sems,
+    sem,
 ):
-    copies = [
-        pltpu.make_async_copy(source, target, sems.at[n])
-        for n, (source, target) in enumerate(
-            (
-                (offsets_hbm, offsets_ref),
-                (coarse_offset_hbm, coarse_offset_ref),
-                (mask_hbm, mask_ref),
-            )
-        )
-    ]
-    for copy in copies:
-        copy.start()
+    copy = pltpu.make_async_copy(offsets_in, offsets_ref, sem)
+    copy.start()
     count = lax.axis_size("gx")
     bands, per_row = chosen_ref.shape
     supers = per_row // GROUP
@@ -267,11 +261,10 @@
     high, low = split(basis_values(lane % HALF, lane % P_SIZE // HALF, row))
     inverse_rows_ref[:P_SIZE] = high
     inverse_rows_ref[P_SIZE:] = jnp.where(lane < P_SIZE, low.astype(f32), 0.0).astype(bf16)
-    for copy in copies:
-        copy.wait()
+    copy.wait()
     row_offset = offsets_ref[0]
     column_offset = offsets_ref[1]
-    coarse_offset = coarse_offset_ref[0]
+    coarse_offset = offsets_ref[2]
     shifts = [column_offset + STRIDE * ((t + side) % 2) for t in range(2)] + [coarse_offset]
     for t, shift in enumerate(shifts):
         moved = pltpu.roll(padded, shift, axis=0)
@@ -302,11 +295,6 @@
     shape = (bands, per_row)
     parity = (iota(shape, 0) + side) % 2
     chosen_ref[...] = pick(2 * iota(shape, 1) + parity)
-    shape = (2 * per_row, per_row)
-    columns = iota(shape, 0) - 2 * iota(shape, 1)
-    mask = mask_ref[...].astype(f32).astype(bf16)
-    masks = [matmul(mask, (columns == n).astype(bf16)) for n in range(2)]
-    mask_out_ref[...] = jnp.where(parity == 0, masks[0], masks[1])
 
 
 def forward_bands(image, stacked, weights, left_rows, first_band, out_ref):
@@ -357,17 +345,19 @@
     return lax.axis_index(axis) == lax.axis_size(axis) - 1
 
 
-def upper_kernel(
-    weights, left_rows_ref, own_ref, own_right_ref, other_ref, other_right_ref, out_ref, image, stacked
-):
-    width = own_ref.shape[1]
-    for s, (main, right) in enumerate(((own_ref, own_right_ref), (other_ref, other_right_ref))):
-        image[s, :, :width] = main[...]
-        image[s, :, width:] = unpack(right[...])
-
-    @pl.when(is_last("gx"))
-    def _():
-        image[:, :, width:] = jnp.zeros((2, image.shape[1], LANES), bf16)
+def upper_kernel(group, weights, left_rows_ref, own_ref, other_ref, *refs):
+    rights, (out_ref, image, stacked) = refs[:-3], refs[-3:]
+    lane = group * 2 * LANES
+    wide = 2 * LANES if rights else 3 * LANES
+    for s, main in enumerate((own_ref, other_ref)):
+        image[s, :, :wide] = main[:, lane : lane + wide]
+        if rights:
+            image[s, :, wide:] = unpack(rights[s][...])
+    if rights:
+
+        @pl.when(is_last("gx"))
+        def _():
+            image[:, :, wide:] = jnp.zeros((2, image.shape[1], LANES), bf16)
 
     forward_bands(image, stacked, weights, left_rows_ref[...], 0, out_ref)
 
@@ -542,33 +532,26 @@
 
 
 def peak_kernel(
+    first_band,
     inverse_ref,
     inverse_rows_ref,
     mask_ref,
     base_ref,
     turns,
-    upper_ref,
-    lower_ref,
-    out_ref,
-    high_ref,
-    low_ref,
-    stacked,
+    *refs,
 ):
-    _, _, wide = upper_ref.shape
-    supers = wide // (2 * LANES)
+    spectra, (out_ref, high_ref, low_ref, stacked) = refs[:-4], refs[-4:]
+    supers = turns.shape[1]
     per_row = supers * GROUP
-    refs = [upper_ref.at[i] for i in range(upper_ref.shape[0])]
-    refs += [lower_ref.at[i] for i in range(lower_ref.shape[0])]
-    bands = len(refs)
+    bands = spectra[0].shape[0]
     for i in range(bands):
-        block = refs[i][...]
         for g in range(supers):
             lane = g * 2 * LANES
-            values = quads(block, g)
+            values = quads(spectra[g][i], 0) if len(spectra) > 1 else quads(spectra[0][i], g)
             for begin, end, first in ROW_PARTS:
                 parts = coefficients(
                     [x[begin:end] for x in values],
-                    [turns[i % 2, g, n, begin:end] for n in range(4)],
+                    [turns[(first_band + i) % 2, g, n, begin:end] for n in range(4)],
                     first,
                 )
                 stacked[begin:end, lane : lane + LANES] = parts[0]
@@ -594,9 +577,24 @@
     for m in range(per_row):
         peak = patch_peak(*sums, m)
         found = [jnp.where(lane == m, p, x) for p, x in zip(peak, found)]
+    shape = (2 * per_row, per_row)
+    columns = iota(shape, 0) - 2 * iota(shape, 1)
+    mask = mask_ref[first_band : first_band + bands].astype(f32).astype(bf16)
+    masks = [matmul(mask, (columns == n).astype(bf16)) for n in range(2)]
+    parity = (iota((bands, per_row), 0) + (first_band + lax.axis_index("gz"))) % 2
+    chosen = jnp.where(parity == 0, masks[0], masks[1])
     for axis in range(2):
-        flow = base_ref[axis] + mask_ref[...] * found[axis][:, :per_row]
-        out_ref[axis, 0] = jnp.transpose(flow)
+        base = base_ref[axis, first_band : first_band + bands]
+        flow = base + chosen * found[axis][:, :per_row]
+        out_ref[axis] = jnp.transpose(flow)
+
+
+def lower_peak_kernel(first_band, upper_flow_ref, *refs):
+    out_ref, *scratch = refs[-5:]
+    flow, scratch = scratch[-1], scratch[:-1]
+    peak_kernel(first_band, *refs[:-5], flow, *scratch)
+    for axis in range(2):
+        out_ref[axis, 0] = jnp.concatenate([upper_flow_ref[axis], flow[axis]], axis=1)
 
 
 def exchanged(value, axis, step):
@@ -643,10 +641,11 @@
             jax.ShapeDtypeStruct((P_SIZE, width), bf16),
             jax.ShapeDtypeStruct((HALF + rows // 2, LANES), bf16),
         ),
-        in_specs=[pl.BlockSpec(memory_space=pl.ANY)],
+        in_specs=[pl.BlockSpec(memory_space=pltpu.HBM)],
         out_specs=(VMEM,) * 3,
-        scratch_shapes=[pltpu.SemaphoreType.DMA],
+        scratch_shapes=[pltpu.SemaphoreType.DMA((PARTS,))],
         compiler_params=params(16),
+        cost_estimate=cost(5.0),
     )(own)
     tables = pl.pallas_call(
         tables_kernel,
@@ -655,52 +654,53 @@
             jax.ShapeDtypeStruct((2 * P_SIZE, 6 * STRIDE), bf16),
             jax.ShapeDtypeStruct((2, supers, 8, LANES), jnp.int32),
             jax.ShapeDtypeStruct((bands, per_row), jnp.int32),
-            jax.ShapeDtypeStruct((bands, per_row), f32),
             jax.ShapeDtypeStruct((2 * P_SIZE, LANES), bf16),
             jax.ShapeDtypeStruct((2 * LANES, 4 * LANES), bf16),
             jax.ShapeDtypeStruct((2 * P_SIZE, LANES), bf16),
         ),
-        in_specs=[pl.BlockSpec(memory_space=pltpu.HBM)] * 3,
-        out_specs=(VMEM,) * 8,
-        scratch_shapes=[
-            pltpu.SMEM(fine_offsets.shape, jnp.int32),
-            pltpu.SMEM(coarse_offset.shape, jnp.int32),
-            pltpu.VMEM(tissue_mask.shape, jnp.int32),
-            pltpu.SemaphoreType.DMA((3,)),
-        ],
+        in_specs=[pl.BlockSpec(memory_space=pl.ANY)],
+        out_specs=(VMEM,) * 7,
+        scratch_shapes=[pltpu.SMEM((3,), jnp.int32), pltpu.SemaphoreType.DMA],
         compiler_params=params(16),
-        cost_estimate=cost(1.5),
-    )(fine_offsets, coarse_offset, tissue_mask)
+        cost_estimate=cost(0.1),
+    )(jnp.concatenate([fine_offsets, coarse_offset]))
+    weights, left_rows, picks, chosen, forward_rows, inverse, inverse_rows = tables
+    low_bands = P_SIZE // STRIDE
+    uppers = []
+
+    def upper(group, *operands):
+        return pl.pallas_call(
+            functools.partial(upper_kernel, group),
+            out_shape=jax.ShapeDtypeStruct((bands - low_bands, P_SIZE, 2 * LANES), f32),
+            in_specs=[VMEM] * (4 + len(operands)),
+            out_specs=VMEM,
+            scratch_shapes=[
+                pltpu.VMEM((2, rows, 3 * LANES), bf16),
+                pltpu.VMEM((2, 2, 2 * rows, 2 * LANES), bf16),
+            ],
+            compiler_params=params(32),
+            cost_estimate=cost(0.1),
+        )(weights, left_rows, own_tile, other, *operands)
+
     got_even = exchanged(packed, "gx", 1)
     got_odd = lax.ppermute(packed[HALF:], "gx", [(i + 1, i) for i in range(1, count - 1, 2)])
-    steps = [packed[:HALF], got_even[:HALF]]
-    right = jnp.where(lax.axis_index("gx") % 2 == 0, got_even[HALF:], got_odd)
-    tiles = jnp.concatenate(steps, axis=0)
+    tiles = jnp.concatenate([packed[:HALF], got_even[:HALF]], axis=0)
     step = 2
-    while step < count:
+    while 2 * step < count:
         tiles = jnp.concatenate([tiles, exchanged(tiles, "gx", step)], axis=0)
         step *= 2
-    weights, left_rows, picks, chosen, mask, forward_rows, inverse, inverse_rows = tables
+    last_tiles = exchanged(tiles, "gx", step)
+    right = jnp.where(lax.axis_index("gx") % 2 == 0, got_even[HALF:], got_odd)
+    other_right = swapped(right)
     low_payload = jnp.concatenate([own_edge, right[:P_SIZE]], axis=1)
-    low_payload, weights = lax.optimization_barrier((low_payload, weights))
+    low_payload, other_right = lax.optimization_barrier((low_payload, other_right))
     own_low = from_later(low_payload, "gy", 1)
-    other_right = swapped(right)
+    uppers = [upper(group) for group in range(supers - 1)]
+    last_tiles, *uppers = lax.optimization_barrier((last_tiles, *uppers))
+    tiles = jnp.concatenate([tiles, last_tiles], axis=0)
     other_tiles = swapped(tiles)
-    other_low = swapped(own_low)
-    low_bands = P_SIZE // STRIDE
-    upper = pl.pallas_call(
-        upper_kernel,
-        out_shape=jax.ShapeDtypeStruct((bands - low_bands, P_SIZE, wide), f32),
-        in_specs=[VMEM] * 6,
-        out_specs=VMEM,
-        scratch_shapes=[
-            pltpu.VMEM((2, rows, width + LANES), bf16),
-            pltpu.VMEM((2, 2, 2 * rows, wide), bf16),
-        ],
-        compiler_params=params(32),
-        cost_estimate=cost(2.6),
-    )(weights, left_rows, own_tile, right, other, other_right)
-    other_tiles, upper = lax.optimization_barrier((other_tiles, upper))
+    uppers.append(upper(supers - 1, right, other_right))
+    other_tiles, *uppers = lax.optimization_barrier((other_tiles, *uppers))
     turns, base = pl.pallas_call(
         turn_kernel,
         out_shape=(
@@ -711,7 +711,7 @@
         out_specs=(VMEM,) * 2,
         scratch_shapes=[pltpu.VMEM((count, 2 * P_SIZE, LANES), f32)],
         compiler_params=params(32),
-        cost_estimate=cost(1.2),
+        cost_estimate=cost(0.1),
     )(
         forward_rows,
         inverse,
@@ -722,6 +722,26 @@
         tiles,
         other_tiles,
     )
+    def peak_scratch(count):
+        return [
+            pltpu.VMEM((count * P_SIZE, wide), bf16),
+            pltpu.VMEM((count * P_SIZE, wide), bf16),
+            pltpu.VMEM((P_SIZE, wide), f32),
+        ]
+
+    upper_bands = bands - low_bands
+    own_low, turns = lax.optimization_barrier((own_low, turns))
+    other_low = swapped(own_low)
+    upper_flow = pl.pallas_call(
+        functools.partial(peak_kernel, 0),
+        out_shape=jax.ShapeDtypeStruct((2, per_row, upper_bands), f32),
+        in_specs=[VMEM] * (5 + supers),
+        out_specs=VMEM,
+        scratch_shapes=peak_scratch(upper_bands),
+        compiler_params=params(40),
+        cost_estimate=cost(0.1),
+    )(inverse, inverse_rows, tissue_mask, base, turns, *uppers)
+    other_low, upper_flow = lax.optimization_barrier((other_low, upper_flow))
     lower = pl.pallas_call(
         lower_kernel,
         out_shape=jax.ShapeDtypeStruct((low_bands, P_SIZE, wide), f32),
@@ -732,29 +752,17 @@
             pltpu.VMEM((2, 2, 4 * P_SIZE, wide), bf16),
         ],
         compiler_params=params(32),
-        cost_estimate=cost(0.6),
+        cost_estimate=cost(0.1),
     )(weights, left_rows, own_tile, right, own_low, other, other_right, other_low)
     flow = pl.pallas_call(
-        peak_kernel,
+        functools.partial(lower_peak_kernel, upper_bands),
         out_shape=jax.ShapeDtypeStruct((2, 1, per_row, bands), f32),
         in_specs=[VMEM] * 7,
         out_specs=VMEM,
-        scratch_shapes=[
-            pltpu.VMEM((bands * P_SIZE, wide), bf16),
-            pltpu.VMEM((bands * P_SIZE, wide), bf16),
-            pltpu.VMEM((P_SIZE, wide), f32),
-        ],
+        scratch_shapes=peak_scratch(low_bands) + [pltpu.VMEM((2, per_row, low_bands), f32)],
         compiler_params=params(40),
-        cost_estimate=cost(3.5),
-    )(
-        inverse,
-        inverse_rows,
-        mask,
-        base,
-        turns,
-        upper,
-        lower,
-    )
+        cost_estimate=cost(0.1),
+    )(upper_flow, inverse, inverse_rows, tissue_mask, base, turns, lower)
     return jnp.swapaxes(flow, 2, 3)
 
 

time: 24.1 us -> 21.9 us (0.909)
  the two profiles are of different devices: /device:TPU:11 before, /device:TPU:15 now
where the time goes in v2:
time: 21.9 us; the launch traced here: 21.7 us
  Pallas kernels  9.85 us (45%)
  starting transfers between devices  6.05 us (28%)
  waiting for transfers between devices  3.82 us (17%)
  local copies, waits for them, and re-layouts  1.07 us (5%)
  between operations  0.84 us (4%)
    ppermute x1, waiting for transfers between devices, local(): lax.ppermute(packed[HALF:], 'gx', [(i + 1, i) for i in range(1, count - 1...  3.01 us
    pallas_call x2, Pallas kernels, upper(): pl.pallas_call(functools.partial(upper_kernel, group), out_shape=jax.Shap...  2.78 us
    ppermute x4, starting transfers between devices, swapped(): return lax.ppermute(value, 'gz', [(0, 1), (1, 0)])  2.29 us
    ppermute x1, starting transfers between devices, from_later(): lax.ppermute(value, axis, [(i, i - step) for i in range(step, lax.axis_si...  2.15 us
    pallas_call x1, Pallas kernels, local(): pl.pallas_call(functools.partial(peak_kernel, 0), out_shape=jax.ShapeDtyp...  2.08 us
    pallas_call x1, Pallas kernels, local(): pl.pallas_call(functools.partial(lower_peak_kernel, upper_bands), out_sha...  1.52 us
    pallas_call x1, Pallas kernels, local(): pl.pallas_call(turn_kernel, out_shape=(jax.ShapeDtypeStruct((2, supers, 4...  1.39 us
    ppermute x1, starting transfers between devices, local(): lax.ppermute(packed[HALF:], 'gx', [(i + 1, i) for i in range(1, count - 1...  1.28 us
  transfers between devices with their start and end apart: 8, of which 2 were waited for; matrix products, arithmetic and copies ran while one was open for 1% of the time, Pallas kernels for 34%

profile of v2, /device:TPU:15, one launch (start us, length us, event | category | flops | bytes accessed | tf_op | source)
XLA Modules:
  0.0 21.7 jit_solution(12762386725661452803)
XLA Ops:
  0.0 0.7 %collective-permute-start.5 = (bf16[512,512]{1,0:T(8,128)(2,1)}, bf16[512,512]{1,0:T(8,128)(2,1)S(1)}, u32[]{:S(2)}, u32[]{:S(2)}) collective-permute-start(bf16[512,512]{1,0:T(8,128)(2,1)} %bitcast.2), channel_id=1, source_target_pairs={{0,1},{1,0},{2,3},{3,2},{4,5},{5,4},{6,7},{7,6},{8,9},{9,8},{10,11... | collective-permute-start | bytes 1572872 | tf_op jit(solution)/shard_map/ppermute | solution.py:609
  0.7 0.0 copy-start
  0.7 1.0 %copy-done = bf16[1,512,512]{2,1,0:T(8,128)(2,1)S(1)} copy-done((bf16[1,512,512]{2,1,0:T(8,128)(2,1)S(1)}, bf16[1,512,512]{2,1,0:T(8,128)(2,1)}, u32[]{:S(2)}) %copy-start) | copy-done | bytes 524312
  1.7 0.4 %shard_map.46 = (bf16[512,512]{1,0:T(8,128)(2,1)S(1)}, bf16[64,512]{1,0:T(8,128)(2,1)S(1)}, bf16[288,128]{1,0:T(8,128)(2,1)S(1)}) custom-call(bf16[512,512]{1,0:T(8,128)(2,1)S(1)} %bitcast.3), custom_call_target="tpu_custom_call" | custom-call | bytes 15000000 | tf_op jit(solution)/shard_map/pallas_call | solution.py:637
  2.1 0.2 %collective-permute-start = (bf16[288,128]{1,0:T(8,128)(2,1)S(1)}, bf16[288,128]{1,0:T(8,128)(2,1)S(1)}, u32[]{:S(2)}, u32[]{:S(2)}) collective-permute-start(bf16[288,128]{1,0:T(8,128)(2,1)S(1)} %get-tuple-element.29), channel_id=1, source_target_pairs={{0,4},{4,0},{8,12},{12,8},{1,5},{5,1},{9,13},{13,9},{2,6},{6,2},{1... | collective-permute-start | bytes 221192 | tf_op jit(solution)/shard_map/ppermute | solution.py:601
  2.3 1.3 %collective-permute-start.1 = (bf16[256,128]{1,0:T(8,128)(2,1)S(1)}, bf16[256,128]{1,0:T(8,128)(2,1)S(1)}, u32[]{:S(2)}, u32[]{:S(2)}) collective-permute-start(bf16[256,128]{1,0:T(8,128)(2,1)S(1)} %slice.16), channel_id=1, source_target_pairs={{8,4},{9,5},{10,6},{11,7},{24,20},{25,21},{26,22},{27,23}} | collective-permute-start | bytes 196616 | tf_op jit(solution)/shard_map/ppermute | solution.py:686
  3.7 0.0 copy-start.2
  4.3 0.0 copy-done.2
  4.3 0.1 pad_add_fusion.offsets_in
  4.4 0.9 %shard_map.47 = (bf16[3,256,512]{2,1,0:T(8,128)(2,1)S(1)}, bf16[128,192]{1,0:T(8,128)(2,1)S(1)}, s32[2,2,8,128]{3,2,1,0:T(8,128)S(1)}, s32[16,8]{1,0:T(8,128)S(1...) custom-call(s32[3]{0:T(128)S(1)} %pad_add_fusion.offsets_in), custom_call_target="tpu_custom_call" | custom-call | bytes 300000 | tf_op jit(solution)/shard_map/pallas_call | solution.py:650
  5.3 3.0 %collective-permute-done.1 = bf16[256,128]{1,0:T(8,128)(2,1)S(1)} collective-permute-done((bf16[256,128]{1,0:T(8,128)(2,1)S(1)}, bf16[256,128]{1,0:T(8,128)(2,1)S(1)}, u32[]{:S(2)}, u32[]{:S(2)}) %collective-permute-start.1) | collective-permute-done | bytes 65568 | tf_op jit(solution)/shard_map/ppermute | solution.py:686
  8.3 0.0 collective-permute-done
  8.3 0.8 %collective-permute-start.2 = (bf16[256,128]{1,0:T(8,128)(2,1)S(1)}, bf16[256,128]{1,0:T(8,128)(2,1)S(1)}, u32[]{:S(2)}, u32[]{:S(2)}) collective-permute-start(bf16[256,128]{1,0:T(8,128)(2,1)S(1)} %slice_select_fusion.refs_0_.own_right_ref), channel_id=1, source_target_pairs={{0,1},{1,0},{2,3},{3,2},{4,5},{5,4},{6,7},{7,6},{8,9},{9,8},{10,11... | collective-permute-start | bytes 196616 | tf_op jit(solution)/shard_map/ppermute | solution.py:609
  9.2 0.1 collective-permute-start.4
  9.3 0.8 %collective-permute-done.2.refs_1_.other_right_ref = bf16[256,128]{1,0:T(8,128)(2,1)S(1)} collective-permute-done((bf16[256,128]{1,0:T(8,128)(2,1)S(1)}, bf16[256,128]{1,0:T(8,128)(2,1)S(1)}, u32[]{:S(2)}, u32[]{:S(2)}) %collective-permute-start.2) | collective-permute-done | bytes 65568 | tf_op jit(solution)/shard_map/ppermute | solution.py:609
  10.1 2.2 %collective-permute-start.3 = (bf16[64,640]{1,0:T(8,128)(2,1)S(1)}, bf16[64,640]{1,0:T(8,128)(2,1)S(1)}, u32[]{:S(2)}, u32[]{:S(2)}) collective-permute-start(bf16[64,640]{1,0:T(8,128)(2,1)S(1)} %pad_maximum_fusion), channel_id=1, source_target_pairs={{2,0},{3,1},{6,4},{7,5},{10,8},{11,9},{14,12},{15,13},{18,16},{19,... | collective-permute-start | bytes 245768 | tf_op jit(solution)/shard_map/ppermute | solution.py:605
  12.2 0.0 collective-permute-done.5.other_ref
  12.2 1.3 %shard_map.48.refs_0_ = f32[14,64,256]{2,1,0:T(8,128)S(1)} custom-call(bf16[3,256,512]{2,1,0:T(8,128)(2,1)S(1)} %get-tuple-element.34.weights, bf16[128,192]{1,0:T(8,128)(2,1)S(1)} %get-tuple-element.37.left_rows_ref, bf16[512,512]{1,0:T(8,128)(2,1)S(1)} %get-tuple-element.38.own_ref, bf16[512,512]{1,0:T(8,128)(2,1)S(1)} %collective-permute-done.5.other_ref), custom_call_target="tpu_custom_call" | custom-call | bytes 300000 | tf_op jit(solution)/shard_map/pallas_call | solution.py:672
  13.6 0.0 collective-permute-done.4
  13.6 0.7 %collective-permute-start.6 = (bf16[128,128]{1,0:T(8,128)(2,1)S(1)}, bf16[128,128]{1,0:T(8,128)(2,1)S(1)}, u32[]{:S(2)}, u32[]{:S(2)}) collective-permute-start(bf16[128,128]{1,0:T(8,128)(2,1)S(1)} %pad_maximum_fusion.1.own_part_ref), channel_id=1, source_target_pairs={{0,1},{1,0},{2,3},{3,2},{4,5},{5,4},{6,7},{7,6},{8,9},{9,8},{10,11... | collective-permute-start | bytes 98312 | tf_op jit(solution)/shard_map/ppermute | solution.py:609
  14.3 1.4 %shard_map.49.refs_1_ = f32[14,64,256]{2,1,0:T(8,128)S(1)} custom-call(bf16[3,256,512]{2,1,0:T(8,128)(2,1)S(1)} %get-tuple-element.34.weights, bf16[128,192]{1,0:T(8,128)(2,1)S(1)} %get-tuple-element.37.left_rows_ref, bf16[512,512]{1,0:T(8,128)(2,1)S(1)} %get-tuple-element.38.own_ref, bf16[512,512]{1,0:T(8,128)(2,1)S(1)} %collective-permute-done.5.other_ref, ...), custom_call_target="tpu_custom_call" | custom-call | bytes 300000 | tf_op jit(solution)/shard_map/pallas_call | solution.py:672
  15.8 0.0 collective-permute-done.6.other_part_ref
  15.8 0.0 copy-start.1
  15.8 1.4 %shard_map.50 = (f32[2,2,4,32,128]{4,3,2,1,0:T(8,128)S(1)}, f32[2,16,8]{2,1,0:T(8,128)S(1)}) custom-call(bf16[128,128]{1,0:T(8,128)(2,1)S(1)} %get-tuple-element.31.forward_rows_ref, bf16[256,512]{1,0:T(8,128)(2,1)S(1)} %get-tuple-element.32.inverse_ref.refs_0_, bf16[128,128]{1,0:T(8,128)(2,1)S(1)} %get-tuple-element.33.inverse_rows_ref.refs_1_, ...), custom_call_target="tpu_custom_call" | custom-call | bytes 300000 | tf_op jit(solution)/shard_map/pallas_call | solution.py:704
  17.2 0.0 collective-permute-done.3.own_low_ref
  17.2 0.1 collective-permute-start.7
  17.3 0.0 copy-done.1
  17.3 2.1 %shard_map.51.upper_flow_ref = f32[2,8,14]{2,1,0:T(8,128)S(1)} custom-call(bf16[256,512]{1,0:T(8,128)(2,1)S(1)} %get-tuple-element.32.inverse_ref.refs_0_, bf16[128,128]{1,0:T(8,128)(2,1)S(1)} %get-tuple-element.33.inverse_rows_ref.refs_1_, s32[16,16]{1,0:T(8,128)S(1)} %copy-done.1, f32[2,16,8]{2,1,0:T(8,128)S(1)} %get-tuple-element.45.base_ref.refs_3_, ...), custom_call_target="tpu_custom_call" | custom-call | bytes 300000 | tf_op jit(solution)/shard_map/pallas_call | solution.py:735
  19.3 0.0 collective-permute-done.7.other_low_ref
  19.3 0.8 %shard_map.52.refs_5_ = f32[2,64,512]{2,1,0:T(8,128)S(1)} custom-call(bf16[3,256,512]{2,1,0:T(8,128)(2,1)S(1)} %get-tuple-element.34.weights, bf16[128,192]{1,0:T(8,128)(2,1)S(1)} %get-tuple-element.37.left_rows_ref, bf16[512,512]{1,0:T(8,128)(2,1)S(1)} %get-tuple-element.38.own_ref, bf16[256,128]{1,0:T(8,128)(2,1)S(1)} %slice_select_fusion.refs_0_.own_right_ref, ...), custom_call_target="tpu_custom_call" | custom-call | bytes 300000 | tf_op jit(solution)/shard_map/pallas_call | solution.py:745
  20.2 1.5 %shard_map.53 = f32[2,1,8,16]{3,2,1,0:T(8,128)} custom-call(f32[2,8,14]{2,1,0:T(8,128)S(1)} %shard_map.51.upper_flow_ref, bf16[256,512]{1,0:T(8,128)(2,1)S(1)} %get-tuple-element.32.inverse_ref.refs_0_, bf16[128,128]{1,0:T(8,128)(2,1)S(1)} %get-tuple-element.33.inverse_rows_ref.refs_1_, s32[16,16]{1,0:T(8,128)S(1)} %copy-done.1, ...), custom_call_target="tpu_custom_call" | custom-call | bytes 300000 | tf_op jit(solution)/shard_map/pallas_call | solution.py:757
  (8 shorter events, 0.0 us)
Async XLA Ops:
  0.0 12.2 %collective-permute-start.5 = (bf16[512,512]{1,0:T(8,128)(2,1)}, bf16[512,512]{1,0:T(8,128)(2,1)S(1)}, u32[]{:S(2)}, u32[]{:S(2)}) collective-permute-start(bf16[512,512]{1,0:T(8,128)(2,1)} %bitcast.2), channel_id=1, source_target_pairs={{0,1},{1,0},{2,3},{3,2},{4,5},{5,4},{6,7},{7,6},{8,9},{9,8},{10,11... | collective-permute-start | bytes 1572872 | tf_op jit(solution)/shard_map/ppermute | solution.py:609
  0.7 1.0 %copy-start = (bf16[1,512,512]{2,1,0:T(8,128)(2,1)S(1)}, bf16[1,512,512]{2,1,0:T(8,128)(2,1)}, u32[]{:S(2)}) copy-start(bf16[1,512,512]{2,1,0:T(8,128)(2,1)} %param.4) | copy-start | bytes 1572868
  2.1 6.2 %collective-permute-start = (bf16[288,128]{1,0:T(8,128)(2,1)S(1)}, bf16[288,128]{1,0:T(8,128)(2,1)S(1)}, u32[]{:S(2)}, u32[]{:S(2)}) collective-permute-start(bf16[288,128]{1,0:T(8,128)(2,1)S(1)} %get-tuple-element.29), channel_id=1, source_target_pairs={{0,4},{4,0},{8,12},{12,8},{1,5},{5,1},{9,13},{13,9},{2,6},{6,2},{1... | collective-permute-start | bytes 221192 | tf_op jit(solution)/shard_map/ppermute | solution.py:601
  2.3 6.0 %collective-permute-start.1 = (bf16[256,128]{1,0:T(8,128)(2,1)S(1)}, bf16[256,128]{1,0:T(8,128)(2,1)S(1)}, u32[]{:S(2)}, u32[]{:S(2)}) collective-permute-start(bf16[256,128]{1,0:T(8,128)(2,1)S(1)} %slice.16), channel_id=1, source_target_pairs={{8,4},{9,5},{10,6},{11,7},{24,20},{25,21},{26,22},{27,23}} | collective-permute-start | bytes 196616 | tf_op jit(solution)/shard_map/ppermute | solution.py:686
  3.7 0.7 %copy-start.2 = (s32[2]{0:T(128)S(1)}, s32[2]{0:T(128)}, u32[]{:S(2)}) copy-start(s32[2]{0:T(128)} %param.5) | copy-start | bytes 28
  8.3 1.7 %collective-permute-start.2 = (bf16[256,128]{1,0:T(8,128)(2,1)S(1)}, bf16[256,128]{1,0:T(8,128)(2,1)S(1)}, u32[]{:S(2)}, u32[]{:S(2)}) collective-permute-start(bf16[256,128]{1,0:T(8,128)(2,1)S(1)} %slice_select_fusion.refs_0_.own_right_ref), channel_id=1, source_target_pairs={{0,1},{1,0},{2,3},{3,2},{4,5},{5,4},{6,7},{7,6},{8,9},{9,8},{10,11... | collective-permute-start | bytes 196616 | tf_op jit(solution)/shard_map/ppermute | solution.py:609
  9.2 4.4 %collective-permute-start.4 = (bf16[64,128]{1,0:T(8,128)(2,1)S(1)}, bf16[64,128]{1,0:T(8,128)(2,1)S(1)}, u32[]{:S(2)}, u32[]{:S(2)}) collective-permute-start(bf16[64,128]{1,0:T(8,128)(2,1)S(1)} %pad_maximum_fusion.2), channel_id=1, source_target_pairs={{0,8},{4,12},{8,0},{12,4},{1,9},{5,13},{9,1},{13,5},{2,10},{6,14},... | collective-permute-start | bytes 49160 | tf_op jit(solution)/shard_map/ppermute | solution.py:601
  10.1 7.1 %collective-permute-start.3 = (bf16[64,640]{1,0:T(8,128)(2,1)S(1)}, bf16[64,640]{1,0:T(8,128)(2,1)S(1)}, u32[]{:S(2)}, u32[]{:S(2)}) collective-permute-start(bf16[64,640]{1,0:T(8,128)(2,1)S(1)} %pad_maximum_fusion), channel_id=1, source_target_pairs={{2,0},{3,1},{6,4},{7,5},{10,8},{11,9},{14,12},{15,13},{18,16},{19,... | collective-permute-start | bytes 245768 | tf_op jit(solution)/shard_map/ppermute | solution.py:605
  13.6 2.1 %collective-permute-start.6 = (bf16[128,128]{1,0:T(8,128)(2,1)S(1)}, bf16[128,128]{1,0:T(8,128)(2,1)S(1)}, u32[]{:S(2)}, u32[]{:S(2)}) collective-permute-start(bf16[128,128]{1,0:T(8,128)(2,1)S(1)} %pad_maximum_fusion.1.own_part_ref), channel_id=1, source_target_pairs={{0,1},{1,0},{2,3},{3,2},{4,5},{5,4},{6,7},{7,6},{8,9},{9,8},{10,11... | collective-permute-start | bytes 98312 | tf_op jit(solution)/shard_map/ppermute | solution.py:609
  15.8 1.5 %copy-start.1 = (s32[16,16]{1,0:T(8,128)S(1)}, s32[16,16]{1,0:T(8,128)}, u32[]{:S(2)}) copy-start(s32[16,16]{1,0:T(8,128)} %refs_2_.1) | copy-start | bytes 3076
  17.2 2.2 %collective-permute-start.7 = (bf16[64,640]{1,0:T(8,128)(2,1)S(1)}, bf16[64,640]{1,0:T(8,128)(2,1)S(1)}, u32[]{:S(2)}, u32[]{:S(2)}) collective-permute-start(bf16[64,640]{1,0:T(8,128)(2,1)S(1)} %collective-permute-done.3.own_low_ref), channel_id=1, source_target_pairs={{0,1},{1,0},{2,3},{3,2},{4,5},{5,4},{6,7},{7,6},{8,9},{9,8},{10,11... | collective-permute-start | bytes 245768 | tf_op jit(solution)/shard_map/ppermute | solution.py:609

commit v3 on v2

--- a/solution.py
+++ b/solution.py
@@ -164,6 +164,18 @@
     along_rows = jnp.sum(factor * moment[:, window], axis=1, keepdims=True)
     along_columns = jnp.sum(weight * columns, axis=1, keepdims=True)
     return along_rows / bottom, along_columns / bottom
+
+
+def band_peaks(largest, total, moment):
+    bands, wide = largest.shape
+    largest, total, moment = (
+        jnp.transpose(x).reshape(wide // P_SIZE, P_SIZE, bands) for x in (largest, total, moment)
+    )
+    factor = jnp.exp2(largest - jnp.max(largest, axis=1, keepdims=True))
+    weight = factor * total
+    columns = signed(lax.broadcasted_iota(jnp.int32, (1, P_SIZE, 1), 1))
+    bottom = jnp.sum(weight, axis=1)
+    return jnp.sum(factor * moment, axis=1) / bottom, jnp.sum(weight * columns, axis=1) / bottom
 
 
 ROW_PARTS = ((0, 8, True), (8, HALF, False))
@@ -212,9 +224,15 @@
     packed_ref[half:] = edge.astype(bf16)
 
 
+def beside(high, low):
+    left = iota(high.shape, 1) < P_SIZE
+    return jnp.concatenate([high, jnp.where(left, low, 0.0)], axis=1).astype(bf16)
+
+
 def tables_kernel(
     offsets_in,
     weights_ref,
+    coarse_weights_ref,
     rows_ref,
     picks_ref,
     chosen_ref,
@@ -227,7 +245,7 @@
     copy = pltpu.make_async_copy(offsets_in, offsets_ref, sem)
     copy.start()
     count = lax.axis_size("gx")
-    bands, per_row = chosen_ref.shape
+    per_row, bands = chosen_ref.shape
     supers = per_row // GROUP
     side = lax.axis_index("gz")
     gx_place = lax.axis_index("gx")
@@ -244,23 +262,20 @@
     row = iota(shape, 0)
     lane = iota(shape, 1)
     basis = basis_values(row % HALF, row // HALF, lane % P_SIZE)
-    high, low = split(basis)
-    forward_rows_ref[:P_SIZE] = high
-    forward_rows_ref[P_SIZE:] = jnp.where(lane < P_SIZE, low.astype(f32), 0.0).astype(bf16)
-    wide_high = jnp.concatenate([high.astype(f32)] * 2, axis=1)
-    wide_low = jnp.concatenate([low.astype(f32)] * 2, axis=1)
+    high, low = (value.astype(f32) for value in split(basis))
+    forward_rows_ref[...] = beside(high, low)
+    wide_high = jnp.concatenate([high] * 2, axis=1)
+    wide_low = jnp.concatenate([low] * 2, axis=1)
     for kind in range(2):
         rows = slice(kind * HALF, (kind + 1) * HALF)
         for patch in range(GROUP):
             mine = iota((HALF, GROUP * P_SIZE), 1) // P_SIZE == patch
             at = (kind * GROUP + patch) * HALF
-            for part, value in enumerate((wide_high, wide_low)):
-                inverse_ref[at : at + HALF, part * 2 * LANES : (part + 1) * 2 * LANES] = jnp.where(
-                    mine, value[rows], 0.0
-                ).astype(bf16)
+            for part, value in enumerate((wide_high, wide_high, wide_low)):
+                begin = at + part * 2 * LANES
+                inverse_ref[begin : begin + HALF] = jnp.where(mine, value[rows], 0.0).astype(bf16)
     high, low = split(basis_values(lane % HALF, lane % P_SIZE // HALF, row))
-    inverse_rows_ref[:P_SIZE] = high
-    inverse_rows_ref[P_SIZE:] = jnp.where(lane < P_SIZE, low.astype(f32), 0.0).astype(bf16)
+    inverse_rows_ref[...] = beside(high.astype(f32), low.astype(f32))
     copy.wait()
     row_offset = offsets_ref[0]
     column_offset = offsets_ref[1]
@@ -269,9 +284,13 @@
     for t, shift in enumerate(shifts):
         moved = pltpu.roll(padded, shift, axis=0)
         for part, value in enumerate(split(moved)):
-            weights_ref[t, :, part * LANES : (part + 1) * LANES] = value
-            value = pltpu.roll(value.astype(f32), P_SIZE, axis=1).astype(bf16)
-            weights_ref[t, :, (part + 2) * LANES : (part + 3) * LANES] = value
+            rows = slice(part * 2 * LANES, (part + 1) * 2 * LANES)
+            turned = pltpu.roll(value.astype(f32), P_SIZE, axis=1).astype(bf16)
+            for order, entry in enumerate((value, turned)):
+                if t < 2:
+                    weights_ref[order, rows, t * LANES : (t + 1) * LANES] = entry
+                else:
+                    coarse_weights_ref[order, rows] = entry
     shape = (P_SIZE, 6 * STRIDE)
     number = iota(shape, 0)
     lane = iota(shape, 1)
@@ -292,9 +311,22 @@
         for g in range(supers):
             column = 2 * (g * GROUP + lane_row // HALF) + (t + side) % 2
             picks_ref[t, g] = jnp.broadcast_to(pick(column), (8, LANES))
-    shape = (bands, per_row)
-    parity = (iota(shape, 0) + side) % 2
-    chosen_ref[...] = pick(2 * iota(shape, 1) + parity)
+    shape = (per_row, bands)
+    parity = (iota(shape, 1) + side) % 2
+    chosen_ref[...] = pick(2 * iota(shape, 0) + parity)
+
+
+def column_transform(pixels, weights):
+    out = []
+    for order in range(2):
+        part = pixels[:, order * LANES : (order + 2) * LANES]
+        out.append(matmul(jnp.concatenate([part, part], axis=1), weights[order]))
+    return out
+
+
+def pair_up(a, b):
+    left = iota(a.shape, 1) < P_SIZE
+    return jnp.where(left, a, b), pltpu.roll(jnp.where(left, b, a), P_SIZE, axis=1)
 
 
 def forward_bands(image, stacked, weights, left_rows, first_band, out_ref):
@@ -303,18 +335,13 @@
     wide = out_ref.shape[2]
     blocks = tall // STRIDE
     supers = wide // (2 * LANES)
-    left = iota((tall, LANES), 1) < P_SIZE
     for s in range(2):
-        for t in range(2):
-            for g in range(supers):
-                lane = g * 2 * LANES
-                a = matmul(image[s, :, lane : lane + 2 * LANES], weights[t, :, : 2 * LANES])
-                b = matmul(image[s, :, lane + LANES : lane + 3 * LANES], weights[t, :, 2 * LANES :])
-                a = a[:, :LANES] + a[:, LANES:]
-                b = b[:, :LANES] + b[:, LANES:]
-                for part, value in enumerate(
-                    (jnp.where(left, a, b), pltpu.roll(jnp.where(left, b, a), P_SIZE, axis=1))
-                ):
+        for g in range(supers):
+            lane = g * 2 * LANES
+            a, b = column_transform(image[s, :, lane : lane + 3 * LANES], weights)
+            for t in range(2):
+                half = slice(t * LANES, (t + 1) * LANES)
+                for part, value in enumerate(pair_up(a[:, half], b[:, half])):
                     high, low = split(value)
                     at = slice(lane + part * LANES, lane + (part + 1) * LANES)
                     for n in range(blocks):
@@ -398,33 +425,27 @@
 
 
 def inverse_columns(high, low, table_ref):
-    table_high = table_ref[:, : 2 * LANES]
-    table_low = table_ref[:, 2 * LANES :]
-    return matmul(high, table_high) + matmul(high, table_low) + matmul(low, table_high)
+    return matmul(jnp.concatenate([high, low, high], axis=1), table_ref[...])
+
+
+def row_transform(table_ref, high, low):
+    return matmul(table_ref[:, : 3 * P_SIZE], jnp.concatenate([high, low, high], axis=0))
 
 
 def coarse_peaks(strip, forward_rows_ref, inverse_ref, inverse_rows_ref, weights, sign):
     supers = len(strip) * 2 // GROUP
-    left = iota((2 * P_SIZE, LANES), 1) < P_SIZE
     strip = strip + [jnp.zeros_like(strip[0])]
     columns = []
     for g in range(supers):
-        a, b = (
-            matmul(
-                jnp.concatenate(strip[2 * g + n : 2 * g + n + 2], axis=1),
-                weights[:, 2 * n * LANES : 2 * (n + 1) * LANES],
-            )
-            for n in range(2)
+        columns += pair_up(
+            *column_transform(jnp.concatenate(strip[2 * g : 2 * g + 3], axis=1), weights)
         )
-        a = a[:, :LANES] + a[:, LANES:]
-        b = b[:, :LANES] + b[:, LANES:]
-        columns += [jnp.where(left, a, b), pltpu.roll(jnp.where(left, b, a), P_SIZE, axis=1)]
     strips = jnp.concatenate(columns, axis=1)
     spectra = []
     for s in range(2):
-        high, low = split(strips[s * P_SIZE : (s + 1) * P_SIZE])
-        stack = jnp.concatenate([high, low], axis=0)
-        spectra.append(add_row_halves(matmul(forward_rows_ref[...], stack)))
+        spectra.append(
+            row_transform(forward_rows_ref, *split(strips[s * P_SIZE : (s + 1) * P_SIZE]))
+        )
     peaks = []
     for g in range(supers):
         own = quads(spectra[0], g)
@@ -443,10 +464,8 @@
         block = jnp.concatenate(
             [jnp.concatenate([cc, cs], axis=1), jnp.concatenate([sc, ss], axis=1)], axis=0
         )
-        high, low = split(block)
-        high, low = split(inverse_columns(high, low, inverse_ref))
-        stack = jnp.concatenate([high, low], axis=0)
-        sums = column_sums(add_row_halves(matmul(inverse_rows_ref[...], stack)))
+        found = inverse_columns(*split(block), inverse_ref)
+        sums = column_sums(row_transform(inverse_rows_ref, *split(found)))
         peaks += [patch_peak(*sums, n) for n in range(GROUP)]
     return peaks
 
@@ -480,7 +499,7 @@
         both = jnp.where(left, ordered[j], pltpu.roll(ordered[j + 1], P_SIZE, axis=1))
         strip.append(both.astype(bf16))
     peaks = coarse_peaks(
-        strip, forward_rows_ref, inverse_ref, inverse_rows_ref, weights.at[2], sign
+        strip, forward_rows_ref, inverse_ref, inverse_rows_ref, weights, sign
     )
     blended = []
     for axis in range(2):
@@ -532,35 +551,41 @@
 
 
 def peak_kernel(
-    first_band,
     inverse_ref,
     inverse_rows_ref,
     mask_ref,
     base_ref,
     turns,
+    lower_ref,
     *refs,
 ):
-    spectra, (out_ref, high_ref, low_ref, stacked) = refs[:-4], refs[-4:]
+    spectra, (out_ref, high_ref, low_ref) = refs[:-3], refs[-3:]
     supers = turns.shape[1]
     per_row = supers * GROUP
-    bands = spectra[0].shape[0]
+    upper_bands = spectra[0].shape[0]
+    bands = upper_bands + lower_ref.shape[0]
     for i in range(bands):
         for g in range(supers):
             lane = g * 2 * LANES
-            values = quads(spectra[g][i], 0) if len(spectra) > 1 else quads(spectra[0][i], g)
+            if i < upper_bands:
+                values = quads(spectra[g][i], 0)
+            else:
+                values = quads(lower_ref[i - upper_bands], g)
+            parts = []
             for begin, end, first in ROW_PARTS:
-                parts = coefficients(
-                    [x[begin:end] for x in values],
-                    [turns[(first_band + i) % 2, g, n, begin:end] for n in range(4)],
-                    first,
+                parts.append(
+                    coefficients(
+                        [x[begin:end] for x in values],
+                        [turns[i % 2, g, n, begin:end] for n in range(4)],
+                        first,
+                    )
                 )
-                stacked[begin:end, lane : lane + LANES] = parts[0]
-                stacked[begin:end, lane + LANES : lane + 2 * LANES] = parts[1]
-                stacked[HALF + begin : HALF + end, lane : lane + LANES] = parts[2]
-                stacked[HALF + begin : HALF + end, lane + LANES : lane + 2 * LANES] = parts[3]
-        high, low = split(stacked[...])
-        high_ref[i * P_SIZE : (i + 1) * P_SIZE] = high
-        low_ref[i * P_SIZE : (i + 1) * P_SIZE] = low
+            for n, (a, b) in enumerate(zip(*parts)):
+                high, low = split(jnp.concatenate([a, b], axis=0))
+                at = slice(i * P_SIZE + n // 2 * HALF, i * P_SIZE + (n // 2 + 1) * HALF)
+                lanes = slice(lane + n % 2 * LANES, lane + (n % 2 + 1) * LANES)
+                high_ref[at, lanes] = high
+                low_ref[at, lanes] = low
     for g in range(supers):
         at = slice(g * 2 * LANES, (g + 1) * 2 * LANES)
         high, low = split(inverse_columns(high_ref[:, at], low_ref[:, at], inverse_ref))
@@ -569,40 +594,39 @@
     sums = []
     for i in range(bands):
         rows = slice(i * P_SIZE, (i + 1) * P_SIZE)
-        stack = jnp.concatenate([high_ref[rows], low_ref[rows]], axis=0)
-        sums.append(column_sums(add_row_halves(matmul(inverse_rows_ref[...], stack))))
-    sums = [jnp.concatenate(parts, axis=0) for parts in zip(*sums)]
-    lane = iota((bands, LANES), 1)
-    found = [jnp.zeros((bands, LANES), f32) for _ in range(2)]
-    for m in range(per_row):
-        peak = patch_peak(*sums, m)
-        found = [jnp.where(lane == m, p, x) for p, x in zip(peak, found)]
-    shape = (2 * per_row, per_row)
-    columns = iota(shape, 0) - 2 * iota(shape, 1)
-    mask = mask_ref[first_band : first_band + bands].astype(f32).astype(bf16)
-    masks = [matmul(mask, (columns == n).astype(bf16)) for n in range(2)]
-    parity = (iota((bands, per_row), 0) + (first_band + lax.axis_index("gz"))) % 2
+        sums.append(column_sums(row_transform(inverse_rows_ref, high_ref[rows], low_ref[rows])))
+    found = band_peaks(*(jnp.concatenate(parts, axis=0) for parts in zip(*sums)))
+    shape = (per_row, 2 * per_row)
+    columns = iota(shape, 1) - 2 * iota(shape, 0)
+    mask = mask_ref[...].astype(f32).astype(bf16)
+    masks = [
+        lax.dot_general(
+            (columns == n).astype(bf16),
+            mask,
+            (((1,), (1,)), ((), ())),
+            preferred_element_type=f32,
+        )
+        for n in range(2)
+    ]
+    parity = (iota((per_row, bands), 1) + lax.axis_index("gz")) % 2
     chosen = jnp.where(parity == 0, masks[0], masks[1])
     for axis in range(2):
-        base = base_ref[axis, first_band : first_band + bands]
-        flow = base + chosen * found[axis][:, :per_row]
-        out_ref[axis] = jnp.transpose(flow)
-
-
-def lower_peak_kernel(first_band, upper_flow_ref, *refs):
-    out_ref, *scratch = refs[-5:]
-    flow, scratch = scratch[-1], scratch[:-1]
-    peak_kernel(first_band, *refs[:-5], flow, *scratch)
-    for axis in range(2):
-        out_ref[axis, 0] = jnp.concatenate([upper_flow_ref[axis], flow[axis]], axis=1)
+        out_ref[axis, 0] = base_ref[axis] + chosen * found[axis]
 
 
 def exchanged(value, axis, step):
     return lax.ppermute(value, axis, [(i, i ^ step) for i in range(lax.axis_size(axis))])
 
 
-def from_later(value, axis, step):
-    return lax.ppermute(value, axis, [(i, i - step) for i in range(step, lax.axis_size(axis))])
+def from_next(value, axis):
+    count = lax.axis_size(axis)
+    got = []
+    for odd in range(min(2, count - 1)):
+        pairs = [(i, i + 1) for i in range(odd, count - 1, 2)]
+        got.append(lax.ppermute(value, axis, pairs + [(j, i) for i, j in pairs]))
+    if len(got) < 2:
+        return got[0] if got else value
+    return jnp.where(lax.axis_index(axis) % 2 == 0, got[0], got[1])
 
 
 def swapped(value):
@@ -650,24 +674,36 @@
     tables = pl.pallas_call(
         tables_kernel,
         out_shape=(
-            jax.ShapeDtypeStruct((3, 2 * LANES, 4 * LANES), bf16),
+            jax.ShapeDtypeStruct((2, 4 * LANES, 2 * LANES), bf16),
+            jax.ShapeDtypeStruct((2, 4 * LANES, LANES), bf16),
             jax.ShapeDtypeStruct((2 * P_SIZE, 6 * STRIDE), bf16),
             jax.ShapeDtypeStruct((2, supers, 8, LANES), jnp.int32),
-            jax.ShapeDtypeStruct((bands, per_row), jnp.int32),
-            jax.ShapeDtypeStruct((2 * P_SIZE, LANES), bf16),
-            jax.ShapeDtypeStruct((2 * LANES, 4 * LANES), bf16),
-            jax.ShapeDtypeStruct((2 * P_SIZE, LANES), bf16),
+            jax.ShapeDtypeStruct((per_row, bands), jnp.int32),
+            jax.ShapeDtypeStruct((P_SIZE, 2 * LANES), bf16),
+            jax.ShapeDtypeStruct((6 * LANES, 2 * LANES), bf16),
+            jax.ShapeDtypeStruct((P_SIZE, 2 * LANES), bf16),
         ),
         in_specs=[pl.BlockSpec(memory_space=pl.ANY)],
-        out_specs=(VMEM,) * 7,
+        out_specs=(VMEM,) * 8,
         scratch_shapes=[pltpu.SMEM((3,), jnp.int32), pltpu.SemaphoreType.DMA],
         compiler_params=params(16),
         cost_estimate=cost(0.1),
     )(jnp.concatenate([fine_offsets, coarse_offset]))
-    weights, left_rows, picks, chosen, forward_rows, inverse, inverse_rows = tables
+    weights, coarse_weights, left_rows, picks, chosen, forward_rows, inverse, inverse_rows = tables
     low_bands = P_SIZE // STRIDE
-    uppers = []
-
+    got_even = exchanged(packed, "gx", 1)
+    got_odd = lax.ppermute(packed[HALF:], "gx", [(i + 1, i) for i in range(1, count - 1, 2)])
+    right = jnp.where(lax.axis_index("gx") % 2 == 0, got_even[HALF:], got_odd)
+    other_right = swapped(right)
+    low_payload = jnp.concatenate([own_edge, right[:P_SIZE]], axis=1)
+    low_payload, other_right = lax.optimization_barrier((low_payload, other_right))
+    own_low = from_next(low_payload, "gy")
+    tiles = jnp.concatenate([packed[:HALF], got_even[:HALF]], axis=0)
+    step = 2
+    while 2 * step < count:
+        tiles = jnp.concatenate([tiles, exchanged(tiles, "gx", step)], axis=0)
+        step *= 2
+    last_tiles = exchanged(tiles, "gx", step)
     def upper(group, *operands):
         return pl.pallas_call(
             functools.partial(upper_kernel, group),
@@ -682,30 +718,17 @@
             cost_estimate=cost(0.1),
         )(weights, left_rows, own_tile, other, *operands)
 
-    got_even = exchanged(packed, "gx", 1)
-    got_odd = lax.ppermute(packed[HALF:], "gx", [(i + 1, i) for i in range(1, count - 1, 2)])
-    tiles = jnp.concatenate([packed[:HALF], got_even[:HALF]], axis=0)
-    step = 2
-    while 2 * step < count:
-        tiles = jnp.concatenate([tiles, exchanged(tiles, "gx", step)], axis=0)
-        step *= 2
-    last_tiles = exchanged(tiles, "gx", step)
-    right = jnp.where(lax.axis_index("gx") % 2 == 0, got_even[HALF:], got_odd)
-    other_right = swapped(right)
-    low_payload = jnp.concatenate([own_edge, right[:P_SIZE]], axis=1)
-    low_payload, other_right = lax.optimization_barrier((low_payload, other_right))
-    own_low = from_later(low_payload, "gy", 1)
     uppers = [upper(group) for group in range(supers - 1)]
     last_tiles, *uppers = lax.optimization_barrier((last_tiles, *uppers))
     tiles = jnp.concatenate([tiles, last_tiles], axis=0)
     other_tiles = swapped(tiles)
     uppers.append(upper(supers - 1, right, other_right))
-    other_tiles, *uppers = lax.optimization_barrier((other_tiles, *uppers))
+    other_tiles, own_low, *uppers = lax.optimization_barrier((other_tiles, own_low, *uppers))
     turns, base = pl.pallas_call(
         turn_kernel,
         out_shape=(
             jax.ShapeDtypeStruct((2, supers, 4, HALF, LANES), f32),
-            jax.ShapeDtypeStruct((2, bands, per_row), f32),
+            jax.ShapeDtypeStruct((2, per_row, bands), f32),
         ),
         in_specs=[VMEM] * 8,
         out_specs=(VMEM,) * 2,
@@ -716,32 +739,13 @@
         forward_rows,
         inverse,
         inverse_rows,
-        weights,
+        coarse_weights,
         picks,
         chosen,
         tiles,
         other_tiles,
     )
-    def peak_scratch(count):
-        return [
-            pltpu.VMEM((count * P_SIZE, wide), bf16),
-            pltpu.VMEM((count * P_SIZE, wide), bf16),
-            pltpu.VMEM((P_SIZE, wide), f32),
-        ]
-
-    upper_bands = bands - low_bands
-    own_low, turns = lax.optimization_barrier((own_low, turns))
     other_low = swapped(own_low)
-    upper_flow = pl.pallas_call(
-        functools.partial(peak_kernel, 0),
-        out_shape=jax.ShapeDtypeStruct((2, per_row, upper_bands), f32),
-        in_specs=[VMEM] * (5 + supers),
-        out_specs=VMEM,
-        scratch_shapes=peak_scratch(upper_bands),
-        compiler_params=params(40),
-        cost_estimate=cost(0.1),
-    )(inverse, inverse_rows, tissue_mask, base, turns, *uppers)
-    other_low, upper_flow = lax.optimization_barrier((other_low, upper_flow))
     lower = pl.pallas_call(
         lower_kernel,
         out_shape=jax.ShapeDtypeStruct((low_bands, P_SIZE, wide), f32),
@@ -755,14 +759,14 @@
         cost_estimate=cost(0.1),
     )(weights, left_rows, own_tile, right, own_low, other, other_right, other_low)
     flow = pl.pallas_call(
-        functools.partial(lower_peak_kernel, upper_bands),
+        peak_kernel,
         out_shape=jax.ShapeDtypeStruct((2, 1, per_row, bands), f32),
-        in_specs=[VMEM] * 7,
+        in_specs=[VMEM] * (6 + supers),
         out_specs=VMEM,
-        scratch_shapes=peak_scratch(low_bands) + [pltpu.VMEM((2, per_row, low_bands), f32)],
+        scratch_shapes=[pltpu.VMEM((bands * P_SIZE, wide), bf16)] * 2,
         compiler_params=params(40),
         cost_estimate=cost(0.1),
-    )(upper_flow, inverse, inverse_rows, tissue_mask, base, turns, lower)
+    )(inverse, inverse_rows, tissue_mask, base, turns, lower, *uppers)
     return jnp.swapaxes(flow, 2, 3)
 
 

time: 21.9 us -> 21.2 us (0.968)
  the two profiles are of different devices: /device:TPU:15 before, /device:TPU:0 now
where the time goes in v3:
time: 21.2 us; the launch traced here: 21 us
  Pallas kernels  9.31 us (44%)
  starting transfers between devices  8.99 us (42%)
  local copies, waits for them, and re-layouts  1.07 us (5%)
  between operations  0.86 us (4%)
  waiting for transfers between devices  0.68 us (3%)
    ppermute x2, starting transfers between devices, exchanged(): lax.ppermute(value, axis, [(i, i ^ step) for i in range(lax.axis_size(axi...  5.64 us
    pallas_call x1, Pallas kernels, local(): pl.pallas_call(peak_kernel, out_shape=jax.ShapeDtypeStruct((2, 1, per_row...  2.9 us
    pallas_call x2, Pallas kernels, upper(): pl.pallas_call(functools.partial(upper_kernel, group), out_shape=jax.Shap...  2.85 us
    ppermute x1, starting transfers between devices, from_next(): got.append(lax.ppermute(value, axis, pairs + [(j, i) for i, j in pairs]))  1.56 us
    pallas_call x1, Pallas kernels, local(): pl.pallas_call(turn_kernel, out_shape=(jax.ShapeDtypeStruct((2, supers, 4...  1.45 us
    ppermute x4, starting transfers between devices, swapped(): return lax.ppermute(value, 'gz', [(0, 1), (1, 0)])  1.13 us
    unnamed x6, local copies, waits for them, and re-layouts  1.05 us
    pallas_call x1, Pallas kernels, local(): pl.pallas_call(lower_kernel, out_shape=jax.ShapeDtypeStruct((low_bands, P...  0.89 us
  transfers between devices with their start and end apart: 8, of which 1 were waited for; matrix products, arithmetic and copies ran while one was open for 1% of the time, Pallas kernels for 26%

profile of v3, /device:TPU:0, one launch (start us, length us, event | category | flops | bytes accessed | tf_op | source)
XLA Modules:
  0.0 21.0 jit_solution(4230546014594355808)
XLA Ops:
  0.0 0.5 %collective-permute-start.2 = (bf16[512,512]{1,0:T(8,128)(2,1)}, bf16[512,512]{1,0:T(8,128)(2,1)S(1)}, u32[]{:S(2)}, u32[]{:S(2)}) collective-permute-start(bf16[512,512]{1,0:T(8,128)(2,1)} %bitcast.2), channel_id=1, source_target_pairs={{0,1},{1,0},{2,3},{3,2},{4,5},{5,4},{6,7},{7,6},{8,9},{9,8},{10,11... | collective-permute-start | bytes 1572872 | tf_op jit(solution)/shard_map/ppermute | solution.py:633
  0.5 0.0 copy-start
  0.5 1.0 %copy-done = bf16[1,512,512]{2,1,0:T(8,128)(2,1)S(1)} copy-done((bf16[1,512,512]{2,1,0:T(8,128)(2,1)S(1)}, bf16[1,512,512]{2,1,0:T(8,128)(2,1)}, u32[]{:S(2)}) %copy-start) | copy-done | bytes 524312
  1.5 0.4 %shard_map.47 = (bf16[512,512]{1,0:T(8,128)(2,1)S(1)}, bf16[64,512]{1,0:T(8,128)(2,1)S(1)}, bf16[288,128]{1,0:T(8,128)(2,1)S(1)}) custom-call(bf16[512,512]{1,0:T(8,128)(2,1)S(1)} %bitcast.3), custom_call_target="tpu_custom_call" | custom-call | bytes 15000000 | tf_op jit(solution)/shard_map/pallas_call | solution.py:661
  1.9 2.6 %collective-permute-start = (bf16[288,128]{1,0:T(8,128)(2,1)S(1)}, bf16[288,128]{1,0:T(8,128)(2,1)S(1)}, u32[]{:S(2)}, u32[]{:S(2)}) collective-permute-start(bf16[288,128]{1,0:T(8,128)(2,1)S(1)} %get-tuple-element.32), channel_id=1, source_target_pairs={{0,4},{4,0},{8,12},{12,8},{1,5},{5,1},{9,13},{13,9},{2,6},{6,2},{1... | collective-permute-start | bytes 221192 | tf_op jit(solution)/shard_map/ppermute | solution.py:618
  4.5 0.7 %collective-permute-start.4 = (bf16[256,128]{1,0:T(8,128)(2,1)S(1)}, bf16[256,128]{1,0:T(8,128)(2,1)S(1)}, u32[]{:S(2)}, u32[]{:S(2)}) collective-permute-start(bf16[256,128]{1,0:T(8,128)(2,1)S(1)} %slice.18), channel_id=1, source_target_pairs={{8,4},{9,5},{10,6},{11,7},{24,20},{25,21},{26,22},{27,23}} | collective-permute-start | bytes 196616 | tf_op jit(solution)/shard_map/ppermute | solution.py:695
  5.2 0.0 copy-start.2
  5.9 0.0 copy-done.2
  5.9 0.1 pad_add_fusion.offsets_in
  6.0 0.9 %shard_map.46 = (bf16[2,512,256]{2,1,0:T(8,128)(2,1)S(1)}, bf16[2,512,128]{2,1,0:T(8,128)(2,1)S(1)}, bf16[128,192]{1,0:T(8,128)(2,1)S(1)}, s32[2,2,8,128]{3,2,1,...) custom-call(s32[3]{0:T(128)S(1)} %pad_add_fusion.offsets_in), custom_call_target="tpu_custom_call" | custom-call | bytes 300000 | tf_op jit(solution)/shard_map/pallas_call | solution.py:674
  6.8 0.0 collective-permute-done.4
  6.8 0.6 %collective-permute-done = bf16[288,128]{1,0:T(8,128)(2,1)S(1)} collective-permute-done((bf16[288,128]{1,0:T(8,128)(2,1)S(1)}, bf16[288,128]{1,0:T(8,128)(2,1)S(1)}, u32[]{:S(2)}, u32[]{:S(2)}) %collective-permute-start) | collective-permute-done | bytes 73760 | tf_op jit(solution)/shard_map/ppermute | solution.py:618
  7.5 0.1 collective-permute-start.5
  7.6 3.0 %collective-permute-start.1 = (bf16[64,128]{1,0:T(8,128)(2,1)S(1)}, bf16[64,128]{1,0:T(8,128)(2,1)S(1)}, u32[]{:S(2)}, u32[]{:S(2)}) collective-permute-start(bf16[64,128]{1,0:T(8,128)(2,1)S(1)} %pad_maximum_fusion.2), channel_id=1, source_target_pairs={{0,8},{4,12},{8,0},{12,4},{1,9},{5,13},{9,1},{13,5},{2,10},{6,14},... | collective-permute-start | bytes 49160 | tf_op jit(solution)/shard_map/ppermute | solution.py:618
  10.6 0.0 collective-permute-done.5.refs_1_.other_right_ref
  10.6 1.6 %collective-permute-start.6 = (bf16[64,640]{1,0:T(8,128)(2,1)S(1)}, bf16[64,640]{1,0:T(8,128)(2,1)S(1)}, u32[]{:S(2)}, u32[]{:S(2)}) collective-permute-start(bf16[64,640]{1,0:T(8,128)(2,1)S(1)} %pad_maximum_fusion), channel_id=1, source_target_pairs={{0,2},{2,0},{1,3},{3,1},{4,6},{6,4},{5,7},{7,5},{8,10},{10,8},{9,1... | collective-permute-start | bytes 245768 | tf_op jit(solution)/shard_map/ppermute | solution.py:626
  12.2 0.0 collective-permute-done.2.other_ref
  12.2 1.4 %shard_map.48.refs_0_ = f32[14,64,256]{2,1,0:T(8,128)S(1)} custom-call(bf16[2,512,256]{2,1,0:T(8,128)(2,1)S(1)} %get-tuple-element.33.weights, bf16[128,192]{1,0:T(8,128)(2,1)S(1)} %get-tuple-element.34.left_rows_ref, bf16[512,512]{1,0:T(8,128)(2,1)S(1)} %get-tuple-element.35.own_ref, bf16[512,512]{1,0:T(8,128)(2,1)S(1)} %collective-permute-done.2.other_ref), custom_call_target="tpu_custom_call" | custom-call | bytes 300000 | tf_op jit(solution)/shard_map/pallas_call | solution.py:708
  13.6 0.0 collective-permute-done.1
  13.6 0.1 collective-permute-start.3
  13.7 1.5 %shard_map.49.refs_1_ = f32[14,64,256]{2,1,0:T(8,128)S(1)} custom-call(bf16[2,512,256]{2,1,0:T(8,128)(2,1)S(1)} %get-tuple-element.33.weights, bf16[128,192]{1,0:T(8,128)(2,1)S(1)} %get-tuple-element.34.left_rows_ref, bf16[512,512]{1,0:T(8,128)(2,1)S(1)} %get-tuple-element.35.own_ref, bf16[512,512]{1,0:T(8,128)(2,1)S(1)} %collective-permute-done.2.other_ref, ...), custom_call_target="tpu_custom_call" | custom-call | bytes 300000 | tf_op jit(solution)/shard_map/pallas_call | solution.py:708
  15.1 0.0 collective-permute-done.6.own_low_ref
  15.2 0.0 collective-permute-done.3.other_part_ref
  15.2 0.5 %collective-permute-start.7 = (bf16[64,640]{1,0:T(8,128)(2,1)S(1)}, bf16[64,640]{1,0:T(8,128)(2,1)S(1)}, u32[]{:S(2)}, u32[]{:S(2)}) collective-permute-start(bf16[64,640]{1,0:T(8,128)(2,1)S(1)} %collective-permute-done.6.own_low_ref), channel_id=1, source_target_pairs={{0,1},{1,0},{2,3},{3,2},{4,5},{5,4},{6,7},{7,6},{8,9},{9,8},{10,11... | collective-permute-start | bytes 245768 | tf_op jit(solution)/shard_map/ppermute | solution.py:633
  15.7 1.5 %shard_map.50 = (f32[2,2,4,32,128]{4,3,2,1,0:T(8,128)S(1)}, f32[2,8,16]{2,1,0:T(8,128)S(1)}) custom-call(bf16[64,256]{1,0:T(8,128)(2,1)S(1)} %get-tuple-element.28.forward_rows_ref, bf16[768,256]{1,0:T(8,128)(2,1)S(1)} %get-tuple-element.26.inverse_ref, bf16[64,256]{1,0:T(8,128)(2,1)S(1)} %get-tuple-element.27.inverse_rows_ref, ...), custom_call_target="tpu_custom_call" | custom-call | bytes 300000 | tf_op jit(solution)/shard_map/pallas_call | solution.py:727
  17.2 0.0 collective-permute-done.7.other_low_ref
  17.2 0.0 copy-start.1
  17.2 0.9 %shard_map.51.lower_ref = f32[2,64,512]{2,1,0:T(8,128)S(1)} custom-call(bf16[2,512,256]{2,1,0:T(8,128)(2,1)S(1)} %get-tuple-element.33.weights, bf16[128,192]{1,0:T(8,128)(2,1)S(1)} %get-tuple-element.34.left_rows_ref, bf16[512,512]{1,0:T(8,128)(2,1)S(1)} %get-tuple-element.35.own_ref, bf16[256,128]{1,0:T(8,128)(2,1)S(1)} %slice_select_fusion.refs_0_.own_right_ref, ...), custom_call_target="tpu_custom_call" | custom-call | bytes 300000 | tf_op jit(solution)/shard_map/pallas_call | solution.py:749
  18.1 0.0 copy-done.1
  18.1 2.9 %shard_map.52 = f32[2,1,8,16]{3,2,1,0:T(8,128)} custom-call(bf16[768,256]{1,0:T(8,128)(2,1)S(1)} %get-tuple-element.26.inverse_ref, bf16[64,256]{1,0:T(8,128)(2,1)S(1)} %get-tuple-element.27.inverse_rows_ref, s32[16,16]{1,0:T(8,128)S(1)} %copy-done.1, f32[2,8,16]{2,1,0:T(8,128)S(1)} %get-tuple-element.42.base_ref, ...), custom_call_target="tpu_custom_call" | custom-call | bytes 300000 | tf_op jit(solution)/shard_map/pallas_call | solution.py:761
  (8 shorter events, 0.0 us)
Async XLA Ops:
  0.0 12.2 %collective-permute-start.2 = (bf16[512,512]{1,0:T(8,128)(2,1)}, bf16[512,512]{1,0:T(8,128)(2,1)S(1)}, u32[]{:S(2)}, u32[]{:S(2)}) collective-permute-start(bf16[512,512]{1,0:T(8,128)(2,1)} %bitcast.2), channel_id=1, source_target_pairs={{0,1},{1,0},{2,3},{3,2},{4,5},{5,4},{6,7},{7,6},{8,9},{9,8},{10,11... | collective-permute-start | bytes 1572872 | tf_op jit(solution)/shard_map/ppermute | solution.py:633
  0.5 1.0 %copy-start = (bf16[1,512,512]{2,1,0:T(8,128)(2,1)S(1)}, bf16[1,512,512]{2,1,0:T(8,128)(2,1)}, u32[]{:S(2)}) copy-start(bf16[1,512,512]{2,1,0:T(8,128)(2,1)} %param.4) | copy-start | bytes 1572868
  1.9 5.6 %collective-permute-start = (bf16[288,128]{1,0:T(8,128)(2,1)S(1)}, bf16[288,128]{1,0:T(8,128)(2,1)S(1)}, u32[]{:S(2)}, u32[]{:S(2)}) collective-permute-start(bf16[288,128]{1,0:T(8,128)(2,1)S(1)} %get-tuple-element.32), channel_id=1, source_target_pairs={{0,4},{4,0},{8,12},{12,8},{1,5},{5,1},{9,13},{13,9},{2,6},{6,2},{1... | collective-permute-start | bytes 221192 | tf_op jit(solution)/shard_map/ppermute | solution.py:618
  4.5 2.3 %collective-permute-start.4 = (bf16[256,128]{1,0:T(8,128)(2,1)S(1)}, bf16[256,128]{1,0:T(8,128)(2,1)S(1)}, u32[]{:S(2)}, u32[]{:S(2)}) collective-permute-start(bf16[256,128]{1,0:T(8,128)(2,1)S(1)} %slice.18), channel_id=1, source_target_pairs={{8,4},{9,5},{10,6},{11,7},{24,20},{25,21},{26,22},{27,23}} | collective-permute-start | bytes 196616 | tf_op jit(solution)/shard_map/ppermute | solution.py:695
  5.2 0.7 %copy-start.2 = (s32[2]{0:T(128)S(1)}, s32[2]{0:T(128)}, u32[]{:S(2)}) copy-start(s32[2]{0:T(128)} %param.5) | copy-start | bytes 28
  7.5 3.1 %collective-permute-start.5 = (bf16[256,128]{1,0:T(8,128)(2,1)S(1)}, bf16[256,128]{1,0:T(8,128)(2,1)S(1)}, u32[]{:S(2)}, u32[]{:S(2)}) collective-permute-start(bf16[256,128]{1,0:T(8,128)(2,1)S(1)} %slice_select_fusion.refs_0_.own_right_ref), channel_id=1, source_target_pairs={{0,1},{1,0},{2,3},{3,2},{4,5},{5,4},{6,7},{7,6},{8,9},{9,8},{10,11... | collective-permute-start | bytes 196616 | tf_op jit(solution)/shard_map/ppermute | solution.py:633
  7.6 6.0 %collective-permute-start.1 = (bf16[64,128]{1,0:T(8,128)(2,1)S(1)}, bf16[64,128]{1,0:T(8,128)(2,1)S(1)}, u32[]{:S(2)}, u32[]{:S(2)}) collective-permute-start(bf16[64,128]{1,0:T(8,128)(2,1)S(1)} %pad_maximum_fusion.2), channel_id=1, source_target_pairs={{0,8},{4,12},{8,0},{12,4},{1,9},{5,13},{9,1},{13,5},{2,10},{6,14},... | collective-permute-start | bytes 49160 | tf_op jit(solution)/shard_map/ppermute | solution.py:618
  10.6 4.6 %collective-permute-start.6 = (bf16[64,640]{1,0:T(8,128)(2,1)S(1)}, bf16[64,640]{1,0:T(8,128)(2,1)S(1)}, u32[]{:S(2)}, u32[]{:S(2)}) collective-permute-start(bf16[64,640]{1,0:T(8,128)(2,1)S(1)} %pad_maximum_fusion), channel_id=1, source_target_pairs={{0,2},{2,0},{1,3},{3,1},{4,6},{6,4},{5,7},{7,5},{8,10},{10,8},{9,1... | collective-permute-start | bytes 245768 | tf_op jit(solution)/shard_map/ppermute | solution.py:626
  13.6 1.6 %collective-permute-start.3 = (bf16[128,128]{1,0:T(8,128)(2,1)S(1)}, bf16[128,128]{1,0:T(8,128)(2,1)S(1)}, u32[]{:S(2)}, u32[]{:S(2)}) collective-permute-start(bf16[128,128]{1,0:T(8,128)(2,1)S(1)} %pad_maximum_fusion.1.own_part_ref), channel_id=1, source_target_pairs={{0,1},{1,0},{2,3},{3,2},{4,5},{5,4},{6,7},{7,6},{8,9},{9,8},{10,11... | collective-permute-start | bytes 98312 | tf_op jit(solution)/shard_map/ppermute | solution.py:633
  15.2 2.0 %collective-permute-start.7 = (bf16[64,640]{1,0:T(8,128)(2,1)S(1)}, bf16[64,640]{1,0:T(8,128)(2,1)S(1)}, u32[]{:S(2)}, u32[]{:S(2)}) collective-permute-start(bf16[64,640]{1,0:T(8,128)(2,1)S(1)} %collective-permute-done.6.own_low_ref), channel_id=1, source_target_pairs={{0,1},{1,0},{2,3},{3,2},{4,5},{5,4},{6,7},{7,6},{8,9},{9,8},{10,11... | collective-permute-start | bytes 245768 | tf_op jit(solution)/shard_map/ppermute | solution.py:633
  17.2 0.9 %copy-start.1 = (s32[16,16]{1,0:T(8,128)S(1)}, s32[16,16]{1,0:T(8,128)}, u32[]{:S(2)}) copy-start(s32[16,16]{1,0:T(8,128)} %mask_ref.1) | copy-start | bytes 3076

commit v4 on v3

--- a/solution.py
+++ b/solution.py
@@ -15,7 +15,6 @@
 LANES = 128
 GROUP = LANES // HALF
 SHARPNESS = 12.0
-PARTS = 1
 SCALE = SHARPNESS / float(P_SIZE) ** 4 * math.log2(math.e)
 
 f32 = jnp.float32
@@ -58,6 +57,14 @@
     return jnp.where(flip, -total, total)
 
 
+def quotient(number, divisor):
+    return number >> (divisor.bit_length() - 1)
+
+
+def remainder(number, divisor):
+    return number & (divisor - 1)
+
+
 def iota(shape, axis):
     return lax.broadcasted_iota(jnp.int32, shape, axis)
 
@@ -77,7 +84,7 @@
 
 
 def first_lane(shape):
-    return iota(shape, 1) % HALF == 0
+    return remainder(iota(shape, 1), HALF) == 0
 
 
 def half_spectra(cc, cs, sc, ss, first):
@@ -153,19 +160,6 @@
     return largest, jnp.sum(weights, axis=0, keepdims=True), jnp.sum(weights * rows, axis=0, keepdims=True)
 
 
-def patch_peak(largest, total, moment, patch):
-    window = slice(patch * P_SIZE, (patch + 1) * P_SIZE)
-    top = largest[:, window]
-    peak = jnp.max(top, axis=1, keepdims=True)
-    factor = jnp.exp2(top - peak)
-    weight = factor * total[:, window]
-    columns = signed(iota((1, P_SIZE), 1))
-    bottom = jnp.sum(weight, axis=1, keepdims=True)
-    along_rows = jnp.sum(factor * moment[:, window], axis=1, keepdims=True)
-    along_columns = jnp.sum(weight * columns, axis=1, keepdims=True)
-    return along_rows / bottom, along_columns / bottom
-
-
 def band_peaks(largest, total, moment):
     bands, wide = largest.shape
     largest, total, moment = (
@@ -197,31 +191,23 @@
     return jnp.concatenate([wide, pltpu.roll(wide, P_SIZE, axis=1)], axis=0).astype(bf16)
 
 
-def prepare_kernel(tile_ref, out_ref, low_ref, packed_ref, sem):
+def prepare_kernel(tile_ref, out_ref, low_ref, packed_ref):
     rows, width = tile_ref.shape
     columns = width // DOWN
-    chunk = rows // PARTS
-    copies = []
-    for n in range(PARTS):
-        at = pl.ds(n * chunk, chunk)
-        copies.append(pltpu.make_async_copy(tile_ref.at[at], out_ref.at[at], sem.at[n]))
-        copies[-1].start()
-    pick = (iota((width, LANES), 0) // DOWN == iota((width, LANES), 1) % columns).astype(bf16)
+    pick = quotient(iota((width, LANES), 0), DOWN) == remainder(iota((width, LANES), 1), columns)
+    pick = pick.astype(bf16)
     left = iota((columns // 2, LANES), 1) < P_SIZE
-    sums = []
-    for n in range(PARTS):
-        copies[n].wait()
-        part = matmul(out_ref[n * chunk : (n + 1) * chunk], pick)
-        sums.append(jnp.sum(part.reshape(chunk // DOWN, DOWN, LANES), axis=1))
-    coarse = jnp.concatenate(sums, axis=0) / DOWN
+    sums = matmul(tile_ref[...], pick)
+    coarse = jnp.sum(sums.reshape(rows // DOWN, DOWN, LANES), axis=1) / DOWN
     half = coarse.shape[0] // 2
     packed_ref[:half] = jnp.where(left, coarse[:half], coarse[half:]).astype(bf16)
-    low_ref[...] = out_ref[:P_SIZE]
-    edge = out_ref[:, :LANES].astype(f32)
+    low_ref[...] = tile_ref[:P_SIZE]
+    edge = tile_ref[:, :LANES].astype(f32)
     half_rows = rows // 2
     left = iota((half_rows, LANES), 1) < P_SIZE
     edge = jnp.where(left, edge[:half_rows], pltpu.roll(edge[half_rows:], P_SIZE, axis=1))
     packed_ref[half:] = edge.astype(bf16)
+    out_ref[...] = tile_ref[...]
 
 
 def beside(high, low):
@@ -239,11 +225,11 @@
     forward_rows_ref,
     inverse_ref,
     inverse_rows_ref,
-    offsets_ref,
-    sem,
 ):
-    copy = pltpu.make_async_copy(offsets_in, offsets_ref, sem)
-    copy.start()
+    offsets = offsets_in[...].astype(f32).reshape(1, 3)
+    row_offset, column_offset, coarse_offset = (
+        jnp.max(offsets[:, n : n + 1]).astype(jnp.int32) for n in range(3)
+    )
     count = lax.axis_size("gx")
     per_row, bands = chosen_ref.shape
     supers = per_row // GROUP
@@ -253,15 +239,15 @@
     lane = iota(shape, 1)
     row = iota(shape, 0)
     values = jnp.where(
-        row // P_SIZE == lane % P_SIZE // HALF,
-        basis_values(lane % HALF, lane // P_SIZE, row % P_SIZE),
+        quotient(row, P_SIZE) == quotient(remainder(lane, P_SIZE), HALF),
+        basis_values(remainder(lane, HALF), quotient(lane, P_SIZE), remainder(row, P_SIZE)),
         0.0,
     )
     padded = jnp.concatenate([values, jnp.zeros((2 * P_SIZE, LANES), f32)], axis=0)
     shape = (P_SIZE, LANES)
     row = iota(shape, 0)
     lane = iota(shape, 1)
-    basis = basis_values(row % HALF, row // HALF, lane % P_SIZE)
+    basis = basis_values(remainder(row, HALF), quotient(row, HALF), remainder(lane, P_SIZE))
     high, low = (value.astype(f32) for value in split(basis))
     forward_rows_ref[...] = beside(high, low)
     wide_high = jnp.concatenate([high] * 2, axis=1)
@@ -269,17 +255,14 @@
     for kind in range(2):
         rows = slice(kind * HALF, (kind + 1) * HALF)
         for patch in range(GROUP):
-            mine = iota((HALF, GROUP * P_SIZE), 1) // P_SIZE == patch
+            mine = quotient(iota((HALF, GROUP * P_SIZE), 1), P_SIZE) == patch
             at = (kind * GROUP + patch) * HALF
             for part, value in enumerate((wide_high, wide_high, wide_low)):
                 begin = at + part * 2 * LANES
                 inverse_ref[begin : begin + HALF] = jnp.where(mine, value[rows], 0.0).astype(bf16)
-    high, low = split(basis_values(lane % HALF, lane % P_SIZE // HALF, row))
+    kind = quotient(remainder(lane, P_SIZE), HALF)
+    high, low = split(basis_values(remainder(lane, HALF), kind, row))
     inverse_rows_ref[...] = beside(high.astype(f32), low.astype(f32))
-    copy.wait()
-    row_offset = offsets_ref[0]
-    column_offset = offsets_ref[1]
-    coarse_offset = offsets_ref[2]
     shifts = [column_offset + STRIDE * ((t + side) % 2) for t in range(2)] + [coarse_offset]
     for t, shift in enumerate(shifts):
         moved = pltpu.roll(padded, shift, axis=0)
@@ -294,34 +277,38 @@
     shape = (P_SIZE, 6 * STRIDE)
     number = iota(shape, 0)
     lane = iota(shape, 1)
-    place = lane // P_SIZE * STRIDE + lane % STRIDE - row_offset
+    place = quotient(lane, P_SIZE) * STRIDE + remainder(lane, STRIDE) - row_offset
     values = jnp.where(
-        (place >= 0) & (place < P_SIZE), basis_values(number % HALF, number // HALF, place), 0.0
+        (place >= 0) & (place < P_SIZE),
+        basis_values(remainder(number, HALF), quotient(number, HALF), place),
+        0.0,
     )
     high, low = split(values)
-    is_low = lane % P_SIZE >= STRIDE
+    is_low = remainder(lane, P_SIZE) >= STRIDE
     rows_ref[:P_SIZE] = high
     rows_ref[P_SIZE:] = jnp.where(is_low, 0.0, low.astype(f32)).astype(bf16)
     def pick(column):
         centre = (gx_place * (2 * per_row) + column) * STRIDE + column_offset + P_SIZE // 2
-        return jnp.clip((centre // DOWN - coarse_offset) // P_SIZE, 0, count - 1)
+        return jnp.clip(quotient(quotient(centre, DOWN) - coarse_offset, P_SIZE), 0, count - 1)
 
     lane_row = iota((1, LANES), 1)
     for t in range(2):
         for g in range(supers):
-            column = 2 * (g * GROUP + lane_row // HALF) + (t + side) % 2
+            column = 2 * (g * GROUP + quotient(lane_row, HALF)) + remainder(t + side, 2)
             picks_ref[t, g] = jnp.broadcast_to(pick(column), (8, LANES))
     shape = (per_row, bands)
-    parity = (iota(shape, 1) + side) % 2
+    parity = remainder(iota(shape, 1) + side, 2)
     chosen_ref[...] = pick(2 * iota(shape, 0) + parity)
 
 
-def column_transform(pixels, weights):
+def column_transform(strips, weights):
+    rows = strips[0].shape[0]
     out = []
     for order in range(2):
-        part = pixels[:, order * LANES : (order + 2) * LANES]
-        out.append(matmul(jnp.concatenate([part, part], axis=1), weights[order]))
-    return out
+        part = [x[:, order * LANES : (order + 2) * LANES] for x in strips]
+        left = jnp.concatenate([jnp.concatenate([x, x], axis=1) for x in part], axis=0)
+        out.append(matmul(left, weights[order]))
+    return [[x[n * rows : (n + 1) * rows] for x in out] for n in range(len(strips))]
 
 
 def pair_up(a, b):
@@ -335,19 +322,19 @@
     wide = out_ref.shape[2]
     blocks = tall // STRIDE
     supers = wide // (2 * LANES)
-    for s in range(2):
-        for g in range(supers):
-            lane = g * 2 * LANES
-            a, b = column_transform(image[s, :, lane : lane + 3 * LANES], weights)
-            for t in range(2):
-                half = slice(t * LANES, (t + 1) * LANES)
-                for part, value in enumerate(pair_up(a[:, half], b[:, half])):
-                    high, low = split(value)
-                    at = slice(lane + part * LANES, lane + (part + 1) * LANES)
-                    for n in range(blocks):
-                        block = slice(n * STRIDE, (n + 1) * STRIDE)
-                        stacked[s, t, 2 * n * STRIDE : (2 * n + 1) * STRIDE, at] = high[block]
-                        stacked[s, t, (2 * n + 1) * STRIDE : (2 * n + 2) * STRIDE, at] = low[block]
+    places = [(s, g) for s in range(2) for g in range(supers)]
+    strips = [image[s, :, g * 2 * LANES : (2 * g + 3) * LANES] for s, g in places]
+    for (s, g), (a, b) in zip(places, column_transform(strips, weights)):
+        lane = g * 2 * LANES
+        for t in range(2):
+            half = slice(t * LANES, (t + 1) * LANES)
+            for part, value in enumerate(pair_up(a[:, half], b[:, half])):
+                high, low = split(value)
+                at = slice(lane + part * LANES, lane + (part + 1) * LANES)
+                for n in range(blocks):
+                    block = slice(n * STRIDE, (n + 1) * STRIDE)
+                    stacked[s, t, 2 * n * STRIDE : (2 * n + 1) * STRIDE, at] = high[block]
+                    stacked[s, t, (2 * n + 1) * STRIDE : (2 * n + 2) * STRIDE, at] = low[block]
     sign = jnp.where(lax.axis_index("gz") == 0, 1.0, -1.0).astype(f32)
     for i in range(bands):
         spectra = []
@@ -437,9 +424,8 @@
     strip = strip + [jnp.zeros_like(strip[0])]
     columns = []
     for g in range(supers):
-        columns += pair_up(
-            *column_transform(jnp.concatenate(strip[2 * g : 2 * g + 3], axis=1), weights)
-        )
+        (pair,) = column_transform([jnp.concatenate(strip[2 * g : 2 * g + 3], axis=1)], weights)
+        columns += pair_up(*pair)
     strips = jnp.concatenate(columns, axis=1)
     spectra = []
     for s in range(2):
@@ -466,8 +452,9 @@
         )
         found = inverse_columns(*split(block), inverse_ref)
         sums = column_sums(row_transform(inverse_rows_ref, *split(found)))
-        peaks += [patch_peak(*sums, n) for n in range(GROUP)]
-    return peaks
+        wide = [jnp.broadcast_to(x, (LANES, GROUP * P_SIZE)) for x in sums]
+        peaks.append(band_peaks(*wide))
+    return [jnp.concatenate(parts, axis=0) for parts in zip(*peaks)]
 
 
 def turn_kernel(
@@ -491,41 +478,37 @@
     for step in range(count):
         for part, ref in enumerate((own_part_ref, other_part_ref)):
             tile = ref[step * HALF : (step + 1) * HALF].astype(f32)
-            tile = jnp.concatenate([tile, pltpu.roll(tile, P_SIZE, axis=1)], axis=0)
-            ordered[place ^ step, part * P_SIZE : (part + 1) * P_SIZE] = tile
+            turned = pltpu.roll(tile, P_SIZE, axis=1)
+            rows = slice(part * P_SIZE, (part + 1) * P_SIZE)
+            ordered[place ^ step, 0, rows] = jnp.concatenate([tile, turned], axis=0)
+            ordered[place ^ step, 1, rows] = jnp.concatenate([turned, tile], axis=0)
     left = iota((2 * P_SIZE, LANES), 1) < P_SIZE
     strip = []
     for j in range(0, count, 2):
-        both = jnp.where(left, ordered[j], pltpu.roll(ordered[j + 1], P_SIZE, axis=1))
-        strip.append(both.astype(bf16))
+        strip.append(jnp.where(left, ordered[j, 0], ordered[j + 1, 1]).astype(bf16))
     peaks = coarse_peaks(
         strip, forward_rows_ref, inverse_ref, inverse_rows_ref, weights, sign
     )
-    blended = []
-    for axis in range(2):
-        values = [peak[axis] for peak in peaks]
-        mean = sum(values[1:], values[0]) / count
-        blended.append([(0.5 * DOWN) * (value + mean) for value in values])
+    blended = [
+        (0.5 * DOWN) * (peak + jnp.sum(peak, axis=0, keepdims=True) / count) for peak in peaks
+    ]
 
     def prior(pick):
-        out = []
-        for values in blended:
-            chosen = jnp.broadcast_to(values[0], pick.shape)
-            for j in range(1, count):
-                chosen = jnp.where(pick == j, values[j], chosen)
-            out.append(chosen)
-        return out
+        choice = pick == iota((count, LANES), 0)
+        return [
+            jnp.sum(jnp.where(choice, values, 0.0), axis=0, keepdims=True) for values in blended
+        ]
 
     shape = (HALF, LANES)
-    frequency_y = iota(shape, 0).astype(f32) / P_SIZE
+    frequency_y = iota(shape, 0).astype(f32) * (1.0 / P_SIZE)
     l0 = first_lane(shape)
     r0 = iota(shape, 0) == 0
     lane_row = iota((1, LANES), 1)
-    frequency_x = (lane_row % HALF).astype(f32) / P_SIZE
+    frequency_x = remainder(lane_row, HALF).astype(f32) * (1.0 / P_SIZE)
     for t in range(2):
         for g in range(supers):
             dy, dx = (
-                value - P_SIZE * jnp.round(value / P_SIZE) for value in prior(picks_ref[t, g, :1])
+                value - P_SIZE * jnp.round(value * (1.0 / P_SIZE)) for value in prior(picks_ref[t, g, :1])
             )
             turn_y = nearest(frequency_y * dy)
             turn_x = nearest(frequency_x * dx)
@@ -545,9 +528,12 @@
             ends = (1.0, half_x, half_y, half_both)
             for n in range(4):
                 turns[t, g, n] = SCALE * jnp.where(corner, ends[n], 2.0 * turn[n])
-    base = prior(chosen_ref[...])
-    for axis in range(2):
-        base_ref[axis] = base[axis]
+    pick = chosen_ref[...]
+    for axis, values in enumerate(blended):
+        base = jnp.zeros(pick.shape, f32)
+        for j in range(count):
+            base = jnp.where(pick == j, values[j : j + 1, : pick.shape[1]], base)
+        base_ref[axis] = base
 
 
 def peak_kernel(
@@ -608,7 +594,7 @@
         )
         for n in range(2)
     ]
-    parity = (iota((per_row, bands), 1) + lax.axis_index("gz")) % 2
+    parity = remainder(iota((per_row, bands), 1) + lax.axis_index("gz"), 2)
     chosen = jnp.where(parity == 0, masks[0], masks[1])
     for axis in range(2):
         out_ref[axis, 0] = base_ref[axis] + chosen * found[axis]
@@ -657,7 +643,6 @@
     assert count % GROUP == 0 and count & (count - 1) == 0
     wide = width
     supers = width // (2 * LANES)
-    other = swapped(own)
     own_tile, own_edge, packed = pl.pallas_call(
         prepare_kernel,
         out_shape=(
@@ -665,12 +650,12 @@
             jax.ShapeDtypeStruct((P_SIZE, width), bf16),
             jax.ShapeDtypeStruct((HALF + rows // 2, LANES), bf16),
         ),
-        in_specs=[pl.BlockSpec(memory_space=pltpu.HBM)],
+        in_specs=[VMEM],
         out_specs=(VMEM,) * 3,
-        scratch_shapes=[pltpu.SemaphoreType.DMA((PARTS,))],
         compiler_params=params(16),
         cost_estimate=cost(5.0),
     )(own)
+    offsets = jnp.concatenate([fine_offsets, coarse_offset])
     tables = pl.pallas_call(
         tables_kernel,
         out_shape=(
@@ -683,14 +668,14 @@
             jax.ShapeDtypeStruct((6 * LANES, 2 * LANES), bf16),
             jax.ShapeDtypeStruct((P_SIZE, 2 * LANES), bf16),
         ),
-        in_specs=[pl.BlockSpec(memory_space=pl.ANY)],
+        in_specs=[VMEM],
         out_specs=(VMEM,) * 8,
-        scratch_shapes=[pltpu.SMEM((3,), jnp.int32), pltpu.SemaphoreType.DMA],
         compiler_params=params(16),
         cost_estimate=cost(0.1),
-    )(jnp.concatenate([fine_offsets, coarse_offset]))
+    )(offsets)
     weights, coarse_weights, left_rows, picks, chosen, forward_rows, inverse, inverse_rows = tables
     low_bands = P_SIZE // STRIDE
+    other = swapped(own_tile)
     got_even = exchanged(packed, "gx", 1)
     got_odd = lax.ppermute(packed[HALF:], "gx", [(i + 1, i) for i in range(1, count - 1, 2)])
     right = jnp.where(lax.axis_index("gx") % 2 == 0, got_even[HALF:], got_odd)
@@ -732,7 +717,7 @@
         ),
         in_specs=[VMEM] * 8,
         out_specs=(VMEM,) * 2,
-        scratch_shapes=[pltpu.VMEM((count, 2 * P_SIZE, LANES), f32)],
+        scratch_shapes=[pltpu.VMEM((count, 2, 2 * P_SIZE, LANES), f32)],
         compiler_params=params(32),
         cost_estimate=cost(0.1),
     )(

time: 21.2 us -> 20.9 us (0.986)
  starting transfers between devices: 8.99 us -> 9.55 us
  Pallas kernels: 9.31 us -> 8.78 us
  waiting for transfers between devices: 0.68 us -> 0.34 us
    ppermute x2, starting transfers between devices: 5.64 us -> 6.41 us  [exchanged(): lax.ppermute(value, axis, [(i, i ^ step) for i in range(lax.axis_size(axi...]
    ppermute x2, waiting for transfers between devices: 0.63 us -> 0.27 us  [exchanged(): lax.ppermute(value, axis, [(i, i ^ step) for i in range(lax.axis_size(axi...]
    pallas_call x1, Pallas kernels: 0.85 us -> 0.52 us  [local(): pl.pallas_call(tables_kernel, out_shape=(jax.ShapeDtypeStruct((2, 4 * LAN...]
  transfers between devices with their start and end apart: 8 -> 8, of which waited for: 1 -> 2; matrix products, arithmetic and copies ran while one was open for 1% -> 1% of each run, Pallas kernels for 26% -> 23%
where the time goes in v4:
time: 20.9 us; the launch traced here: 20.7 us
  starting transfers between devices  9.55 us (46%)
  Pallas kernels  8.78 us (42%)
  local copies, waits for them, and re-layouts  1.07 us (5%)
  between operations  0.84 us (4%)
  waiting for transfers between devices  0.34 us (2%)
    ppermute x2, starting transfers between devices, exchanged(): lax.ppermute(value, axis, [(i, i ^ step) for i in range(lax.axis_size(axi...  6.41 us
    pallas_call x1, Pallas kernels, local(): pl.pallas_call(peak_kernel, out_shape=jax.ShapeDtypeStruct((2, 1, per_row...  2.9 us
    pallas_call x2, Pallas kernels, upper(): pl.pallas_call(functools.partial(upper_kernel, group), out_shape=jax.Shap...  2.83 us
    ppermute x1, starting transfers between devices, from_next(): got.append(lax.ppermute(value, axis, pairs + [(j, i) for i, j in pairs]))  1.56 us
    pallas_call x1, Pallas kernels, local(): pl.pallas_call(turn_kernel, out_shape=(jax.ShapeDtypeStruct((2, supers, 4...  1.34 us
    unnamed x6, local copies, waits for them, and re-layouts  1.05 us
    ppermute x4, starting transfers between devices, swapped(): return lax.ppermute(value, 'gz', [(0, 1), (1, 0)])  0.94 us
    pallas_call x1, Pallas kernels, local(): pl.pallas_call(lower_kernel, out_shape=jax.ShapeDtypeStruct((low_bands, P...  0.89 us
  transfers between devices with their start and end apart: 8, of which 2 were waited for; matrix products, arithmetic and copies ran while one was open for 1% of the time, Pallas kernels for 23%

profile of v4, /device:TPU:0, one launch (start us, length us, event | category | flops | bytes accessed | tf_op | source)
XLA Modules:
  0.0 20.7 jit_solution(7822807312374107856)
XLA Ops:
  0.0 0.0 copy-start
  0.0 1.0 %copy-done = bf16[1,512,512]{2,1,0:T(8,128)(2,1)S(1)} copy-done((bf16[1,512,512]{2,1,0:T(8,128)(2,1)S(1)}, bf16[1,512,512]{2,1,0:T(8,128)(2,1)}, u32[]{:S(2)}) %copy-start) | copy-done | bytes 524312
  1.0 0.3 %shard_map.47 = (bf16[512,512]{1,0:T(8,128)(2,1)S(1)}, bf16[64,512]{1,0:T(8,128)(2,1)S(1)}, bf16[288,128]{1,0:T(8,128)(2,1)S(1)}) custom-call(bf16[512,512]{1,0:T(8,128)(2,1)S(1)} %bitcast.2), custom_call_target="tpu_custom_call" | custom-call | bytes 15000000 | tf_op jit(solution)/shard_map/pallas_call | solution.py:646
  1.4 3.1 %collective-permute-start = (bf16[288,128]{1,0:T(8,128)(2,1)S(1)}, bf16[288,128]{1,0:T(8,128)(2,1)S(1)}, u32[]{:S(2)}, u32[]{:S(2)}) collective-permute-start(bf16[288,128]{1,0:T(8,128)(2,1)S(1)} %get-tuple-element.32), channel_id=1, source_target_pairs={{0,4},{4,0},{8,12},{12,8},{1,5},{5,1},{9,13},{13,9},{2,6},{6,2},{1... | collective-permute-start | bytes 221192 | tf_op jit(solution)/shard_map/ppermute | solution.py:604
  4.5 0.7 %collective-permute-start.4 = (bf16[256,128]{1,0:T(8,128)(2,1)S(1)}, bf16[256,128]{1,0:T(8,128)(2,1)S(1)}, u32[]{:S(2)}, u32[]{:S(2)}) collective-permute-start(bf16[256,128]{1,0:T(8,128)(2,1)S(1)} %slice.18), channel_id=1, source_target_pairs={{8,4},{9,5},{10,6},{11,7},{24,20},{25,21},{26,22},{27,23}} | collective-permute-start | bytes 196616 | tf_op jit(solution)/shard_map/ppermute | solution.py:680
  5.1 0.1 collective-permute-start.2
  5.2 0.0 copy-start.2
  5.9 0.0 copy-done.2
  5.9 0.1 pad_add_fusion.offsets_in
  6.0 0.5 %shard_map.46 = (bf16[2,512,256]{2,1,0:T(8,128)(2,1)S(1)}, bf16[2,512,128]{2,1,0:T(8,128)(2,1)S(1)}, bf16[128,192]{1,0:T(8,128)(2,1)S(1)}, s32[2,2,8,128]{3,2,1,...) custom-call(s32[3]{0:T(128)S(1)} %pad_add_fusion.offsets_in), custom_call_target="tpu_custom_call" | custom-call | bytes 300000 | tf_op jit(solution)/shard_map/pallas_call | solution.py:659
  6.5 0.0 collective-permute-done.4
  6.5 0.3 %collective-permute-done = bf16[288,128]{1,0:T(8,128)(2,1)S(1)} collective-permute-done((bf16[288,128]{1,0:T(8,128)(2,1)S(1)}, bf16[288,128]{1,0:T(8,128)(2,1)S(1)}, u32[]{:S(2)}, u32[]{:S(2)}) %collective-permute-start) | collective-permute-done | bytes 73760 | tf_op jit(solution)/shard_map/ppermute | solution.py:604
  6.8 0.3 %collective-permute-start.5 = (bf16[256,128]{1,0:T(8,128)(2,1)S(1)}, bf16[256,128]{1,0:T(8,128)(2,1)S(1)}, u32[]{:S(2)}, u32[]{:S(2)}) collective-permute-start(bf16[256,128]{1,0:T(8,128)(2,1)S(1)} %slice_select_fusion.refs_0_.own_right_ref), channel_id=1, source_target_pairs={{0,1},{1,0},{2,3},{3,2},{4,5},{5,4},{6,7},{7,6},{8,9},{9,8},{10,11... | collective-permute-start | bytes 196616 | tf_op jit(solution)/shard_map/ppermute | solution.py:619
  7.1 3.3 %collective-permute-start.1 = (bf16[64,128]{1,0:T(8,128)(2,1)S(1)}, bf16[64,128]{1,0:T(8,128)(2,1)S(1)}, u32[]{:S(2)}, u32[]{:S(2)}) collective-permute-start(bf16[64,128]{1,0:T(8,128)(2,1)S(1)} %pad_maximum_fusion.2), channel_id=1, source_target_pairs={{0,8},{4,12},{8,0},{12,4},{1,9},{5,13},{9,1},{13,5},{2,10},{6,14},... | collective-permute-start | bytes 49160 | tf_op jit(solution)/shard_map/ppermute | solution.py:604
  10.4 0.0 collective-permute-done.5.refs_1_.other_right_ref
  10.4 1.6 %collective-permute-start.6 = (bf16[64,640]{1,0:T(8,128)(2,1)S(1)}, bf16[64,640]{1,0:T(8,128)(2,1)S(1)}, u32[]{:S(2)}, u32[]{:S(2)}) collective-permute-start(bf16[64,640]{1,0:T(8,128)(2,1)S(1)} %pad_maximum_fusion), channel_id=1, source_target_pairs={{0,2},{2,0},{1,3},{3,1},{4,6},{6,4},{5,7},{7,5},{8,10},{10,8},{9,1... | collective-permute-start | bytes 245768 | tf_op jit(solution)/shard_map/ppermute | solution.py:612
  12.0 0.0 collective-permute-done.2.other_ref
  12.0 1.4 %shard_map.48.refs_0_ = f32[14,64,256]{2,1,0:T(8,128)S(1)} custom-call(bf16[2,512,256]{2,1,0:T(8,128)(2,1)S(1)} %get-tuple-element.33.weights, bf16[128,192]{1,0:T(8,128)(2,1)S(1)} %get-tuple-element.34.left_rows_ref, bf16[512,512]{1,0:T(8,128)(2,1)S(1)} %get-tuple-element.35.own_ref, bf16[512,512]{1,0:T(8,128)(2,1)S(1)} %collective-permute-done.2.other_ref), custom_call_target="tpu_custom_call" | custom-call | bytes 300000 | tf_op jit(solution)/shard_map/pallas_call | solution.py:693
  13.4 0.0 collective-permute-done.1
  13.4 0.1 collective-permute-start.3
  13.5 1.5 %shard_map.49.refs_1_ = f32[14,64,256]{2,1,0:T(8,128)S(1)} custom-call(bf16[2,512,256]{2,1,0:T(8,128)(2,1)S(1)} %get-tuple-element.33.weights, bf16[128,192]{1,0:T(8,128)(2,1)S(1)} %get-tuple-element.34.left_rows_ref, bf16[512,512]{1,0:T(8,128)(2,1)S(1)} %get-tuple-element.35.own_ref, bf16[512,512]{1,0:T(8,128)(2,1)S(1)} %collective-permute-done.2.other_ref, ...), custom_call_target="tpu_custom_call" | custom-call | bytes 300000 | tf_op jit(solution)/shard_map/pallas_call | solution.py:693
  14.9 0.1 collective-permute-done.6.own_low_ref
  15.0 0.0 collective-permute-done.3.other_part_ref
  15.0 0.5 %collective-permute-start.7 = (bf16[64,640]{1,0:T(8,128)(2,1)S(1)}, bf16[64,640]{1,0:T(8,128)(2,1)S(1)}, u32[]{:S(2)}, u32[]{:S(2)}) collective-permute-start(bf16[64,640]{1,0:T(8,128)(2,1)S(1)} %collective-permute-done.6.own_low_ref), channel_id=1, source_target_pairs={{0,1},{1,0},{2,3},{3,2},{4,5},{5,4},{6,7},{7,6},{8,9},{9,8},{10,11... | collective-permute-start | bytes 245768 | tf_op jit(solution)/shard_map/ppermute | solution.py:619
  15.5 1.3 %shard_map.50 = (f32[2,2,4,32,128]{4,3,2,1,0:T(8,128)S(1)}, f32[2,8,16]{2,1,0:T(8,128)S(1)}) custom-call(bf16[64,256]{1,0:T(8,128)(2,1)S(1)} %get-tuple-element.28.forward_rows_ref, bf16[768,256]{1,0:T(8,128)(2,1)S(1)} %get-tuple-element.26.inverse_ref, bf16[64,256]{1,0:T(8,128)(2,1)S(1)} %get-tuple-element.27.inverse_rows_ref, ...), custom_call_target="tpu_custom_call" | custom-call | bytes 300000 | tf_op jit(solution)/shard_map/pallas_call | solution.py:712
  16.9 0.0 collective-permute-done.7.other_low_ref
  16.9 0.0 copy-start.1
  16.9 0.9 %shard_map.51.lower_ref = f32[2,64,512]{2,1,0:T(8,128)S(1)} custom-call(bf16[2,512,256]{2,1,0:T(8,128)(2,1)S(1)} %get-tuple-element.33.weights, bf16[128,192]{1,0:T(8,128)(2,1)S(1)} %get-tuple-element.34.left_rows_ref, bf16[512,512]{1,0:T(8,128)(2,1)S(1)} %get-tuple-element.35.own_ref, bf16[256,128]{1,0:T(8,128)(2,1)S(1)} %slice_select_fusion.refs_0_.own_right_ref, ...), custom_call_target="tpu_custom_call" | custom-call | bytes 300000 | tf_op jit(solution)/shard_map/pallas_call | solution.py:734
  17.8 0.0 copy-done.1
  17.8 2.9 %shard_map.52 = f32[2,1,8,16]{3,2,1,0:T(8,128)} custom-call(bf16[768,256]{1,0:T(8,128)(2,1)S(1)} %get-tuple-element.26.inverse_ref, bf16[64,256]{1,0:T(8,128)(2,1)S(1)} %get-tuple-element.27.inverse_rows_ref, s32[16,16]{1,0:T(8,128)S(1)} %copy-done.1, f32[2,8,16]{2,1,0:T(8,128)S(1)} %get-tuple-element.42.base_ref, ...), custom_call_target="tpu_custom_call" | custom-call | bytes 300000 | tf_op jit(solution)/shard_map/pallas_call | solution.py:746
  (8 shorter events, 0.0 us)
Async XLA Ops:
  0.0 1.0 %copy-start = (bf16[1,512,512]{2,1,0:T(8,128)(2,1)S(1)}, bf16[1,512,512]{2,1,0:T(8,128)(2,1)}, u32[]{:S(2)}) copy-start(bf16[1,512,512]{2,1,0:T(8,128)(2,1)} %param.4) | copy-start | bytes 1572868
  1.4 5.4 %collective-permute-start = (bf16[288,128]{1,0:T(8,128)(2,1)S(1)}, bf16[288,128]{1,0:T(8,128)(2,1)S(1)}, u32[]{:S(2)}, u32[]{:S(2)}) collective-permute-start(bf16[288,128]{1,0:T(8,128)(2,1)S(1)} %get-tuple-element.32), channel_id=1, source_target_pairs={{0,4},{4,0},{8,12},{12,8},{1,5},{5,1},{9,13},{13,9},{2,6},{6,2},{1... | collective-permute-start | bytes 221192 | tf_op jit(solution)/shard_map/ppermute | solution.py:604
  4.5 2.1 %collective-permute-start.4 = (bf16[256,128]{1,0:T(8,128)(2,1)S(1)}, bf16[256,128]{1,0:T(8,128)(2,1)S(1)}, u32[]{:S(2)}, u32[]{:S(2)}) collective-permute-start(bf16[256,128]{1,0:T(8,128)(2,1)S(1)} %slice.18), channel_id=1, source_target_pairs={{8,4},{9,5},{10,6},{11,7},{24,20},{25,21},{26,22},{27,23}} | collective-permute-start | bytes 196616 | tf_op jit(solution)/shard_map/ppermute | solution.py:680
  5.1 6.9 %collective-permute-start.2 = (bf16[512,512]{1,0:T(8,128)(2,1)S(1)}, bf16[512,512]{1,0:T(8,128)(2,1)S(1)}, u32[]{:S(2)}, u32[]{:S(2)}) collective-permute-start(bf16[512,512]{1,0:T(8,128)(2,1)S(1)} %get-tuple-element.35.own_ref), channel_id=1, source_target_pairs={{0,1},{1,0},{2,3},{3,2},{4,5},{5,4},{6,7},{7,6},{8,9},{9,8},{10,11... | collective-permute-start | bytes 1572872 | tf_op jit(solution)/shard_map/ppermute | solution.py:619
  5.2 0.7 %copy-start.2 = (s32[2]{0:T(128)S(1)}, s32[2]{0:T(128)}, u32[]{:S(2)}) copy-start(s32[2]{0:T(128)} %param.5) | copy-start | bytes 28
  6.8 3.6 %collective-permute-start.5 = (bf16[256,128]{1,0:T(8,128)(2,1)S(1)}, bf16[256,128]{1,0:T(8,128)(2,1)S(1)}, u32[]{:S(2)}, u32[]{:S(2)}) collective-permute-start(bf16[256,128]{1,0:T(8,128)(2,1)S(1)} %slice_select_fusion.refs_0_.own_right_ref), channel_id=1, source_target_pairs={{0,1},{1,0},{2,3},{3,2},{4,5},{5,4},{6,7},{7,6},{8,9},{9,8},{10,11... | collective-permute-start | bytes 196616 | tf_op jit(solution)/shard_map/ppermute | solution.py:619
  7.1 6.3 %collective-permute-start.1 = (bf16[64,128]{1,0:T(8,128)(2,1)S(1)}, bf16[64,128]{1,0:T(8,128)(2,1)S(1)}, u32[]{:S(2)}, u32[]{:S(2)}) collective-permute-start(bf16[64,128]{1,0:T(8,128)(2,1)S(1)} %pad_maximum_fusion.2), channel_id=1, source_target_pairs={{0,8},{4,12},{8,0},{12,4},{1,9},{5,13},{9,1},{13,5},{2,10},{6,14},... | collective-permute-start | bytes 49160 | tf_op jit(solution)/shard_map/ppermute | solution.py:604
  10.4 4.6 %collective-permute-start.6 = (bf16[64,640]{1,0:T(8,128)(2,1)S(1)}, bf16[64,640]{1,0:T(8,128)(2,1)S(1)}, u32[]{:S(2)}, u32[]{:S(2)}) collective-permute-start(bf16[64,640]{1,0:T(8,128)(2,1)S(1)} %pad_maximum_fusion), channel_id=1, source_target_pairs={{0,2},{2,0},{1,3},{3,1},{4,6},{6,4},{5,7},{7,5},{8,10},{10,8},{9,1... | collective-permute-start | bytes 245768 | tf_op jit(solution)/shard_map/ppermute | solution.py:612
  13.4 1.6 %collective-permute-start.3 = (bf16[128,128]{1,0:T(8,128)(2,1)S(1)}, bf16[128,128]{1,0:T(8,128)(2,1)S(1)}, u32[]{:S(2)}, u32[]{:S(2)}) collective-permute-start(bf16[128,128]{1,0:T(8,128)(2,1)S(1)} %pad_maximum_fusion.1.own_part_ref), channel_id=1, source_target_pairs={{0,1},{1,0},{2,3},{3,2},{4,5},{5,4},{6,7},{7,6},{8,9},{9,8},{10,11... | collective-permute-start | bytes 98312 | tf_op jit(solution)/shard_map/ppermute | solution.py:619
  15.0 1.9 %collective-permute-start.7 = (bf16[64,640]{1,0:T(8,128)(2,1)S(1)}, bf16[64,640]{1,0:T(8,128)(2,1)S(1)}, u32[]{:S(2)}, u32[]{:S(2)}) collective-permute-start(bf16[64,640]{1,0:T(8,128)(2,1)S(1)} %collective-permute-done.6.own_low_ref), channel_id=1, source_target_pairs={{0,1},{1,0},{2,3},{3,2},{4,5},{5,4},{6,7},{7,6},{8,9},{9,8},{10,11... | collective-permute-start | bytes 245768 | tf_op jit(solution)/shard_map/ppermute | solution.py:619
  16.9 0.9 %copy-start.1 = (s32[16,16]{1,0:T(8,128)S(1)}, s32[16,16]{1,0:T(8,128)}, u32[]{:S(2)}) copy-start(s32[16,16]{1,0:T(8,128)} %mask_ref.1) | copy-start | bytes 3076

commit v5 on v4

--- a/solution.py
+++ b/solution.py
@@ -316,12 +316,9 @@
     return jnp.where(left, a, b), pltpu.roll(jnp.where(left, b, a), P_SIZE, axis=1)
 
 
-def forward_bands(image, stacked, weights, left_rows, first_band, out_ref):
-    bands = out_ref.shape[0]
-    tall = image.shape[1]
-    wide = out_ref.shape[2]
-    blocks = tall // STRIDE
-    supers = wide // (2 * LANES)
+def forward_columns(image, stacked, weights):
+    blocks = image.shape[1] // STRIDE
+    supers = stacked.shape[3] // (2 * LANES)
     places = [(s, g) for s in range(2) for g in range(supers)]
     strips = [image[s, :, g * 2 * LANES : (2 * g + 3) * LANES] for s, g in places]
     for (s, g), (a, b) in zip(places, column_transform(strips, weights)):
@@ -335,6 +332,11 @@
                     block = slice(n * STRIDE, (n + 1) * STRIDE)
                     stacked[s, t, 2 * n * STRIDE : (2 * n + 1) * STRIDE, at] = high[block]
                     stacked[s, t, (2 * n + 1) * STRIDE : (2 * n + 2) * STRIDE, at] = low[block]
+
+
+def forward_rows(stacked, left_rows, first_band, out_ref):
+    bands, _, wide = out_ref.shape
+    supers = wide // (2 * LANES)
     sign = jnp.where(lax.axis_index("gz") == 0, 1.0, -1.0).astype(f32)
     for i in range(bands):
         spectra = []
@@ -373,42 +375,23 @@
         def _():
             image[:, :, wide:] = jnp.zeros((2, image.shape[1], LANES), bf16)
 
-    forward_bands(image, stacked, weights, left_rows_ref[...], 0, out_ref)
-
-
-def lower_kernel(
-    weights,
-    left_rows_ref,
-    own_ref,
-    own_right_ref,
-    own_low_ref,
-    other_ref,
-    other_right_ref,
-    other_low_ref,
-    out_ref,
-    image,
-    stacked,
-):
+    forward_columns(image, stacked, weights)
+    forward_rows(stacked, left_rows_ref[...], 0, out_ref)
+
+
+def lower_image(own_ref, own_right_ref, own_low_ref, other_ref, other_right_ref, other_low_ref, image):
     rows, width = own_ref.shape
+    inside = 1.0 - is_last("gx").astype(f32)
+    above = 1.0 - is_last("gy").astype(f32)
+    lane = iota((P_SIZE, width + LANES), 1)
+    keep = jnp.where(lane < width, above, above * inside)
     for s, (main, right, low) in enumerate(
         ((own_ref, own_right_ref, own_low_ref), (other_ref, other_right_ref, other_low_ref))
     ):
         image[s, :P_SIZE, :width] = main[rows - P_SIZE :]
-        edge = right[rows // 2 - P_SIZE :].astype(f32)
+        edge = right[rows // 2 - P_SIZE :].astype(f32) * inside
         image[s, :P_SIZE, width:] = pltpu.roll(edge, P_SIZE, axis=1).astype(bf16)
-        image[s, P_SIZE:] = low[...]
-
-    @pl.when(is_last("gx"))
-    def _():
-        image[:, :, width:] = jnp.zeros((2, 2 * P_SIZE, LANES), bf16)
-
-    @pl.when(is_last("gy"))
-    def _():
-        image[:, P_SIZE:, :] = jnp.zeros((2, P_SIZE, width + LANES), bf16)
-
-    forward_bands(
-        image, stacked, weights, left_rows_ref[...], rows // STRIDE - out_ref.shape[0], out_ref
-    )
+        image[s, P_SIZE:] = (low[...].astype(f32) * keep).astype(bf16)
 
 
 def inverse_columns(high, low, table_ref):
@@ -542,15 +525,18 @@
     mask_ref,
     base_ref,
     turns,
-    lower_ref,
+    weights,
+    left_rows_ref,
     *refs,
 ):
-    spectra, (out_ref, high_ref, low_ref) = refs[:-3], refs[-3:]
+    halves, spectra = refs[:6], refs[6:-6]
+    out_ref, image, stacked, lower_ref, high_ref, low_ref = refs[-6:]
     supers = turns.shape[1]
     per_row = supers * GROUP
     upper_bands = spectra[0].shape[0]
     bands = upper_bands + lower_ref.shape[0]
-    for i in range(bands):
+
+    def turn_band(i):
         for g in range(supers):
             lane = g * 2 * LANES
             if i < upper_bands:
@@ -572,6 +558,14 @@
                 lanes = slice(lane + n % 2 * LANES, lane + (n % 2 + 1) * LANES)
                 high_ref[at, lanes] = high
                 low_ref[at, lanes] = low
+
+    lower_image(*halves, image)
+    forward_columns(image, stacked, weights)
+    for i in range(upper_bands // 2):
+        turn_band(i)
+    forward_rows(stacked, left_rows_ref[...], upper_bands, lower_ref)
+    for i in range(upper_bands // 2, bands):
+        turn_band(i)
     for g in range(supers):
         at = slice(g * 2 * LANES, (g + 1) * 2 * LANES)
         high, low = split(inverse_columns(high_ref[:, at], low_ref[:, at], inverse_ref))
@@ -731,27 +725,36 @@
         other_tiles,
     )
     other_low = swapped(own_low)
-    lower = pl.pallas_call(
-        lower_kernel,
-        out_shape=jax.ShapeDtypeStruct((low_bands, P_SIZE, wide), f32),
-        in_specs=[VMEM] * 8,
+    flow = pl.pallas_call(
+        peak_kernel,
+        out_shape=jax.ShapeDtypeStruct((2, 1, per_row, bands), f32),
+        in_specs=[VMEM] * (13 + supers),
         out_specs=VMEM,
         scratch_shapes=[
             pltpu.VMEM((2, 2 * P_SIZE, width + LANES), bf16),
             pltpu.VMEM((2, 2, 4 * P_SIZE, wide), bf16),
+            pltpu.VMEM((low_bands, P_SIZE, wide), f32),
+            pltpu.VMEM((bands * P_SIZE, wide), bf16),
+            pltpu.VMEM((bands * P_SIZE, wide), bf16),
         ],
-        compiler_params=params(32),
-        cost_estimate=cost(0.1),
-    )(weights, left_rows, own_tile, right, own_low, other, other_right, other_low)
-    flow = pl.pallas_call(
-        peak_kernel,
-        out_shape=jax.ShapeDtypeStruct((2, 1, per_row, bands), f32),
-        in_specs=[VMEM] * (6 + supers),
-        out_specs=VMEM,
-        scratch_shapes=[pltpu.VMEM((bands * P_SIZE, wide), bf16)] * 2,
         compiler_params=params(40),
         cost_estimate=cost(0.1),
-    )(inverse, inverse_rows, tissue_mask, base, turns, lower, *uppers)
+    )(
+        inverse,
+        inverse_rows,
+        tissue_mask,
+        base,
+        turns,
+        weights,
+        left_rows,
+        own_tile,
+        right,
+        own_low,
+        other,
+        other_right,
+        other_low,
+        *uppers,
+    )
     return jnp.swapaxes(flow, 2, 3)
 
 

time: 20.9 us -> 20.6 us (0.986)
  Pallas kernels: 8.78 us -> 8.54 us
    pallas_call x1 -> x0, Pallas kernels: 0.89 us -> none  [local(): pl.pallas_call(lower_kernel, out_shape=jax.ShapeDtypeStruct((low_bands, P...]
    pallas_call x1, Pallas kernels: 2.9 us -> 3.57 us  [local(): pl.pallas_call(peak_kernel, out_shape=jax.ShapeDtypeStruct((2, 1, per_row...]
where the time goes in v5:
time: 20.6 us; the launch traced here: 20.4 us
  starting transfers between devices  9.53 us (46%)
  Pallas kernels  8.54 us (41%)
  local copies, waits for them, and re-layouts  1.06 us (5%)
  between operations  0.83 us (4%)
  waiting for transfers between devices  0.36 us (2%)
    ppermute x2, starting transfers between devices, exchanged(): lax.ppermute(value, axis, [(i, i ^ step) for i in range(lax.axis_size(axi...  6.41 us
    pallas_call x1, Pallas kernels, local(): pl.pallas_call(peak_kernel, out_shape=jax.ShapeDtypeStruct((2, 1, per_row...  3.57 us
    pallas_call x2, Pallas kernels, upper(): pl.pallas_call(functools.partial(upper_kernel, group), out_shape=jax.Shap...  2.81 us
    ppermute x1, starting transfers between devices, from_next(): got.append(lax.ppermute(value, axis, pairs + [(j, i) for i, j in pairs]))  1.56 us
    pallas_call x1, Pallas kernels, local(): pl.pallas_call(turn_kernel, out_shape=(jax.ShapeDtypeStruct((2, supers, 4...  1.34 us
    unnamed x6, local copies, waits for them, and re-layouts  1.05 us
    ppermute x4, starting transfers between devices, swapped(): return lax.ppermute(value, 'gz', [(0, 1), (1, 0)])  0.92 us
    ppermute x1, starting transfers between devices, local(): lax.ppermute(packed[HALF:], 'gx', [(i + 1, i) for i in range(1, count - 1...  0.65 us
  transfers between devices with their start and end apart: 8, of which 2 were waited for; matrix products, arithmetic and copies ran while one was open for 1% of the time, Pallas kernels for 23%

profile of v5, /device:TPU:0, one launch (start us, length us, event | category | flops | bytes accessed | tf_op | source)
XLA Modules:
  0.0 20.4 jit_solution(9575321104312561884)
XLA Ops:
  0.0 0.0 copy-start
  0.0 1.0 %copy-done = bf16[1,512,512]{2,1,0:T(8,128)(2,1)S(1)} copy-done((bf16[1,512,512]{2,1,0:T(8,128)(2,1)S(1)}, bf16[1,512,512]{2,1,0:T(8,128)(2,1)}, u32[]{:S(2)}) %copy-start) | copy-done | bytes 524312
  1.0 0.3 %shard_map.47 = (bf16[512,512]{1,0:T(8,128)(2,1)S(1)}, bf16[64,512]{1,0:T(8,128)(2,1)S(1)}, bf16[288,128]{1,0:T(8,128)(2,1)S(1)}) custom-call(bf16[512,512]{1,0:T(8,128)(2,1)S(1)} %bitcast.2), custom_call_target="tpu_custom_call" | custom-call | bytes 15000000 | tf_op jit(solution)/shard_map/pallas_call | solution.py:640
  1.4 3.1 %collective-permute-start = (bf16[288,128]{1,0:T(8,128)(2,1)S(1)}, bf16[288,128]{1,0:T(8,128)(2,1)S(1)}, u32[]{:S(2)}, u32[]{:S(2)}) collective-permute-start(bf16[288,128]{1,0:T(8,128)(2,1)S(1)} %get-tuple-element.32), channel_id=1, source_target_pairs={{0,4},{4,0},{8,12},{12,8},{1,5},{5,1},{9,13},{13,9},{2,6},{6,2},{1... | collective-permute-start | bytes 221192 | tf_op jit(solution)/shard_map/ppermute | solution.py:598
  4.5 0.7 %collective-permute-start.4 = (bf16[256,128]{1,0:T(8,128)(2,1)S(1)}, bf16[256,128]{1,0:T(8,128)(2,1)S(1)}, u32[]{:S(2)}, u32[]{:S(2)}) collective-permute-start(bf16[256,128]{1,0:T(8,128)(2,1)S(1)} %slice.18), channel_id=1, source_target_pairs={{8,4},{9,5},{10,6},{11,7},{24,20},{25,21},{26,22},{27,23}} | collective-permute-start | bytes 196616 | tf_op jit(solution)/shard_map/ppermute | solution.py:674
  5.1 0.1 collective-permute-start.2
  5.2 0.0 copy-start.2
  5.9 0.0 copy-done.2
  5.9 0.1 pad_add_fusion.offsets_in
  6.0 0.5 %shard_map.46 = (bf16[2,512,256]{2,1,0:T(8,128)(2,1)S(1)}, bf16[2,512,128]{2,1,0:T(8,128)(2,1)S(1)}, bf16[128,192]{1,0:T(8,128)(2,1)S(1)}, s32[2,2,8,128]{3,2,1,...) custom-call(s32[3]{0:T(128)S(1)} %pad_add_fusion.offsets_in), custom_call_target="tpu_custom_call" | custom-call | bytes 300000 | tf_op jit(solution)/shard_map/pallas_call | solution.py:653
  6.5 0.0 collective-permute-done.4
  6.5 0.3 %collective-permute-done = bf16[288,128]{1,0:T(8,128)(2,1)S(1)} collective-permute-done((bf16[288,128]{1,0:T(8,128)(2,1)S(1)}, bf16[288,128]{1,0:T(8,128)(2,1)S(1)}, u32[]{:S(2)}, u32[]{:S(2)}) %collective-permute-start) | collective-permute-done | bytes 73760 | tf_op jit(solution)/shard_map/ppermute | solution.py:598
  6.8 0.3 %collective-permute-start.5 = (bf16[256,128]{1,0:T(8,128)(2,1)S(1)}, bf16[256,128]{1,0:T(8,128)(2,1)S(1)}, u32[]{:S(2)}, u32[]{:S(2)}) collective-permute-start(bf16[256,128]{1,0:T(8,128)(2,1)S(1)} %slice_select_fusion.refs_0_.refs_1_), channel_id=1, source_target_pairs={{0,1},{1,0},{2,3},{3,2},{4,5},{5,4},{6,7},{7,6},{8,9},{9,8},{10,11... | collective-permute-start | bytes 196616 | tf_op jit(solution)/shard_map/ppermute | solution.py:613
  7.1 3.3 %collective-permute-start.1 = (bf16[64,128]{1,0:T(8,128)(2,1)S(1)}, bf16[64,128]{1,0:T(8,128)(2,1)S(1)}, u32[]{:S(2)}, u32[]{:S(2)}) collective-permute-start(bf16[64,128]{1,0:T(8,128)(2,1)S(1)} %pad_maximum_fusion.2), channel_id=1, source_target_pairs={{0,8},{4,12},{8,0},{12,4},{1,9},{5,13},{9,1},{13,5},{2,10},{6,14},... | collective-permute-start | bytes 49160 | tf_op jit(solution)/shard_map/ppermute | solution.py:598
  10.4 0.0 collective-permute-done.5.refs_1_.refs_4_
  10.4 1.6 %collective-permute-start.6 = (bf16[64,640]{1,0:T(8,128)(2,1)S(1)}, bf16[64,640]{1,0:T(8,128)(2,1)S(1)}, u32[]{:S(2)}, u32[]{:S(2)}) collective-permute-start(bf16[64,640]{1,0:T(8,128)(2,1)S(1)} %pad_maximum_fusion), channel_id=1, source_target_pairs={{0,2},{2,0},{1,3},{3,1},{4,6},{6,4},{5,7},{7,5},{8,10},{10,8},{9,1... | collective-permute-start | bytes 245768 | tf_op jit(solution)/shard_map/ppermute | solution.py:606
  12.0 0.0 collective-permute-done.2.other_ref.refs_3_
  12.0 1.4 %shard_map.48.refs_6_ = f32[14,64,256]{2,1,0:T(8,128)S(1)} custom-call(bf16[2,512,256]{2,1,0:T(8,128)(2,1)S(1)} %get-tuple-element.33.weights, bf16[128,192]{1,0:T(8,128)(2,1)S(1)} %get-tuple-element.34.left_rows_ref, bf16[512,512]{1,0:T(8,128)(2,1)S(1)} %get-tuple-element.35.own_ref.refs_0_, bf16[512,512]{1,0:T(8,128)(2,1)S(1)} %collective-permute-done.2.other_ref.refs_3_), custom_call_target="tpu_custom_call" | custom-call | bytes 300000 | tf_op jit(solution)/shard_map/pallas_call | solution.py:687
  13.4 0.0 collective-permute-done.1
  13.4 0.1 collective-permute-start.3
  13.5 1.5 %shard_map.49.refs_7_ = f32[14,64,256]{2,1,0:T(8,128)S(1)} custom-call(bf16[2,512,256]{2,1,0:T(8,128)(2,1)S(1)} %get-tuple-element.33.weights, bf16[128,192]{1,0:T(8,128)(2,1)S(1)} %get-tuple-element.34.left_rows_ref, bf16[512,512]{1,0:T(8,128)(2,1)S(1)} %get-tuple-element.35.own_ref.refs_0_, bf16[512,512]{1,0:T(8,128)(2,1)S(1)} %collective-permute-done.2.other_ref.refs_3_, ...), custom_call_target="tpu_custom_call" | custom-call | bytes 300000 | tf_op jit(solution)/shard_map/pallas_call | solution.py:687
  14.9 0.1 collective-permute-done.6.refs_2_
  15.0 0.0 collective-permute-done.3.other_part_ref
  15.0 0.5 %collective-permute-start.7 = (bf16[64,640]{1,0:T(8,128)(2,1)S(1)}, bf16[64,640]{1,0:T(8,128)(2,1)S(1)}, u32[]{:S(2)}, u32[]{:S(2)}) collective-permute-start(bf16[64,640]{1,0:T(8,128)(2,1)S(1)} %collective-permute-done.6.refs_2_), channel_id=1, source_target_pairs={{0,1},{1,0},{2,3},{3,2},{4,5},{5,4},{6,7},{7,6},{8,9},{9,8},{10,11... | collective-permute-start | bytes 245768 | tf_op jit(solution)/shard_map/ppermute | solution.py:613
  15.5 0.0 copy-start.1
  15.5 1.3 %shard_map.50 = (f32[2,2,4,32,128]{4,3,2,1,0:T(8,128)S(1)}, f32[2,8,16]{2,1,0:T(8,128)S(1)}) custom-call(bf16[64,256]{1,0:T(8,128)(2,1)S(1)} %get-tuple-element.28.forward_rows_ref, bf16[768,256]{1,0:T(8,128)(2,1)S(1)} %get-tuple-element.26.inverse_ref, bf16[64,256]{1,0:T(8,128)(2,1)S(1)} %get-tuple-element.27.inverse_rows_ref, ...), custom_call_target="tpu_custom_call" | custom-call | bytes 300000 | tf_op jit(solution)/shard_map/pallas_call | solution.py:706
  16.8 0.0 collective-permute-done.7.refs_5_
  16.8 0.0 copy-done.1
  16.9 3.6 %shard_map.51 = f32[2,1,8,16]{3,2,1,0:T(8,128)} custom-call(bf16[768,256]{1,0:T(8,128)(2,1)S(1)} %get-tuple-element.26.inverse_ref, bf16[64,256]{1,0:T(8,128)(2,1)S(1)} %get-tuple-element.27.inverse_rows_ref, s32[16,16]{1,0:T(8,128)S(1)} %copy-done.1, f32[2,8,16]{2,1,0:T(8,128)S(1)} %get-tuple-element.42.base_ref, ...), custom_call_target="tpu_custom_call" | custom-call | bytes 300000 | tf_op jit(solution)/shard_map/pallas_call | solution.py:728
  (8 shorter events, 0.0 us)
Async XLA Ops:
  0.0 1.0 %copy-start = (bf16[1,512,512]{2,1,0:T(8,128)(2,1)S(1)}, bf16[1,512,512]{2,1,0:T(8,128)(2,1)}, u32[]{:S(2)}) copy-start(bf16[1,512,512]{2,1,0:T(8,128)(2,1)} %param.4) | copy-start | bytes 1572868
  1.4 5.4 %collective-permute-start = (bf16[288,128]{1,0:T(8,128)(2,1)S(1)}, bf16[288,128]{1,0:T(8,128)(2,1)S(1)}, u32[]{:S(2)}, u32[]{:S(2)}) collective-permute-start(bf16[288,128]{1,0:T(8,128)(2,1)S(1)} %get-tuple-element.32), channel_id=1, source_target_pairs={{0,4},{4,0},{8,12},{12,8},{1,5},{5,1},{9,13},{13,9},{2,6},{6,2},{1... | collective-permute-start | bytes 221192 | tf_op jit(solution)/shard_map/ppermute | solution.py:598
  4.5 2.1 %collective-permute-start.4 = (bf16[256,128]{1,0:T(8,128)(2,1)S(1)}, bf16[256,128]{1,0:T(8,128)(2,1)S(1)}, u32[]{:S(2)}, u32[]{:S(2)}) collective-permute-start(bf16[256,128]{1,0:T(8,128)(2,1)S(1)} %slice.18), channel_id=1, source_target_pairs={{8,4},{9,5},{10,6},{11,7},{24,20},{25,21},{26,22},{27,23}} | collective-permute-start | bytes 196616 | tf_op jit(solution)/shard_map/ppermute | solution.py:674
  5.1 6.9 %collective-permute-start.2 = (bf16[512,512]{1,0:T(8,128)(2,1)S(1)}, bf16[512,512]{1,0:T(8,128)(2,1)S(1)}, u32[]{:S(2)}, u32[]{:S(2)}) collective-permute-start(bf16[512,512]{1,0:T(8,128)(2,1)S(1)} %get-tuple-element.35.own_ref.refs_0_), channel_id=1, source_target_pairs={{0,1},{1,0},{2,3},{3,2},{4,5},{5,4},{6,7},{7,6},{8,9},{9,8},{10,11... | collective-permute-start | bytes 1572872 | tf_op jit(solution)/shard_map/ppermute | solution.py:613
  5.2 0.7 %copy-start.2 = (s32[2]{0:T(128)S(1)}, s32[2]{0:T(128)}, u32[]{:S(2)}) copy-start(s32[2]{0:T(128)} %param.5) | copy-start | bytes 28
  6.8 3.6 %collective-permute-start.5 = (bf16[256,128]{1,0:T(8,128)(2,1)S(1)}, bf16[256,128]{1,0:T(8,128)(2,1)S(1)}, u32[]{:S(2)}, u32[]{:S(2)}) collective-permute-start(bf16[256,128]{1,0:T(8,128)(2,1)S(1)} %slice_select_fusion.refs_0_.refs_1_), channel_id=1, source_target_pairs={{0,1},{1,0},{2,3},{3,2},{4,5},{5,4},{6,7},{7,6},{8,9},{9,8},{10,11... | collective-permute-start | bytes 196616 | tf_op jit(solution)/shard_map/ppermute | solution.py:613
  7.1 6.3 %collective-permute-start.1 = (bf16[64,128]{1,0:T(8,128)(2,1)S(1)}, bf16[64,128]{1,0:T(8,128)(2,1)S(1)}, u32[]{:S(2)}, u32[]{:S(2)}) collective-permute-start(bf16[64,128]{1,0:T(8,128)(2,1)S(1)} %pad_maximum_fusion.2), channel_id=1, source_target_pairs={{0,8},{4,12},{8,0},{12,4},{1,9},{5,13},{9,1},{13,5},{2,10},{6,14},... | collective-permute-start | bytes 49160 | tf_op jit(solution)/shard_map/ppermute | solution.py:598
  10.4 4.6 %collective-permute-start.6 = (bf16[64,640]{1,0:T(8,128)(2,1)S(1)}, bf16[64,640]{1,0:T(8,128)(2,1)S(1)}, u32[]{:S(2)}, u32[]{:S(2)}) collective-permute-start(bf16[64,640]{1,0:T(8,128)(2,1)S(1)} %pad_maximum_fusion), channel_id=1, source_target_pairs={{0,2},{2,0},{1,3},{3,1},{4,6},{6,4},{5,7},{7,5},{8,10},{10,8},{9,1... | collective-permute-start | bytes 245768 | tf_op jit(solution)/shard_map/ppermute | solution.py:606
  13.4 1.6 %collective-permute-start.3 = (bf16[128,128]{1,0:T(8,128)(2,1)S(1)}, bf16[128,128]{1,0:T(8,128)(2,1)S(1)}, u32[]{:S(2)}, u32[]{:S(2)}) collective-permute-start(bf16[128,128]{1,0:T(8,128)(2,1)S(1)} %pad_maximum_fusion.1.own_part_ref), channel_id=1, source_target_pairs={{0,1},{1,0},{2,3},{3,2},{4,5},{5,4},{6,7},{7,6},{8,9},{9,8},{10,11... | collective-permute-start | bytes 98312 | tf_op jit(solution)/shard_map/ppermute | solution.py:613
  15.0 1.8 %collective-permute-start.7 = (bf16[64,640]{1,0:T(8,128)(2,1)S(1)}, bf16[64,640]{1,0:T(8,128)(2,1)S(1)}, u32[]{:S(2)}, u32[]{:S(2)}) collective-permute-start(bf16[64,640]{1,0:T(8,128)(2,1)S(1)} %collective-permute-done.6.refs_2_), channel_id=1, source_target_pairs={{0,1},{1,0},{2,3},{3,2},{4,5},{5,4},{6,7},{7,6},{8,9},{9,8},{10,11... | collective-permute-start | bytes 245768 | tf_op jit(solution)/shard_map/ppermute | solution.py:613
  15.5 1.4 %copy-start.1 = (s32[16,16]{1,0:T(8,128)S(1)}, s32[16,16]{1,0:T(8,128)}, u32[]{:S(2)}) copy-start(s32[16,16]{1,0:T(8,128)} %mask_ref.1) | copy-start | bytes 3076

commit v6 on v5

--- a/solution.py
+++ b/solution.py
@@ -184,6 +184,11 @@
         bottom[:, lane : lane + LANES],
         bottom[:, lane + LANES : lane + 2 * LANES],
     )
+
+
+def from_right(refs, rows):
+    even = lax.axis_index("gx") % 2 == 0
+    return jnp.where(even, refs[0][rows].astype(f32), refs[1][rows].astype(f32))
 
 
 def unpack(packed):
@@ -368,7 +373,7 @@
     for s, main in enumerate((own_ref, other_ref)):
         image[s, :, :wide] = main[:, lane : lane + wide]
         if rights:
-            image[s, :, wide:] = unpack(rights[s][...])
+            image[s, :, wide:] = unpack(from_right(rights[2 * s : 2 * s + 2], slice(None)))
     if rights:
 
         @pl.when(is_last("gx"))
@@ -379,17 +384,17 @@
     forward_rows(stacked, left_rows_ref[...], 0, out_ref)
 
 
-def lower_image(own_ref, own_right_ref, own_low_ref, other_ref, other_right_ref, other_low_ref, image):
+def lower_image(own_ref, own_rights, own_low_ref, other_ref, other_rights, other_low_ref, image):
     rows, width = own_ref.shape
     inside = 1.0 - is_last("gx").astype(f32)
     above = 1.0 - is_last("gy").astype(f32)
     lane = iota((P_SIZE, width + LANES), 1)
     keep = jnp.where(lane < width, above, above * inside)
     for s, (main, right, low) in enumerate(
-        ((own_ref, own_right_ref, own_low_ref), (other_ref, other_right_ref, other_low_ref))
+        ((own_ref, own_rights, own_low_ref), (other_ref, other_rights, other_low_ref))
     ):
         image[s, :P_SIZE, :width] = main[rows - P_SIZE :]
-        edge = right[rows // 2 - P_SIZE :].astype(f32) * inside
+        edge = from_right(right, slice(rows // 2 - P_SIZE, None)) * inside
         image[s, :P_SIZE, width:] = pltpu.roll(edge, P_SIZE, axis=1).astype(bf16)
         image[s, P_SIZE:] = (low[...].astype(f32) * keep).astype(bf16)
 
@@ -529,7 +534,9 @@
     left_rows_ref,
     *refs,
 ):
-    halves, spectra = refs[:6], refs[6:-6]
+    own_ref, *own_rights, own_low_ref, other_ref = refs[:5]
+    *other_rights, other_low_ref = refs[5:8]
+    spectra = refs[8:-6]
     out_ref, image, stacked, lower_ref, high_ref, low_ref = refs[-6:]
     supers = turns.shape[1]
     per_row = supers * GROUP
@@ -559,7 +566,7 @@
                 high_ref[at, lanes] = high
                 low_ref[at, lanes] = low
 
-    lower_image(*halves, image)
+    lower_image(own_ref, own_rights, own_low_ref, other_ref, other_rights, other_low_ref, image)
     forward_columns(image, stacked, weights)
     for i in range(upper_bands // 2):
         turn_band(i)
@@ -672,11 +679,13 @@
     other = swapped(own_tile)
     got_even = exchanged(packed, "gx", 1)
     got_odd = lax.ppermute(packed[HALF:], "gx", [(i + 1, i) for i in range(1, count - 1, 2)])
-    right = jnp.where(lax.axis_index("gx") % 2 == 0, got_even[HALF:], got_odd)
-    other_right = swapped(right)
-    low_payload = jnp.concatenate([own_edge, right[:P_SIZE]], axis=1)
-    low_payload, other_right = lax.optimization_barrier((low_payload, other_right))
-    own_low = from_next(low_payload, "gy")
+    got_right = got_even[HALF:]
+    other_right = swapped(got_right)
+    got_odd, other_right = lax.optimization_barrier((got_odd, other_right))
+    even = lax.axis_index("gx") % 2 == 0
+    corner = jnp.where(even, got_right[:P_SIZE], got_odd[:P_SIZE])
+    own_low = from_next(jnp.concatenate([own_edge, corner], axis=1), "gy")
+    other_odd = swapped(got_odd)
     tiles = jnp.concatenate([packed[:HALF], got_even[:HALF]], axis=0)
     step = 2
     while 2 * step < count:
@@ -701,7 +710,7 @@
     last_tiles, *uppers = lax.optimization_barrier((last_tiles, *uppers))
     tiles = jnp.concatenate([tiles, last_tiles], axis=0)
     other_tiles = swapped(tiles)
-    uppers.append(upper(supers - 1, right, other_right))
+    uppers.append(upper(supers - 1, got_right, got_odd, other_right, other_odd))
     other_tiles, own_low, *uppers = lax.optimization_barrier((other_tiles, own_low, *uppers))
     turns, base = pl.pallas_call(
         turn_kernel,
@@ -728,7 +737,7 @@
     flow = pl.pallas_call(
         peak_kernel,
         out_shape=jax.ShapeDtypeStruct((2, 1, per_row, bands), f32),
-        in_specs=[VMEM] * (13 + supers),
+        in_specs=[VMEM] * (15 + supers),
         out_specs=VMEM,
         scratch_shapes=[
             pltpu.VMEM((2, 2 * P_SIZE, width + LANES), bf16),
@@ -748,10 +757,12 @@
         weights,
         left_rows,
         own_tile,
-        right,
+        got_right,
+        got_odd,
         own_low,
         other,
         other_right,
+        other_odd,
         other_low,
         *uppers,
     )

time: 20.6 us -> 20.5 us (level)
  starting transfers between devices: 9.53 us -> 9.32 us
    ppermute x4 -> x5, starting transfers between devices: 0.92 us -> 0.8 us  [swapped(): return lax.ppermute(value, 'gz', [(0, 1), (1, 0)])]
  transfers between devices with their start and end apart: 8 -> 9, of which waited for: 2 -> 2; matrix products, arithmetic and copies ran while one was open for 1% -> 1% of each run, Pallas kernels for 23% -> 23%
where the time goes in v6:
time: 20.5 us; the launch traced here: 20.4 us
  starting transfers between devices  9.32 us (45%)
  Pallas kernels  8.58 us (42%)
  local copies, waits for them, and re-layouts  1.07 us (5%)
  between operations  0.81 us (4%)
  waiting for transfers between devices  0.5 us (2%)
    ppermute x2, starting transfers between devices, exchanged(): lax.ppermute(value, axis, [(i, i ^ step) for i in range(lax.axis_size(axi...  6.31 us
    pallas_call x1, Pallas kernels, local(): pl.pallas_call(peak_kernel, out_shape=jax.ShapeDtypeStruct((2, 1, per_row...  3.59 us
    pallas_call x2, Pallas kernels, upper(): pl.pallas_call(functools.partial(upper_kernel, group), out_shape=jax.Shap...  2.83 us
    ppermute x1, starting transfers between devices, from_next(): got.append(lax.ppermute(value, axis, pairs + [(j, i) for i, j in pairs]))  1.56 us
    pallas_call x1, Pallas kernels, local(): pl.pallas_call(turn_kernel, out_shape=(jax.ShapeDtypeStruct((2, supers, 4...  1.34 us
    unnamed x6, local copies, waits for them, and re-layouts  1.05 us
    ppermute x5, starting transfers between devices, swapped(): return lax.ppermute(value, 'gz', [(0, 1), (1, 0)])  0.8 us
    ppermute x1, starting transfers between devices, local(): lax.ppermute(packed[HALF:], 'gx', [(i + 1, i) for i in range(1, count - 1...  0.65 us
  transfers between devices with their start and end apart: 9, of which 2 were waited for; matrix products, arithmetic and copies ran while one was open for 1% of the time, Pallas kernels for 23%

profile of v6, /device:TPU:0, one launch (start us, length us, event | category | flops | bytes accessed | tf_op | source)
XLA Modules:
  0.0 20.4 jit_solution(12259183015304890827)
XLA Ops:
  0.0 0.0 copy-start
  0.0 1.0 %copy-done = bf16[1,512,512]{2,1,0:T(8,128)(2,1)S(1)} copy-done((bf16[1,512,512]{2,1,0:T(8,128)(2,1)S(1)}, bf16[1,512,512]{2,1,0:T(8,128)(2,1)}, u32[]{:S(2)}) %copy-start) | copy-done | bytes 524312
  1.0 0.3 %shard_map.47 = (bf16[512,512]{1,0:T(8,128)(2,1)S(1)}, bf16[64,512]{1,0:T(8,128)(2,1)S(1)}, bf16[288,128]{1,0:T(8,128)(2,1)S(1)}) custom-call(bf16[512,512]{1,0:T(8,128)(2,1)S(1)} %bitcast.2), custom_call_target="tpu_custom_call" | custom-call | bytes 15000000 | tf_op jit(solution)/shard_map/pallas_call | solution.py:647
  1.4 3.1 %collective-permute-start = (bf16[288,128]{1,0:T(8,128)(2,1)S(1)}, bf16[288,128]{1,0:T(8,128)(2,1)S(1)}, u32[]{:S(2)}, u32[]{:S(2)}) collective-permute-start(bf16[288,128]{1,0:T(8,128)(2,1)S(1)} %get-tuple-element.32), channel_id=1, source_target_pairs={{0,4},{4,0},{8,12},{12,8},{1,5},{5,1},{9,13},{13,9},{2,6},{6,2},{1... | collective-permute-start | bytes 221192 | tf_op jit(solution)/shard_map/ppermute | solution.py:605
  4.5 0.7 %collective-permute-start.4 = (bf16[256,128]{1,0:T(8,128)(2,1)S(1)}, bf16[256,128]{1,0:T(8,128)(2,1)S(1)}, u32[]{:S(2)}, u32[]{:S(2)}) collective-permute-start(bf16[256,128]{1,0:T(8,128)(2,1)S(1)} %slice.22), channel_id=1, source_target_pairs={{8,4},{9,5},{10,6},{11,7},{24,20},{25,21},{26,22},{27,23}} | collective-permute-start | bytes 196616 | tf_op jit(solution)/shard_map/ppermute | solution.py:681
  5.1 0.1 collective-permute-start.2
  5.2 0.0 copy-start.2
  5.9 0.0 copy-done.2
  5.9 0.1 pad_add_fusion.offsets_in
  6.0 0.5 %shard_map.46 = (bf16[2,512,256]{2,1,0:T(8,128)(2,1)S(1)}, bf16[2,512,128]{2,1,0:T(8,128)(2,1)S(1)}, bf16[128,192]{1,0:T(8,128)(2,1)S(1)}, s32[2,2,8,128]{3,2,1,...) custom-call(s32[3]{0:T(128)S(1)} %pad_add_fusion.offsets_in), custom_call_target="tpu_custom_call" | custom-call | bytes 300000 | tf_op jit(solution)/shard_map/pallas_call | solution.py:660
  6.5 0.3 %collective-permute-done = bf16[288,128]{1,0:T(8,128)(2,1)S(1)} collective-permute-done((bf16[288,128]{1,0:T(8,128)(2,1)S(1)}, bf16[288,128]{1,0:T(8,128)(2,1)S(1)}, u32[]{:S(2)}, u32[]{:S(2)}) %collective-permute-start) | collective-permute-done | bytes 73760 | tf_op jit(solution)/shard_map/ppermute | solution.py:605
  6.8 0.3 %collective-permute-start.5 = (bf16[256,128]{1,0:T(8,128)(2,1)S(1)}, bf16[256,128]{1,0:T(8,128)(2,1)S(1)}, u32[]{:S(2)}, u32[]{:S(2)}) collective-permute-start(bf16[256,128]{1,0:T(8,128)(2,1)S(1)} %slice.27.refs_0_.refs_1_), channel_id=1, source_target_pairs={{0,1},{1,0},{2,3},{3,2},{4,5},{5,4},{6,7},{7,6},{8,9},{9,8},{10,11... | collective-permute-start | bytes 196616 | tf_op jit(solution)/shard_map/ppermute | solution.py:620
  7.1 3.2 %collective-permute-start.1 = (bf16[64,128]{1,0:T(8,128)(2,1)S(1)}, bf16[64,128]{1,0:T(8,128)(2,1)S(1)}, u32[]{:S(2)}, u32[]{:S(2)}) collective-permute-start(bf16[64,128]{1,0:T(8,128)(2,1)S(1)} %pad_maximum_fusion.2), channel_id=1, source_target_pairs={{0,8},{4,12},{8,0},{12,4},{1,9},{5,13},{9,1},{13,5},{2,10},{6,14},... | collective-permute-start | bytes 49160 | tf_op jit(solution)/shard_map/ppermute | solution.py:605
  10.3 0.0 collective-permute-done.4.refs_1_.refs_2_
  10.3 0.0 collective-permute-done.5.refs_2_.refs_5_
  10.3 0.0 collective-permute-start.7
  10.3 1.6 %collective-permute-start.6 = (bf16[64,640]{1,0:T(8,128)(2,1)S(1)}, bf16[64,640]{1,0:T(8,128)(2,1)S(1)}, u32[]{:S(2)}, u32[]{:S(2)}) collective-permute-start(bf16[64,640]{1,0:T(8,128)(2,1)S(1)} %pad_maximum_fusion), channel_id=1, source_target_pairs={{0,2},{2,0},{1,3},{3,1},{4,6},{6,4},{5,7},{7,5},{8,10},{10,8},{9,1... | collective-permute-start | bytes 245768 | tf_op jit(solution)/shard_map/ppermute | solution.py:613
  11.9 0.0 collective-permute-done.2.other_ref.refs_4_
  11.9 1.4 %shard_map.48.refs_8_ = f32[14,64,256]{2,1,0:T(8,128)S(1)} custom-call(bf16[2,512,256]{2,1,0:T(8,128)(2,1)S(1)} %get-tuple-element.33.weights, bf16[128,192]{1,0:T(8,128)(2,1)S(1)} %get-tuple-element.34.left_rows_ref, bf16[512,512]{1,0:T(8,128)(2,1)S(1)} %get-tuple-element.35.own_ref.refs_0_, bf16[512,512]{1,0:T(8,128)(2,1)S(1)} %collective-permute-done.2.other_ref.refs_4_), custom_call_target="tpu_custom_call" | custom-call | bytes 300000 | tf_op jit(solution)/shard_map/pallas_call | solution.py:696
  13.2 0.0 collective-permute-done.1
  13.3 0.3 %collective-permute-start.3 = (bf16[128,128]{1,0:T(8,128)(2,1)S(1)}, bf16[128,128]{1,0:T(8,128)(2,1)S(1)}, u32[]{:S(2)}, u32[]{:S(2)}) collective-permute-start(bf16[128,128]{1,0:T(8,128)(2,1)S(1)} %pad_maximum_fusion.1.own_part_ref), channel_id=1, source_target_pairs={{0,1},{1,0},{2,3},{3,2},{4,5},{5,4},{6,7},{7,6},{8,9},{9,8},{10,11... | collective-permute-start | bytes 98312 | tf_op jit(solution)/shard_map/ppermute | solution.py:620
  13.5 0.0 collective-permute-done.7.refs_3_.refs_6_
  13.5 1.5 %shard_map.49.refs_9_ = f32[14,64,256]{2,1,0:T(8,128)S(1)} custom-call(bf16[2,512,256]{2,1,0:T(8,128)(2,1)S(1)} %get-tuple-element.33.weights, bf16[128,192]{1,0:T(8,128)(2,1)S(1)} %get-tuple-element.34.left_rows_ref, bf16[512,512]{1,0:T(8,128)(2,1)S(1)} %get-tuple-element.35.own_ref.refs_0_, bf16[512,512]{1,0:T(8,128)(2,1)S(1)} %collective-permute-done.2.other_ref.refs_4_, ...), custom_call_target="tpu_custom_call" | custom-call | bytes 300000 | tf_op jit(solution)/shard_map/pallas_call | solution.py:696
  15.0 0.2 %collective-permute-done.6.refs_3_ = bf16[64,640]{1,0:T(8,128)(2,1)S(1)} collective-permute-done((bf16[64,640]{1,0:T(8,128)(2,1)S(1)}, bf16[64,640]{1,0:T(8,128)(2,1)S(1)}, u32[]{:S(2)}, u32[]{:S(2)}) %collective-permute-start.6) | collective-permute-done | bytes 81952 | tf_op jit(solution)/shard_map/ppermute | solution.py:613
  15.2 0.0 collective-permute-done.3.other_part_ref
  15.2 0.2 collective-permute-start.8
  15.4 0.0 copy-start.1
  15.4 1.3 %shard_map.50 = (f32[2,2,4,32,128]{4,3,2,1,0:T(8,128)S(1)}, f32[2,8,16]{2,1,0:T(8,128)S(1)}) custom-call(bf16[64,256]{1,0:T(8,128)(2,1)S(1)} %get-tuple-element.28.forward_rows_ref, bf16[768,256]{1,0:T(8,128)(2,1)S(1)} %get-tuple-element.26.inverse_ref, bf16[64,256]{1,0:T(8,128)(2,1)S(1)} %get-tuple-element.27.inverse_rows_ref, ...), custom_call_target="tpu_custom_call" | custom-call | bytes 300000 | tf_op jit(solution)/shard_map/pallas_call | solution.py:715
  16.8 0.0 collective-permute-done.8.refs_7_
  16.8 0.0 copy-done.1
  16.8 3.6 %shard_map.51 = f32[2,1,8,16]{3,2,1,0:T(8,128)} custom-call(bf16[768,256]{1,0:T(8,128)(2,1)S(1)} %get-tuple-element.26.inverse_ref, bf16[64,256]{1,0:T(8,128)(2,1)S(1)} %get-tuple-element.27.inverse_rows_ref, s32[16,16]{1,0:T(8,128)S(1)} %copy-done.1, f32[2,8,16]{2,1,0:T(8,128)S(1)} %get-tuple-element.42.base_ref, ...), custom_call_target="tpu_custom_call" | custom-call | bytes 300000 | tf_op jit(solution)/shard_map/pallas_call | solution.py:737
  (8 shorter events, 0.0 us)
Async XLA Ops:
  0.0 1.0 %copy-start = (bf16[1,512,512]{2,1,0:T(8,128)(2,1)S(1)}, bf16[1,512,512]{2,1,0:T(8,128)(2,1)}, u32[]{:S(2)}) copy-start(bf16[1,512,512]{2,1,0:T(8,128)(2,1)} %param.4) | copy-start | bytes 1572868
  1.4 5.4 %collective-permute-start = (bf16[288,128]{1,0:T(8,128)(2,1)S(1)}, bf16[288,128]{1,0:T(8,128)(2,1)S(1)}, u32[]{:S(2)}, u32[]{:S(2)}) collective-permute-start(bf16[288,128]{1,0:T(8,128)(2,1)S(1)} %get-tuple-element.32), channel_id=1, source_target_pairs={{0,4},{4,0},{8,12},{12,8},{1,5},{5,1},{9,13},{13,9},{2,6},{6,2},{1... | collective-permute-start | bytes 221192 | tf_op jit(solution)/shard_map/ppermute | solution.py:605
  4.5 5.8 %collective-permute-start.4 = (bf16[256,128]{1,0:T(8,128)(2,1)S(1)}, bf16[256,128]{1,0:T(8,128)(2,1)S(1)}, u32[]{:S(2)}, u32[]{:S(2)}) collective-permute-start(bf16[256,128]{1,0:T(8,128)(2,1)S(1)} %slice.22), channel_id=1, source_target_pairs={{8,4},{9,5},{10,6},{11,7},{24,20},{25,21},{26,22},{27,23}} | collective-permute-start | bytes 196616 | tf_op jit(solution)/shard_map/ppermute | solution.py:681
  5.1 6.8 %collective-permute-start.2 = (bf16[512,512]{1,0:T(8,128)(2,1)S(1)}, bf16[512,512]{1,0:T(8,128)(2,1)S(1)}, u32[]{:S(2)}, u32[]{:S(2)}) collective-permute-start(bf16[512,512]{1,0:T(8,128)(2,1)S(1)} %get-tuple-element.35.own_ref.refs_0_), channel_id=1, source_target_pairs={{0,1},{1,0},{2,3},{3,2},{4,5},{5,4},{6,7},{7,6},{8,9},{9,8},{10,11... | collective-permute-start | bytes 1572872 | tf_op jit(solution)/shard_map/ppermute | solution.py:620
  5.2 0.7 %copy-start.2 = (s32[2]{0:T(128)S(1)}, s32[2]{0:T(128)}, u32[]{:S(2)}) copy-start(s32[2]{0:T(128)} %param.5) | copy-start | bytes 28
  6.8 3.5 %collective-permute-start.5 = (bf16[256,128]{1,0:T(8,128)(2,1)S(1)}, bf16[256,128]{1,0:T(8,128)(2,1)S(1)}, u32[]{:S(2)}, u32[]{:S(2)}) collective-permute-start(bf16[256,128]{1,0:T(8,128)(2,1)S(1)} %slice.27.refs_0_.refs_1_), channel_id=1, source_target_pairs={{0,1},{1,0},{2,3},{3,2},{4,5},{5,4},{6,7},{7,6},{8,9},{9,8},{10,11... | collective-permute-start | bytes 196616 | tf_op jit(solution)/shard_map/ppermute | solution.py:620
  7.1 6.2 %collective-permute-start.1 = (bf16[64,128]{1,0:T(8,128)(2,1)S(1)}, bf16[64,128]{1,0:T(8,128)(2,1)S(1)}, u32[]{:S(2)}, u32[]{:S(2)}) collective-permute-start(bf16[64,128]{1,0:T(8,128)(2,1)S(1)} %pad_maximum_fusion.2), channel_id=1, source_target_pairs={{0,8},{4,12},{8,0},{12,4},{1,9},{5,13},{9,1},{13,5},{2,10},{6,14},... | collective-permute-start | bytes 49160 | tf_op jit(solution)/shard_map/ppermute | solution.py:605
  10.3 3.3 %collective-permute-start.7 = (bf16[256,128]{1,0:T(8,128)(2,1)S(1)}, bf16[256,128]{1,0:T(8,128)(2,1)S(1)}, u32[]{:S(2)}, u32[]{:S(2)}) collective-permute-start(bf16[256,128]{1,0:T(8,128)(2,1)S(1)} %collective-permute-done.4.refs_1_.refs_2_), channel_id=1, source_target_pairs={{0,1},{1,0},{2,3},{3,2},{4,5},{5,4},{6,7},{7,6},{8,9},{9,8},{10,11... | collective-permute-start | bytes 196616 | tf_op jit(solution)/shard_map/ppermute | solution.py:620
  10.3 4.9 %collective-permute-start.6 = (bf16[64,640]{1,0:T(8,128)(2,1)S(1)}, bf16[64,640]{1,0:T(8,128)(2,1)S(1)}, u32[]{:S(2)}, u32[]{:S(2)}) collective-permute-start(bf16[64,640]{1,0:T(8,128)(2,1)S(1)} %pad_maximum_fusion), channel_id=1, source_target_pairs={{0,2},{2,0},{1,3},{3,1},{4,6},{6,4},{5,7},{7,5},{8,10},{10,8},{9,1... | collective-permute-start | bytes 245768 | tf_op jit(solution)/shard_map/ppermute | solution.py:613
  13.3 2.0 %collective-permute-start.3 = (bf16[128,128]{1,0:T(8,128)(2,1)S(1)}, bf16[128,128]{1,0:T(8,128)(2,1)S(1)}, u32[]{:S(2)}, u32[]{:S(2)}) collective-permute-start(bf16[128,128]{1,0:T(8,128)(2,1)S(1)} %pad_maximum_fusion.1.own_part_ref), channel_id=1, source_target_pairs={{0,1},{1,0},{2,3},{3,2},{4,5},{5,4},{6,7},{7,6},{8,9},{9,8},{10,11... | collective-permute-start | bytes 98312 | tf_op jit(solution)/shard_map/ppermute | solution.py:620
  15.2 1.5 %collective-permute-start.8 = (bf16[64,640]{1,0:T(8,128)(2,1)S(1)}, bf16[64,640]{1,0:T(8,128)(2,1)S(1)}, u32[]{:S(2)}, u32[]{:S(2)}) collective-permute-start(bf16[64,640]{1,0:T(8,128)(2,1)S(1)} %collective-permute-done.6.refs_3_), channel_id=1, source_target_pairs={{0,1},{1,0},{2,3},{3,2},{4,5},{5,4},{6,7},{7,6},{8,9},{9,8},{10,11... | collective-permute-start | bytes 245768 | tf_op jit(solution)/shard_map/ppermute | solution.py:620
  15.4 1.4 %copy-start.1 = (s32[16,16]{1,0:T(8,128)S(1)}, s32[16,16]{1,0:T(8,128)}, u32[]{:S(2)}) copy-start(s32[16,16]{1,0:T(8,128)} %mask_ref.1) | copy-start | bytes 3076

commit v7 on v6

--- a/solution.py
+++ b/solution.py
@@ -321,7 +321,7 @@
     return jnp.where(left, a, b), pltpu.roll(jnp.where(left, b, a), P_SIZE, axis=1)
 
 
-def forward_columns(image, stacked, weights):
+def forward_columns(image, stacked, weights, first_block=0):
     blocks = image.shape[1] // STRIDE
     supers = stacked.shape[3] // (2 * LANES)
     places = [(s, g) for s in range(2) for g in range(supers)]
@@ -335,8 +335,9 @@
                 at = slice(lane + part * LANES, lane + (part + 1) * LANES)
                 for n in range(blocks):
                     block = slice(n * STRIDE, (n + 1) * STRIDE)
-                    stacked[s, t, 2 * n * STRIDE : (2 * n + 1) * STRIDE, at] = high[block]
-                    stacked[s, t, (2 * n + 1) * STRIDE : (2 * n + 2) * STRIDE, at] = low[block]
+                    begin = 2 * (first_block + n) * STRIDE
+                    stacked[s, t, begin : begin + STRIDE, at] = high[block]
+                    stacked[s, t, begin + STRIDE : begin + 2 * STRIDE, at] = low[block]
 
 
 def forward_rows(stacked, left_rows, first_band, out_ref):
@@ -367,7 +368,7 @@
 
 
 def upper_kernel(group, weights, left_rows_ref, own_ref, other_ref, *refs):
-    rights, (out_ref, image, stacked) = refs[:-3], refs[-3:]
+    rights, (out_ref, tail_ref, image, stacked) = refs[:-4], refs[-4:]
     lane = group * 2 * LANES
     wide = 2 * LANES if rights else 3 * LANES
     for s, main in enumerate((own_ref, other_ref)):
@@ -381,22 +382,17 @@
             image[:, :, wide:] = jnp.zeros((2, image.shape[1], LANES), bf16)
 
     forward_columns(image, stacked, weights)
+    tail_ref[...] = stacked[:, :, stacked.shape[2] - 2 * P_SIZE :]
     forward_rows(stacked, left_rows_ref[...], 0, out_ref)
 
 
-def lower_image(own_ref, own_rights, own_low_ref, other_ref, other_rights, other_low_ref, image):
-    rows, width = own_ref.shape
+def lower_image(own_low_ref, other_low_ref, image):
+    shape = own_low_ref.shape
     inside = 1.0 - is_last("gx").astype(f32)
     above = 1.0 - is_last("gy").astype(f32)
-    lane = iota((P_SIZE, width + LANES), 1)
-    keep = jnp.where(lane < width, above, above * inside)
-    for s, (main, right, low) in enumerate(
-        ((own_ref, own_rights, own_low_ref), (other_ref, other_rights, other_low_ref))
-    ):
-        image[s, :P_SIZE, :width] = main[rows - P_SIZE :]
-        edge = from_right(right, slice(rows // 2 - P_SIZE, None)) * inside
-        image[s, :P_SIZE, width:] = pltpu.roll(edge, P_SIZE, axis=1).astype(bf16)
-        image[s, P_SIZE:] = (low[...].astype(f32) * keep).astype(bf16)
+    keep = jnp.where(iota(shape, 1) < shape[1] - LANES, above, above * inside)
+    for s, low in enumerate((own_low_ref, other_low_ref)):
+        image[s] = (low[...].astype(f32) * keep).astype(bf16)
 
 
 def inverse_columns(high, low, table_ref):
@@ -532,13 +528,13 @@
     turns,
     weights,
     left_rows_ref,
+    own_low_ref,
+    other_low_ref,
     *refs,
 ):
-    own_ref, *own_rights, own_low_ref, other_ref = refs[:5]
-    *other_rights, other_low_ref = refs[5:8]
-    spectra = refs[8:-6]
     out_ref, image, stacked, lower_ref, high_ref, low_ref = refs[-6:]
     supers = turns.shape[1]
+    tails, spectra = refs[:supers], refs[supers : 2 * supers]
     per_row = supers * GROUP
     upper_bands = spectra[0].shape[0]
     bands = upper_bands + lower_ref.shape[0]
@@ -566,8 +562,10 @@
                 high_ref[at, lanes] = high
                 low_ref[at, lanes] = low
 
-    lower_image(own_ref, own_rights, own_low_ref, other_ref, other_rights, other_low_ref, image)
-    forward_columns(image, stacked, weights)
+    lower_image(own_low_ref, other_low_ref, image)
+    for g in range(supers):
+        stacked[:, :, : 2 * P_SIZE, g * 2 * LANES : (g + 1) * 2 * LANES] = tails[g][...]
+    forward_columns(image, stacked, weights, P_SIZE // STRIDE)
     for i in range(upper_bands // 2):
         turn_band(i)
     forward_rows(stacked, left_rows_ref[...], upper_bands, lower_ref)
@@ -695,9 +693,12 @@
     def upper(group, *operands):
         return pl.pallas_call(
             functools.partial(upper_kernel, group),
-            out_shape=jax.ShapeDtypeStruct((bands - low_bands, P_SIZE, 2 * LANES), f32),
+            out_shape=(
+                jax.ShapeDtypeStruct((bands - low_bands, P_SIZE, 2 * LANES), f32),
+                jax.ShapeDtypeStruct((2, 2, 2 * P_SIZE, 2 * LANES), bf16),
+            ),
             in_specs=[VMEM] * (4 + len(operands)),
-            out_specs=VMEM,
+            out_specs=(VMEM,) * 2,
             scratch_shapes=[
                 pltpu.VMEM((2, rows, 3 * LANES), bf16),
                 pltpu.VMEM((2, 2, 2 * rows, 2 * LANES), bf16),
@@ -737,10 +738,10 @@
     flow = pl.pallas_call(
         peak_kernel,
         out_shape=jax.ShapeDtypeStruct((2, 1, per_row, bands), f32),
-        in_specs=[VMEM] * (15 + supers),
+        in_specs=[VMEM] * (9 + 2 * supers),
         out_specs=VMEM,
         scratch_shapes=[
-            pltpu.VMEM((2, 2 * P_SIZE, width + LANES), bf16),
+            pltpu.VMEM((2, P_SIZE, width + LANES), bf16),
             pltpu.VMEM((2, 2, 4 * P_SIZE, wide), bf16),
             pltpu.VMEM((low_bands, P_SIZE, wide), f32),
             pltpu.VMEM((bands * P_SIZE, wide), bf16),
@@ -756,15 +757,10 @@
         turns,
         weights,
         left_rows,
-        own_tile,
-        got_right,
-        got_odd,
         own_low,
-        other,
-        other_right,
-        other_odd,
         other_low,
-        *uppers,
+        *(tail for _, tail in uppers),
+        *(spectra for spectra, _ in uppers),
     )
     return jnp.swapaxes(flow, 2, 3)
 

time: 20.5 us -> 20.3 us (level)
  Pallas kernels: 8.58 us -> 8.36 us
    pallas_call x1, Pallas kernels: 3.59 us -> 3.29 us  [local(): pl.pallas_call(peak_kernel, out_shape=jax.ShapeDtypeStruct((2, 1, per_row...]
  transfers between devices with their start and end apart: 9 -> 9, of which waited for: 2 -> 2; matrix products, arithmetic and copies ran while one was open for 1% -> 1% of each run, Pallas kernels for 23% -> 24%
where the time goes in v7:
time: 20.3 us; the launch traced here: 20.1 us
  starting transfers between devices  9.38 us (46%)
  Pallas kernels  8.36 us (41%)
  local copies, waits for them, and re-layouts  1.07 us (5%)
  between operations  0.81 us (4%)
  waiting for transfers between devices  0.43 us (2%)
    ppermute x2, starting transfers between devices, exchanged(): lax.ppermute(value, axis, [(i, i ^ step) for i in range(lax.axis_size(axi...  6.31 us
    pallas_call x1, Pallas kernels, local(): pl.pallas_call(peak_kernel, out_shape=jax.ShapeDtypeStruct((2, 1, per_row...  3.29 us
    pallas_call x2, Pallas kernels, upper(): pl.pallas_call(functools.partial(upper_kernel, group), out_shape=(jax.Sha...  2.9 us
    ppermute x1, starting transfers between devices, from_next(): got.append(lax.ppermute(value, axis, pairs + [(j, i) for i, j in pairs]))  1.56 us
    pallas_call x1, Pallas kernels, local(): pl.pallas_call(turn_kernel, out_shape=(jax.ShapeDtypeStruct((2, supers, 4...  1.34 us
    unnamed x6, local copies, waits for them, and re-layouts  1.05 us
    ppermute x5, starting transfers between devices, swapped(): return lax.ppermute(value, 'gz', [(0, 1), (1, 0)])  0.86 us
    ppermute x1, starting transfers between devices, local(): lax.ppermute(packed[HALF:], 'gx', [(i + 1, i) for i in range(1, count - 1...  0.65 us
  transfers between devices with their start and end apart: 9, of which 2 were waited for; matrix products, arithmetic and copies ran while one was open for 1% of the time, Pallas kernels for 24%

profile of v7, /device:TPU:0, one launch (start us, length us, event | category | flops | bytes accessed | tf_op | source)
XLA Modules:
  0.0 20.1 jit_solution(10304041025944637983)
XLA Ops:
  0.0 0.0 copy-start
  0.0 1.0 %copy-done = bf16[1,512,512]{2,1,0:T(8,128)(2,1)S(1)} copy-done((bf16[1,512,512]{2,1,0:T(8,128)(2,1)S(1)}, bf16[1,512,512]{2,1,0:T(8,128)(2,1)}, u32[]{:S(2)}) %copy-start) | copy-done | bytes 524312
  1.0 0.3 %shard_map.47 = (bf16[512,512]{1,0:T(8,128)(2,1)S(1)}, bf16[64,512]{1,0:T(8,128)(2,1)S(1)}, bf16[288,128]{1,0:T(8,128)(2,1)S(1)}) custom-call(bf16[512,512]{1,0:T(8,128)(2,1)S(1)} %bitcast.2), custom_call_target="tpu_custom_call" | custom-call | bytes 15000000 | tf_op jit(solution)/shard_map/pallas_call | solution.py:645
  1.4 3.1 %collective-permute-start = (bf16[288,128]{1,0:T(8,128)(2,1)S(1)}, bf16[288,128]{1,0:T(8,128)(2,1)S(1)}, u32[]{:S(2)}, u32[]{:S(2)}) collective-permute-start(bf16[288,128]{1,0:T(8,128)(2,1)S(1)} %get-tuple-element.39), channel_id=1, source_target_pairs={{0,4},{4,0},{8,12},{12,8},{1,5},{5,1},{9,13},{13,9},{2,6},{6,2},{1... | collective-permute-start | bytes 221192 | tf_op jit(solution)/shard_map/ppermute | solution.py:603
  4.5 0.7 %collective-permute-start.4 = (bf16[256,128]{1,0:T(8,128)(2,1)S(1)}, bf16[256,128]{1,0:T(8,128)(2,1)S(1)}, u32[]{:S(2)}, u32[]{:S(2)}) collective-permute-start(bf16[256,128]{1,0:T(8,128)(2,1)S(1)} %slice.22), channel_id=1, source_target_pairs={{8,4},{9,5},{10,6},{11,7},{24,20},{25,21},{26,22},{27,23}} | collective-permute-start | bytes 196616 | tf_op jit(solution)/shard_map/ppermute | solution.py:679
  5.1 0.1 collective-permute-start.2
  5.2 0.0 copy-start.2
  5.9 0.0 copy-done.2
  5.9 0.1 pad_add_fusion.offsets_in
  6.0 0.5 %shard_map.46 = (bf16[2,512,256]{2,1,0:T(8,128)(2,1)S(1)}, bf16[2,512,128]{2,1,0:T(8,128)(2,1)S(1)}, bf16[128,192]{1,0:T(8,128)(2,1)S(1)}, s32[2,2,8,128]{3,2,1,...) custom-call(s32[3]{0:T(128)S(1)} %pad_add_fusion.offsets_in), custom_call_target="tpu_custom_call" | custom-call | bytes 300000 | tf_op jit(solution)/shard_map/pallas_call | solution.py:658
  6.5 0.3 %collective-permute-done = bf16[288,128]{1,0:T(8,128)(2,1)S(1)} collective-permute-done((bf16[288,128]{1,0:T(8,128)(2,1)S(1)}, bf16[288,128]{1,0:T(8,128)(2,1)S(1)}, u32[]{:S(2)}, u32[]{:S(2)}) %collective-permute-start) | collective-permute-done | bytes 73760 | tf_op jit(solution)/shard_map/ppermute | solution.py:603
  6.8 0.3 %collective-permute-start.5 = (bf16[256,128]{1,0:T(8,128)(2,1)S(1)}, bf16[256,128]{1,0:T(8,128)(2,1)S(1)}, u32[]{:S(2)}, u32[]{:S(2)}) collective-permute-start(bf16[256,128]{1,0:T(8,128)(2,1)S(1)} %slice.27.refs_0_), channel_id=1, source_target_pairs={{0,1},{1,0},{2,3},{3,2},{4,5},{5,4},{6,7},{7,6},{8,9},{9,8},{10,11... | collective-permute-start | bytes 196616 | tf_op jit(solution)/shard_map/ppermute | solution.py:618
  7.1 3.2 %collective-permute-start.1 = (bf16[64,128]{1,0:T(8,128)(2,1)S(1)}, bf16[64,128]{1,0:T(8,128)(2,1)S(1)}, u32[]{:S(2)}, u32[]{:S(2)}) collective-permute-start(bf16[64,128]{1,0:T(8,128)(2,1)S(1)} %pad_maximum_fusion.2), channel_id=1, source_target_pairs={{0,8},{4,12},{8,0},{12,4},{1,9},{5,13},{9,1},{13,5},{2,10},{6,14},... | collective-permute-start | bytes 49160 | tf_op jit(solution)/shard_map/ppermute | solution.py:603
  10.3 0.0 collective-permute-done.4.refs_1_
  10.3 0.0 collective-permute-done.5.refs_2_
  10.3 0.0 collective-permute-start.7
  10.3 1.6 %collective-permute-start.6 = (bf16[64,640]{1,0:T(8,128)(2,1)S(1)}, bf16[64,640]{1,0:T(8,128)(2,1)S(1)}, u32[]{:S(2)}, u32[]{:S(2)}) collective-permute-start(bf16[64,640]{1,0:T(8,128)(2,1)S(1)} %pad_maximum_fusion), channel_id=1, source_target_pairs={{0,2},{2,0},{1,3},{3,1},{4,6},{6,4},{5,7},{7,5},{8,10},{10,8},{9,1... | collective-permute-start | bytes 245768 | tf_op jit(solution)/shard_map/ppermute | solution.py:611
  11.9 0.0 collective-permute-done.2.other_ref
  11.9 1.4 %shard_map.48 = (f32[14,64,256]{2,1,0:T(8,128)S(1)}, bf16[2,2,128,256]{3,2,1,0:T(8,128)(2,1)S(1)}) custom-call(bf16[2,512,256]{2,1,0:T(8,128)(2,1)S(1)} %get-tuple-element.40.weights, bf16[128,192]{1,0:T(8,128)(2,1)S(1)} %get-tuple-element.41.left_rows_ref, bf16[512,512]{1,0:T(8,128)(2,1)S(1)} %get-tuple-element.42.own_ref, ...), custom_call_target="tpu_custom_call" | custom-call | bytes 300000 | tf_op jit(solution)/shard_map/pallas_call | solution.py:694
  13.3 0.0 collective-permute-done.1
  13.3 0.3 %collective-permute-start.3 = (bf16[128,128]{1,0:T(8,128)(2,1)S(1)}, bf16[128,128]{1,0:T(8,128)(2,1)S(1)}, u32[]{:S(2)}, u32[]{:S(2)}) collective-permute-start(bf16[128,128]{1,0:T(8,128)(2,1)S(1)} %pad_maximum_fusion.1.own_part_ref), channel_id=1, source_target_pairs={{0,1},{1,0},{2,3},{3,2},{4,5},{5,4},{6,7},{7,6},{8,9},{9,8},{10,11... | collective-permute-start | bytes 98312 | tf_op jit(solution)/shard_map/ppermute | solution.py:618
  13.6 0.0 collective-permute-done.7.refs_3_
  13.6 1.5 %shard_map.49 = (f32[14,64,256]{2,1,0:T(8,128)S(1)}, bf16[2,2,128,256]{3,2,1,0:T(8,128)(2,1)S(1)}) custom-call(bf16[2,512,256]{2,1,0:T(8,128)(2,1)S(1)} %get-tuple-element.40.weights, bf16[128,192]{1,0:T(8,128)(2,1)S(1)} %get-tuple-element.41.left_rows_ref, bf16[512,512]{1,0:T(8,128)(2,1)S(1)} %get-tuple-element.42.own_ref, ...), custom_call_target="tpu_custom_call" | custom-call | bytes 300000 | tf_op jit(solution)/shard_map/pallas_call | solution.py:694
  15.1 0.1 collective-permute-done.6.own_low_ref
  15.2 0.0 collective-permute-done.3.other_part_ref
  15.2 0.2 %collective-permute-start.8 = (bf16[64,640]{1,0:T(8,128)(2,1)S(1)}, bf16[64,640]{1,0:T(8,128)(2,1)S(1)}, u32[]{:S(2)}, u32[]{:S(2)}) collective-permute-start(bf16[64,640]{1,0:T(8,128)(2,1)S(1)} %collective-permute-done.6.own_low_ref), channel_id=1, source_target_pairs={{0,1},{1,0},{2,3},{3,2},{4,5},{5,4},{6,7},{7,6},{8,9},{9,8},{10,11... | collective-permute-start | bytes 245768 | tf_op jit(solution)/shard_map/ppermute | solution.py:618
  15.5 0.0 copy-start.1
  15.5 1.3 %shard_map.50 = (f32[2,2,4,32,128]{4,3,2,1,0:T(8,128)S(1)}, f32[2,8,16]{2,1,0:T(8,128)S(1)}) custom-call(bf16[64,256]{1,0:T(8,128)(2,1)S(1)} %get-tuple-element.35.forward_rows_ref, bf16[768,256]{1,0:T(8,128)(2,1)S(1)} %get-tuple-element.33.inverse_ref, bf16[64,256]{1,0:T(8,128)(2,1)S(1)} %get-tuple-element.34.inverse_rows_ref, ...), custom_call_target="tpu_custom_call" | custom-call | bytes 300000 | tf_op jit(solution)/shard_map/pallas_call | solution.py:716
  16.8 0.0 collective-permute-done.8.other_low_ref
  16.8 0.0 copy-done.1
  16.9 3.3 %shard_map.51 = f32[2,1,8,16]{3,2,1,0:T(8,128)} custom-call(bf16[768,256]{1,0:T(8,128)(2,1)S(1)} %get-tuple-element.33.inverse_ref, bf16[64,256]{1,0:T(8,128)(2,1)S(1)} %get-tuple-element.34.inverse_rows_ref, s32[16,16]{1,0:T(8,128)S(1)} %copy-done.1, f32[2,8,16]{2,1,0:T(8,128)S(1)} %get-tuple-element.54.base_ref, ...), custom_call_target="tpu_custom_call" | custom-call | bytes 300000 | tf_op jit(solution)/shard_map/pallas_call | solution.py:738
  (8 shorter events, 0.0 us)
Async XLA Ops:
  0.0 1.0 %copy-start = (bf16[1,512,512]{2,1,0:T(8,128)(2,1)S(1)}, bf16[1,512,512]{2,1,0:T(8,128)(2,1)}, u32[]{:S(2)}) copy-start(bf16[1,512,512]{2,1,0:T(8,128)(2,1)} %param.4) | copy-start | bytes 1572868
  1.4 5.4 %collective-permute-start = (bf16[288,128]{1,0:T(8,128)(2,1)S(1)}, bf16[288,128]{1,0:T(8,128)(2,1)S(1)}, u32[]{:S(2)}, u32[]{:S(2)}) collective-permute-start(bf16[288,128]{1,0:T(8,128)(2,1)S(1)} %get-tuple-element.39), channel_id=1, source_target_pairs={{0,4},{4,0},{8,12},{12,8},{1,5},{5,1},{9,13},{13,9},{2,6},{6,2},{1... | collective-permute-start | bytes 221192 | tf_op jit(solution)/shard_map/ppermute | solution.py:603
  4.5 5.8 %collective-permute-start.4 = (bf16[256,128]{1,0:T(8,128)(2,1)S(1)}, bf16[256,128]{1,0:T(8,128)(2,1)S(1)}, u32[]{:S(2)}, u32[]{:S(2)}) collective-permute-start(bf16[256,128]{1,0:T(8,128)(2,1)S(1)} %slice.22), channel_id=1, source_target_pairs={{8,4},{9,5},{10,6},{11,7},{24,20},{25,21},{26,22},{27,23}} | collective-permute-start | bytes 196616 | tf_op jit(solution)/shard_map/ppermute | solution.py:679
  5.1 6.8 %collective-permute-start.2 = (bf16[512,512]{1,0:T(8,128)(2,1)S(1)}, bf16[512,512]{1,0:T(8,128)(2,1)S(1)}, u32[]{:S(2)}, u32[]{:S(2)}) collective-permute-start(bf16[512,512]{1,0:T(8,128)(2,1)S(1)} %get-tuple-element.42.own_ref), channel_id=1, source_target_pairs={{0,1},{1,0},{2,3},{3,2},{4,5},{5,4},{6,7},{7,6},{8,9},{9,8},{10,11... | collective-permute-start | bytes 1572872 | tf_op jit(solution)/shard_map/ppermute | solution.py:618
  5.2 0.7 %copy-start.2 = (s32[2]{0:T(128)S(1)}, s32[2]{0:T(128)}, u32[]{:S(2)}) copy-start(s32[2]{0:T(128)} %param.5) | copy-start | bytes 28
  6.8 3.5 %collective-permute-start.5 = (bf16[256,128]{1,0:T(8,128)(2,1)S(1)}, bf16[256,128]{1,0:T(8,128)(2,1)S(1)}, u32[]{:S(2)}, u32[]{:S(2)}) collective-permute-start(bf16[256,128]{1,0:T(8,128)(2,1)S(1)} %slice.27.refs_0_), channel_id=1, source_target_pairs={{0,1},{1,0},{2,3},{3,2},{4,5},{5,4},{6,7},{7,6},{8,9},{9,8},{10,11... | collective-permute-start | bytes 196616 | tf_op jit(solution)/shard_map/ppermute | solution.py:618
  7.1 6.2 %collective-permute-start.1 = (bf16[64,128]{1,0:T(8,128)(2,1)S(1)}, bf16[64,128]{1,0:T(8,128)(2,1)S(1)}, u32[]{:S(2)}, u32[]{:S(2)}) collective-permute-start(bf16[64,128]{1,0:T(8,128)(2,1)S(1)} %pad_maximum_fusion.2), channel_id=1, source_target_pairs={{0,8},{4,12},{8,0},{12,4},{1,9},{5,13},{9,1},{13,5},{2,10},{6,14},... | collective-permute-start | bytes 49160 | tf_op jit(solution)/shard_map/ppermute | solution.py:603
  10.3 3.3 %collective-permute-start.7 = (bf16[256,128]{1,0:T(8,128)(2,1)S(1)}, bf16[256,128]{1,0:T(8,128)(2,1)S(1)}, u32[]{:S(2)}, u32[]{:S(2)}) collective-permute-start(bf16[256,128]{1,0:T(8,128)(2,1)S(1)} %collective-permute-done.4.refs_1_), channel_id=1, source_target_pairs={{0,1},{1,0},{2,3},{3,2},{4,5},{5,4},{6,7},{7,6},{8,9},{9,8},{10,11... | collective-permute-start | bytes 196616 | tf_op jit(solution)/shard_map/ppermute | solution.py:618
  10.3 4.9 %collective-permute-start.6 = (bf16[64,640]{1,0:T(8,128)(2,1)S(1)}, bf16[64,640]{1,0:T(8,128)(2,1)S(1)}, u32[]{:S(2)}, u32[]{:S(2)}) collective-permute-start(bf16[64,640]{1,0:T(8,128)(2,1)S(1)} %pad_maximum_fusion), channel_id=1, source_target_pairs={{0,2},{2,0},{1,3},{3,1},{4,6},{6,4},{5,7},{7,5},{8,10},{10,8},{9,1... | collective-permute-start | bytes 245768 | tf_op jit(solution)/shard_map/ppermute | solution.py:611
  13.3 1.9 %collective-permute-start.3 = (bf16[128,128]{1,0:T(8,128)(2,1)S(1)}, bf16[128,128]{1,0:T(8,128)(2,1)S(1)}, u32[]{:S(2)}, u32[]{:S(2)}) collective-permute-start(bf16[128,128]{1,0:T(8,128)(2,1)S(1)} %pad_maximum_fusion.1.own_part_ref), channel_id=1, source_target_pairs={{0,1},{1,0},{2,3},{3,2},{4,5},{5,4},{6,7},{7,6},{8,9},{9,8},{10,11... | collective-permute-start | bytes 98312 | tf_op jit(solution)/shard_map/ppermute | solution.py:618
  15.2 1.6 %collective-permute-start.8 = (bf16[64,640]{1,0:T(8,128)(2,1)S(1)}, bf16[64,640]{1,0:T(8,128)(2,1)S(1)}, u32[]{:S(2)}, u32[]{:S(2)}) collective-permute-start(bf16[64,640]{1,0:T(8,128)(2,1)S(1)} %collective-permute-done.6.own_low_ref), channel_id=1, source_target_pairs={{0,1},{1,0},{2,3},{3,2},{4,5},{5,4},{6,7},{7,6},{8,9},{9,8},{10,11... | collective-permute-start | bytes 245768 | tf_op jit(solution)/shard_map/ppermute | solution.py:618
  15.5 1.4 %copy-start.1 = (s32[16,16]{1,0:T(8,128)S(1)}, s32[16,16]{1,0:T(8,128)}, u32[]{:S(2)}) copy-start(s32[16,16]{1,0:T(8,128)} %mask_ref.1) | copy-start | bytes 3076

commit v8 on v7

--- a/solution.py
+++ b/solution.py
@@ -15,6 +15,7 @@
 LANES = 128
 GROUP = LANES // HALF
 SHARPNESS = 12.0
+SUBLANES = 8
 SCALE = SHARPNESS / float(P_SIZE) ** 4 * math.log2(math.e)
 
 f32 = jnp.float32
@@ -484,23 +485,34 @@
         ]
 
     shape = (HALF, LANES)
-    frequency_y = iota(shape, 0).astype(f32) * (1.0 / P_SIZE)
     l0 = first_lane(shape)
     r0 = iota(shape, 0) == 0
-    lane_row = iota((1, LANES), 1)
-    frequency_x = remainder(lane_row, HALF).astype(f32) * (1.0 / P_SIZE)
+    row = iota((SUBLANES, LANES), 0)
+    steps = row.astype(f32) * (1.0 / P_SIZE)
+    frequency_x = remainder(iota((1, LANES), 1), HALF).astype(f32) * (1.0 / P_SIZE)
+    blocks = HALF // SUBLANES
     for t in range(2):
         for g in range(supers):
             dy, dx = (
                 value - P_SIZE * jnp.round(value * (1.0 / P_SIZE)) for value in prior(picks_ref[t, g, :1])
             )
-            turn_y = nearest(frequency_y * dy)
-            turn_x = nearest(frequency_x * dx)
-            cy, sy = cosine_of_turns(turn_y), sine_of_turns(turn_y)
-            cx, sx = cosine_of_turns(turn_x), sine_of_turns(turn_x)
-            half_y = cosine_of_turns(nearest(0.5 * dy))
-            half_x = cosine_of_turns(nearest(0.5 * dx))
-            half_both = cosine_of_turns(nearest(0.5 * (dy + dx)))
+            few = SUBLANES * steps * dy
+            for n, value in enumerate((frequency_x * dx, 0.5 * dy, 0.5 * dx, 0.5 * (dy + dx))):
+                few = jnp.where(row == blocks + n, value, few)
+            few = nearest(few)
+            near = nearest(steps * dy)
+            few_cosine, few_sine = cosine_of_turns(few), sine_of_turns(few)
+            cosine, sine = cosine_of_turns(near), sine_of_turns(near)
+            cy, sy = [], []
+            for n in range(blocks):
+                c, s = few_cosine[n : n + 1], few_sine[n : n + 1]
+                cy.append(cosine * c - sine * s)
+                sy.append(sine * c + cosine * s)
+            cy, sy = jnp.concatenate(cy, axis=0), jnp.concatenate(sy, axis=0)
+            cx, sx = few_cosine[blocks : blocks + 1], few_sine[blocks : blocks + 1]
+            half_y, half_x, half_both = (
+                few_cosine[n : n + 1] for n in range(blocks + 1, blocks + 4)
+            )
             plus_real = cy * cx - sy * sx
             plus_imaginary = sy * cx + cy * sx
             minus_real = cy * cx + sy * sx

time: 20.3 us -> 20.2 us (level)
  transfers between devices with their start and end apart: 9 -> 9, of which waited for: 2 -> 2; matrix products, arithmetic and copies ran while one was open for 1% -> 1% of each run, Pallas kernels for 24% -> 23%
where the time goes in v8:
time: 20.2 us; the launch traced here: 20.1 us
  starting transfers between devices  9.38 us (46%)
  Pallas kernels  8.27 us (41%)
  local copies, waits for them, and re-layouts  1.07 us (5%)
  between operations  0.81 us (4%)
  waiting for transfers between devices  0.43 us (2%)
    ppermute x2, starting transfers between devices, exchanged(): lax.ppermute(value, axis, [(i, i ^ step) for i in range(lax.axis_size(axi...  6.31 us
    pallas_call x1, Pallas kernels, local(): pl.pallas_call(peak_kernel, out_shape=jax.ShapeDtypeStruct((2, 1, per_row...  3.29 us
    pallas_call x2, Pallas kernels, upper(): pl.pallas_call(functools.partial(upper_kernel, group), out_shape=(jax.Sha...  2.9 us
    ppermute x1, starting transfers between devices, from_next(): got.append(lax.ppermute(value, axis, pairs + [(j, i) for i, j in pairs]))  1.56 us
    pallas_call x1, Pallas kernels, local(): pl.pallas_call(turn_kernel, out_shape=(jax.ShapeDtypeStruct((2, supers, 4...  1.26 us
    unnamed x6, local copies, waits for them, and re-layouts  1.05 us
    ppermute x5, starting transfers between devices, swapped(): return lax.ppermute(value, 'gz', [(0, 1), (1, 0)])  0.86 us
    ppermute x1, starting transfers between devices, local(): lax.ppermute(packed[HALF:], 'gx', [(i + 1, i) for i in range(1, count - 1...  0.65 us
  transfers between devices with their start and end apart: 9, of which 2 were waited for; matrix products, arithmetic and copies ran while one was open for 1% of the time, Pallas kernels for 23%

profile of v8, /device:TPU:0, one launch (start us, length us, event | category | flops | bytes accessed | tf_op | source)
XLA Modules:
  0.0 20.1 jit_solution(13594507409783440509)
XLA Ops:
  0.0 0.0 copy-start
  0.0 1.0 %copy-done = bf16[1,512,512]{2,1,0:T(8,128)(2,1)S(1)} copy-done((bf16[1,512,512]{2,1,0:T(8,128)(2,1)S(1)}, bf16[1,512,512]{2,1,0:T(8,128)(2,1)}, u32[]{:S(2)}) %copy-start) | copy-done | bytes 524312
  1.0 0.3 %shard_map.47 = (bf16[512,512]{1,0:T(8,128)(2,1)S(1)}, bf16[64,512]{1,0:T(8,128)(2,1)S(1)}, bf16[288,128]{1,0:T(8,128)(2,1)S(1)}) custom-call(bf16[512,512]{1,0:T(8,128)(2,1)S(1)} %bitcast.2), custom_call_target="tpu_custom_call" | custom-call | bytes 15000000 | tf_op jit(solution)/shard_map/pallas_call | solution.py:657
  1.4 3.1 %collective-permute-start = (bf16[288,128]{1,0:T(8,128)(2,1)S(1)}, bf16[288,128]{1,0:T(8,128)(2,1)S(1)}, u32[]{:S(2)}, u32[]{:S(2)}) collective-permute-start(bf16[288,128]{1,0:T(8,128)(2,1)S(1)} %get-tuple-element.39), channel_id=1, source_target_pairs={{0,4},{4,0},{8,12},{12,8},{1,5},{5,1},{9,13},{13,9},{2,6},{6,2},{1... | collective-permute-start | bytes 221192 | tf_op jit(solution)/shard_map/ppermute | solution.py:615
  4.5 0.7 %collective-permute-start.4 = (bf16[256,128]{1,0:T(8,128)(2,1)S(1)}, bf16[256,128]{1,0:T(8,128)(2,1)S(1)}, u32[]{:S(2)}, u32[]{:S(2)}) collective-permute-start(bf16[256,128]{1,0:T(8,128)(2,1)S(1)} %slice.22), channel_id=1, source_target_pairs={{8,4},{9,5},{10,6},{11,7},{24,20},{25,21},{26,22},{27,23}} | collective-permute-start | bytes 196616 | tf_op jit(solution)/shard_map/ppermute | solution.py:691
  5.1 0.1 collective-permute-start.2
  5.2 0.0 copy-start.2
  5.9 0.0 copy-done.2
  5.9 0.1 pad_add_fusion.offsets_in
  6.0 0.5 %shard_map.46 = (bf16[2,512,256]{2,1,0:T(8,128)(2,1)S(1)}, bf16[2,512,128]{2,1,0:T(8,128)(2,1)S(1)}, bf16[128,192]{1,0:T(8,128)(2,1)S(1)}, s32[2,2,8,128]{3,2,1,...) custom-call(s32[3]{0:T(128)S(1)} %pad_add_fusion.offsets_in), custom_call_target="tpu_custom_call" | custom-call | bytes 300000 | tf_op jit(solution)/shard_map/pallas_call | solution.py:670
  6.5 0.3 %collective-permute-done = bf16[288,128]{1,0:T(8,128)(2,1)S(1)} collective-permute-done((bf16[288,128]{1,0:T(8,128)(2,1)S(1)}, bf16[288,128]{1,0:T(8,128)(2,1)S(1)}, u32[]{:S(2)}, u32[]{:S(2)}) %collective-permute-start) | collective-permute-done | bytes 73760 | tf_op jit(solution)/shard_map/ppermute | solution.py:615
  6.8 0.3 %collective-permute-start.5 = (bf16[256,128]{1,0:T(8,128)(2,1)S(1)}, bf16[256,128]{1,0:T(8,128)(2,1)S(1)}, u32[]{:S(2)}, u32[]{:S(2)}) collective-permute-start(bf16[256,128]{1,0:T(8,128)(2,1)S(1)} %slice.27.refs_0_), channel_id=1, source_target_pairs={{0,1},{1,0},{2,3},{3,2},{4,5},{5,4},{6,7},{7,6},{8,9},{9,8},{10,11... | collective-permute-start | bytes 196616 | tf_op jit(solution)/shard_map/ppermute | solution.py:630
  7.1 3.2 %collective-permute-start.1 = (bf16[64,128]{1,0:T(8,128)(2,1)S(1)}, bf16[64,128]{1,0:T(8,128)(2,1)S(1)}, u32[]{:S(2)}, u32[]{:S(2)}) collective-permute-start(bf16[64,128]{1,0:T(8,128)(2,1)S(1)} %pad_maximum_fusion.2), channel_id=1, source_target_pairs={{0,8},{4,12},{8,0},{12,4},{1,9},{5,13},{9,1},{13,5},{2,10},{6,14},... | collective-permute-start | bytes 49160 | tf_op jit(solution)/shard_map/ppermute | solution.py:615
  10.3 0.0 collective-permute-done.4.refs_1_
  10.3 0.0 collective-permute-done.5.refs_2_
  10.3 0.0 collective-permute-start.7
  10.3 1.6 %collective-permute-start.6 = (bf16[64,640]{1,0:T(8,128)(2,1)S(1)}, bf16[64,640]{1,0:T(8,128)(2,1)S(1)}, u32[]{:S(2)}, u32[]{:S(2)}) collective-permute-start(bf16[64,640]{1,0:T(8,128)(2,1)S(1)} %pad_maximum_fusion), channel_id=1, source_target_pairs={{0,2},{2,0},{1,3},{3,1},{4,6},{6,4},{5,7},{7,5},{8,10},{10,8},{9,1... | collective-permute-start | bytes 245768 | tf_op jit(solution)/shard_map/ppermute | solution.py:623
  11.9 0.0 collective-permute-done.2.other_ref
  11.9 1.4 %shard_map.48 = (f32[14,64,256]{2,1,0:T(8,128)S(1)}, bf16[2,2,128,256]{3,2,1,0:T(8,128)(2,1)S(1)}) custom-call(bf16[2,512,256]{2,1,0:T(8,128)(2,1)S(1)} %get-tuple-element.40.weights, bf16[128,192]{1,0:T(8,128)(2,1)S(1)} %get-tuple-element.41.left_rows_ref, bf16[512,512]{1,0:T(8,128)(2,1)S(1)} %get-tuple-element.42.own_ref, ...), custom_call_target="tpu_custom_call" | custom-call | bytes 300000 | tf_op jit(solution)/shard_map/pallas_call | solution.py:706
  13.3 0.0 collective-permute-done.1
  13.3 0.3 %collective-permute-start.3 = (bf16[128,128]{1,0:T(8,128)(2,1)S(1)}, bf16[128,128]{1,0:T(8,128)(2,1)S(1)}, u32[]{:S(2)}, u32[]{:S(2)}) collective-permute-start(bf16[128,128]{1,0:T(8,128)(2,1)S(1)} %pad_maximum_fusion.1.own_part_ref), channel_id=1, source_target_pairs={{0,1},{1,0},{2,3},{3,2},{4,5},{5,4},{6,7},{7,6},{8,9},{9,8},{10,11... | collective-permute-start | bytes 98312 | tf_op jit(solution)/shard_map/ppermute | solution.py:630
  13.6 0.0 collective-permute-done.7.refs_3_
  13.6 1.5 %shard_map.49 = (f32[14,64,256]{2,1,0:T(8,128)S(1)}, bf16[2,2,128,256]{3,2,1,0:T(8,128)(2,1)S(1)}) custom-call(bf16[2,512,256]{2,1,0:T(8,128)(2,1)S(1)} %get-tuple-element.40.weights, bf16[128,192]{1,0:T(8,128)(2,1)S(1)} %get-tuple-element.41.left_rows_ref, bf16[512,512]{1,0:T(8,128)(2,1)S(1)} %get-tuple-element.42.own_ref, ...), custom_call_target="tpu_custom_call" | custom-call | bytes 300000 | tf_op jit(solution)/shard_map/pallas_call | solution.py:706
  15.1 0.1 collective-permute-done.6.own_low_ref
  15.2 0.0 collective-permute-done.3.other_part_ref
  15.2 0.2 %collective-permute-start.8 = (bf16[64,640]{1,0:T(8,128)(2,1)S(1)}, bf16[64,640]{1,0:T(8,128)(2,1)S(1)}, u32[]{:S(2)}, u32[]{:S(2)}) collective-permute-start(bf16[64,640]{1,0:T(8,128)(2,1)S(1)} %collective-permute-done.6.own_low_ref), channel_id=1, source_target_pairs={{0,1},{1,0},{2,3},{3,2},{4,5},{5,4},{6,7},{7,6},{8,9},{9,8},{10,11... | collective-permute-start | bytes 245768 | tf_op jit(solution)/shard_map/ppermute | solution.py:630
  15.5 0.0 copy-start.1
  15.5 1.3 %shard_map.50 = (f32[2,2,4,32,128]{4,3,2,1,0:T(8,128)S(1)}, f32[2,8,16]{2,1,0:T(8,128)S(1)}) custom-call(bf16[64,256]{1,0:T(8,128)(2,1)S(1)} %get-tuple-element.35.forward_rows_ref, bf16[768,256]{1,0:T(8,128)(2,1)S(1)} %get-tuple-element.33.inverse_ref, bf16[64,256]{1,0:T(8,128)(2,1)S(1)} %get-tuple-element.34.inverse_rows_ref, ...), custom_call_target="tpu_custom_call" | custom-call | bytes 300000 | tf_op jit(solution)/shard_map/pallas_call | solution.py:728
  16.8 0.0 collective-permute-done.8.other_low_ref
  16.8 0.0 copy-done.1
  16.8 3.3 %shard_map.51 = f32[2,1,8,16]{3,2,1,0:T(8,128)} custom-call(bf16[768,256]{1,0:T(8,128)(2,1)S(1)} %get-tuple-element.33.inverse_ref, bf16[64,256]{1,0:T(8,128)(2,1)S(1)} %get-tuple-element.34.inverse_rows_ref, s32[16,16]{1,0:T(8,128)S(1)} %copy-done.1, f32[2,8,16]{2,1,0:T(8,128)S(1)} %get-tuple-element.54.base_ref, ...), custom_call_target="tpu_custom_call" | custom-call | bytes 300000 | tf_op jit(solution)/shard_map/pallas_call | solution.py:750
  (8 shorter events, 0.0 us)
Async XLA Ops:
  0.0 1.0 %copy-start = (bf16[1,512,512]{2,1,0:T(8,128)(2,1)S(1)}, bf16[1,512,512]{2,1,0:T(8,128)(2,1)}, u32[]{:S(2)}) copy-start(bf16[1,512,512]{2,1,0:T(8,128)(2,1)} %param.4) | copy-start | bytes 1572868
  1.4 5.4 %collective-permute-start = (bf16[288,128]{1,0:T(8,128)(2,1)S(1)}, bf16[288,128]{1,0:T(8,128)(2,1)S(1)}, u32[]{:S(2)}, u32[]{:S(2)}) collective-permute-start(bf16[288,128]{1,0:T(8,128)(2,1)S(1)} %get-tuple-element.39), channel_id=1, source_target_pairs={{0,4},{4,0},{8,12},{12,8},{1,5},{5,1},{9,13},{13,9},{2,6},{6,2},{1... | collective-permute-start | bytes 221192 | tf_op jit(solution)/shard_map/ppermute | solution.py:615
  4.5 5.8 %collective-permute-start.4 = (bf16[256,128]{1,0:T(8,128)(2,1)S(1)}, bf16[256,128]{1,0:T(8,128)(2,1)S(1)}, u32[]{:S(2)}, u32[]{:S(2)}) collective-permute-start(bf16[256,128]{1,0:T(8,128)(2,1)S(1)} %slice.22), channel_id=1, source_target_pairs={{8,4},{9,5},{10,6},{11,7},{24,20},{25,21},{26,22},{27,23}} | collective-permute-start | bytes 196616 | tf_op jit(solution)/shard_map/ppermute | solution.py:691
  5.1 6.8 %collective-permute-start.2 = (bf16[512,512]{1,0:T(8,128)(2,1)S(1)}, bf16[512,512]{1,0:T(8,128)(2,1)S(1)}, u32[]{:S(2)}, u32[]{:S(2)}) collective-permute-start(bf16[512,512]{1,0:T(8,128)(2,1)S(1)} %get-tuple-element.42.own_ref), channel_id=1, source_target_pairs={{0,1},{1,0},{2,3},{3,2},{4,5},{5,4},{6,7},{7,6},{8,9},{9,8},{10,11... | collective-permute-start | bytes 1572872 | tf_op jit(solution)/shard_map/ppermute | solution.py:630
  5.2 0.7 %copy-start.2 = (s32[2]{0:T(128)S(1)}, s32[2]{0:T(128)}, u32[]{:S(2)}) copy-start(s32[2]{0:T(128)} %param.5) | copy-start | bytes 28
  6.8 3.5 %collective-permute-start.5 = (bf16[256,128]{1,0:T(8,128)(2,1)S(1)}, bf16[256,128]{1,0:T(8,128)(2,1)S(1)}, u32[]{:S(2)}, u32[]{:S(2)}) collective-permute-start(bf16[256,128]{1,0:T(8,128)(2,1)S(1)} %slice.27.refs_0_), channel_id=1, source_target_pairs={{0,1},{1,0},{2,3},{3,2},{4,5},{5,4},{6,7},{7,6},{8,9},{9,8},{10,11... | collective-permute-start | bytes 196616 | tf_op jit(solution)/shard_map/ppermute | solution.py:630
  7.1 6.2 %collective-permute-start.1 = (bf16[64,128]{1,0:T(8,128)(2,1)S(1)}, bf16[64,128]{1,0:T(8,128)(2,1)S(1)}, u32[]{:S(2)}, u32[]{:S(2)}) collective-permute-start(bf16[64,128]{1,0:T(8,128)(2,1)S(1)} %pad_maximum_fusion.2), channel_id=1, source_target_pairs={{0,8},{4,12},{8,0},{12,4},{1,9},{5,13},{9,1},{13,5},{2,10},{6,14},... | collective-permute-start | bytes 49160 | tf_op jit(solution)/shard_map/ppermute | solution.py:615
  10.3 3.3 %collective-permute-start.7 = (bf16[256,128]{1,0:T(8,128)(2,1)S(1)}, bf16[256,128]{1,0:T(8,128)(2,1)S(1)}, u32[]{:S(2)}, u32[]{:S(2)}) collective-permute-start(bf16[256,128]{1,0:T(8,128)(2,1)S(1)} %collective-permute-done.4.refs_1_), channel_id=1, source_target_pairs={{0,1},{1,0},{2,3},{3,2},{4,5},{5,4},{6,7},{7,6},{8,9},{9,8},{10,11... | collective-permute-start | bytes 196616 | tf_op jit(solution)/shard_map/ppermute | solution.py:630
  10.3 4.9 %collective-permute-start.6 = (bf16[64,640]{1,0:T(8,128)(2,1)S(1)}, bf16[64,640]{1,0:T(8,128)(2,1)S(1)}, u32[]{:S(2)}, u32[]{:S(2)}) collective-permute-start(bf16[64,640]{1,0:T(8,128)(2,1)S(1)} %pad_maximum_fusion), channel_id=1, source_target_pairs={{0,2},{2,0},{1,3},{3,1},{4,6},{6,4},{5,7},{7,5},{8,10},{10,8},{9,1... | collective-permute-start | bytes 245768 | tf_op jit(solution)/shard_map/ppermute | solution.py:623
  13.3 1.9 %collective-permute-start.3 = (bf16[128,128]{1,0:T(8,128)(2,1)S(1)}, bf16[128,128]{1,0:T(8,128)(2,1)S(1)}, u32[]{:S(2)}, u32[]{:S(2)}) collective-permute-start(bf16[128,128]{1,0:T(8,128)(2,1)S(1)} %pad_maximum_fusion.1.own_part_ref), channel_id=1, source_target_pairs={{0,1},{1,0},{2,3},{3,2},{4,5},{5,4},{6,7},{7,6},{8,9},{9,8},{10,11... | collective-permute-start | bytes 98312 | tf_op jit(solution)/shard_map/ppermute | solution.py:630
  15.2 1.5 %collective-permute-start.8 = (bf16[64,640]{1,0:T(8,128)(2,1)S(1)}, bf16[64,640]{1,0:T(8,128)(2,1)S(1)}, u32[]{:S(2)}, u32[]{:S(2)}) collective-permute-start(bf16[64,640]{1,0:T(8,128)(2,1)S(1)} %collective-permute-done.6.own_low_ref), channel_id=1, source_target_pairs={{0,1},{1,0},{2,3},{3,2},{4,5},{5,4},{6,7},{7,6},{8,9},{9,8},{10,11... | collective-permute-start | bytes 245768 | tf_op jit(solution)/shard_map/ppermute | solution.py:630
  15.5 1.3 %copy-start.1 = (s32[16,16]{1,0:T(8,128)S(1)}, s32[16,16]{1,0:T(8,128)}, u32[]{:S(2)}) copy-start(s32[16,16]{1,0:T(8,128)} %mask_ref.1) | copy-start | bytes 3076

commit v9 on v8

--- a/solution.py
+++ b/solution.py
@@ -322,7 +322,7 @@
     return jnp.where(left, a, b), pltpu.roll(jnp.where(left, b, a), P_SIZE, axis=1)
 
 
-def forward_columns(image, stacked, weights, first_block=0):
+def forward_columns(image, stacked, weights, unread, first_block=0):
     blocks = image.shape[1] // STRIDE
     supers = stacked.shape[3] // (2 * LANES)
     places = [(s, g) for s in range(2) for g in range(supers)]
@@ -335,6 +335,8 @@
                 high, low = split(value)
                 at = slice(lane + part * LANES, lane + (part + 1) * LANES)
                 for n in range(blocks):
+                    if (t, n) == unread:
+                        continue
                     block = slice(n * STRIDE, (n + 1) * STRIDE)
                     begin = 2 * (first_block + n) * STRIDE
                     stacked[s, t, begin : begin + STRIDE, at] = high[block]
@@ -382,7 +384,7 @@
         def _():
             image[:, :, wide:] = jnp.zeros((2, image.shape[1], LANES), bf16)
 
-    forward_columns(image, stacked, weights)
+    forward_columns(image, stacked, weights, (1, 0))
     tail_ref[...] = stacked[:, :, stacked.shape[2] - 2 * P_SIZE :]
     forward_rows(stacked, left_rows_ref[...], 0, out_ref)
 
@@ -577,7 +579,7 @@
     lower_image(own_low_ref, other_low_ref, image)
     for g in range(supers):
         stacked[:, :, : 2 * P_SIZE, g * 2 * LANES : (g + 1) * 2 * LANES] = tails[g][...]
-    forward_columns(image, stacked, weights, P_SIZE // STRIDE)
+    forward_columns(image, stacked, weights, (0, P_SIZE // STRIDE - 1), P_SIZE // STRIDE)
     for i in range(upper_bands // 2):
         turn_band(i)
     forward_rows(stacked, left_rows_ref[...], upper_bands, lower_ref)

time: 20.2 us -> 20.3 us (level)
  no operation moved by 1% of the time
where the time goes in v9:
time: 20.3 us; the launch traced here: 20.1 us
  starting transfers between devices  9.38 us (46%)
  Pallas kernels  8.27 us (41%)
  local copies, waits for them, and re-layouts  1.07 us (5%)
  between operations  0.81 us (4%)
  waiting for transfers between devices  0.44 us (2%)
    ppermute x2, starting transfers between devices, exchanged(): lax.ppermute(value, axis, [(i, i ^ step) for i in range(lax.axis_size(axi...  6.31 us
    pallas_call x1, Pallas kernels, local(): pl.pallas_call(peak_kernel, out_shape=jax.ShapeDtypeStruct((2, 1, per_row...  3.3 us
    pallas_call x2, Pallas kernels, upper(): pl.pallas_call(functools.partial(upper_kernel, group), out_shape=(jax.Sha...  2.89 us
    ppermute x1, starting transfers between devices, from_next(): got.append(lax.ppermute(value, axis, pairs + [(j, i) for i, j in pairs]))  1.56 us
    pallas_call x1, Pallas kernels, local(): pl.pallas_call(turn_kernel, out_shape=(jax.ShapeDtypeStruct((2, supers, 4...  1.26 us
    unnamed x6, local copies, waits for them, and re-layouts  1.05 us
    ppermute x5, starting transfers between devices, swapped(): return lax.ppermute(value, 'gz', [(0, 1), (1, 0)])  0.87 us
    ppermute x1, starting transfers between devices, local(): lax.ppermute(packed[HALF:], 'gx', [(i + 1, i) for i in range(1, count - 1...  0.65 us
  transfers between devices with their start and end apart: 9, of which 2 were waited for; matrix products, arithmetic and copies ran while one was open for 1% of the time, Pallas kernels for 23%

profile of v9, /device:TPU:0, one launch (start us, length us, event | category | flops | bytes accessed | tf_op | source)
XLA Modules:
  0.0 20.1 jit_solution(9980938027039208206)
XLA Ops:
  0.0 0.0 copy-start
  0.0 1.0 %copy-done = bf16[1,512,512]{2,1,0:T(8,128)(2,1)S(1)} copy-done((bf16[1,512,512]{2,1,0:T(8,128)(2,1)S(1)}, bf16[1,512,512]{2,1,0:T(8,128)(2,1)}, u32[]{:S(2)}) %copy-start) | copy-done | bytes 524312
  1.0 0.3 %shard_map.47 = (bf16[512,512]{1,0:T(8,128)(2,1)S(1)}, bf16[64,512]{1,0:T(8,128)(2,1)S(1)}, bf16[288,128]{1,0:T(8,128)(2,1)S(1)}) custom-call(bf16[512,512]{1,0:T(8,128)(2,1)S(1)} %bitcast.2), custom_call_target="tpu_custom_call" | custom-call | bytes 15000000 | tf_op jit(solution)/shard_map/pallas_call | solution.py:659
  1.4 3.1 %collective-permute-start = (bf16[288,128]{1,0:T(8,128)(2,1)S(1)}, bf16[288,128]{1,0:T(8,128)(2,1)S(1)}, u32[]{:S(2)}, u32[]{:S(2)}) collective-permute-start(bf16[288,128]{1,0:T(8,128)(2,1)S(1)} %get-tuple-element.39), channel_id=1, source_target_pairs={{0,4},{4,0},{8,12},{12,8},{1,5},{5,1},{9,13},{13,9},{2,6},{6,2},{1... | collective-permute-start | bytes 221192 | tf_op jit(solution)/shard_map/ppermute | solution.py:617
  4.5 0.7 %collective-permute-start.4 = (bf16[256,128]{1,0:T(8,128)(2,1)S(1)}, bf16[256,128]{1,0:T(8,128)(2,1)S(1)}, u32[]{:S(2)}, u32[]{:S(2)}) collective-permute-start(bf16[256,128]{1,0:T(8,128)(2,1)S(1)} %slice.22), channel_id=1, source_target_pairs={{8,4},{9,5},{10,6},{11,7},{24,20},{25,21},{26,22},{27,23}} | collective-permute-start | bytes 196616 | tf_op jit(solution)/shard_map/ppermute | solution.py:693
  5.1 0.1 collective-permute-start.2
  5.2 0.0 copy-start.2
  5.9 0.0 copy-done.2
  5.9 0.1 pad_add_fusion.offsets_in
  6.0 0.5 %shard_map.46 = (bf16[2,512,256]{2,1,0:T(8,128)(2,1)S(1)}, bf16[2,512,128]{2,1,0:T(8,128)(2,1)S(1)}, bf16[128,192]{1,0:T(8,128)(2,1)S(1)}, s32[2,2,8,128]{3,2,1,...) custom-call(s32[3]{0:T(128)S(1)} %pad_add_fusion.offsets_in), custom_call_target="tpu_custom_call" | custom-call | bytes 300000 | tf_op jit(solution)/shard_map/pallas_call | solution.py:672
  6.5 0.3 %collective-permute-done = bf16[288,128]{1,0:T(8,128)(2,1)S(1)} collective-permute-done((bf16[288,128]{1,0:T(8,128)(2,1)S(1)}, bf16[288,128]{1,0:T(8,128)(2,1)S(1)}, u32[]{:S(2)}, u32[]{:S(2)}) %collective-permute-start) | collective-permute-done | bytes 73760 | tf_op jit(solution)/shard_map/ppermute | solution.py:617
  6.8 0.3 %collective-permute-start.5 = (bf16[256,128]{1,0:T(8,128)(2,1)S(1)}, bf16[256,128]{1,0:T(8,128)(2,1)S(1)}, u32[]{:S(2)}, u32[]{:S(2)}) collective-permute-start(bf16[256,128]{1,0:T(8,128)(2,1)S(1)} %slice.27.refs_0_), channel_id=1, source_target_pairs={{0,1},{1,0},{2,3},{3,2},{4,5},{5,4},{6,7},{7,6},{8,9},{9,8},{10,11... | collective-permute-start | bytes 196616 | tf_op jit(solution)/shard_map/ppermute | solution.py:632
  7.1 3.2 %collective-permute-start.1 = (bf16[64,128]{1,0:T(8,128)(2,1)S(1)}, bf16[64,128]{1,0:T(8,128)(2,1)S(1)}, u32[]{:S(2)}, u32[]{:S(2)}) collective-permute-start(bf16[64,128]{1,0:T(8,128)(2,1)S(1)} %pad_maximum_fusion.2), channel_id=1, source_target_pairs={{0,8},{4,12},{8,0},{12,4},{1,9},{5,13},{9,1},{13,5},{2,10},{6,14},... | collective-permute-start | bytes 49160 | tf_op jit(solution)/shard_map/ppermute | solution.py:617
  10.3 0.0 collective-permute-done.4.refs_1_
  10.3 0.0 collective-permute-done.5.refs_2_
  10.3 0.0 collective-permute-start.7
  10.3 1.6 %collective-permute-start.6 = (bf16[64,640]{1,0:T(8,128)(2,1)S(1)}, bf16[64,640]{1,0:T(8,128)(2,1)S(1)}, u32[]{:S(2)}, u32[]{:S(2)}) collective-permute-start(bf16[64,640]{1,0:T(8,128)(2,1)S(1)} %pad_maximum_fusion), channel_id=1, source_target_pairs={{0,2},{2,0},{1,3},{3,1},{4,6},{6,4},{5,7},{7,5},{8,10},{10,8},{9,1... | collective-permute-start | bytes 245768 | tf_op jit(solution)/shard_map/ppermute | solution.py:625
  11.9 0.0 collective-permute-done.2.other_ref
  11.9 1.4 %shard_map.48 = (f32[14,64,256]{2,1,0:T(8,128)S(1)}, bf16[2,2,128,256]{3,2,1,0:T(8,128)(2,1)S(1)}) custom-call(bf16[2,512,256]{2,1,0:T(8,128)(2,1)S(1)} %get-tuple-element.40.weights, bf16[128,192]{1,0:T(8,128)(2,1)S(1)} %get-tuple-element.41.left_rows_ref, bf16[512,512]{1,0:T(8,128)(2,1)S(1)} %get-tuple-element.42.own_ref, ...), custom_call_target="tpu_custom_call" | custom-call | bytes 300000 | tf_op jit(solution)/shard_map/pallas_call | solution.py:708
  13.3 0.0 collective-permute-done.1
  13.3 0.3 %collective-permute-start.3 = (bf16[128,128]{1,0:T(8,128)(2,1)S(1)}, bf16[128,128]{1,0:T(8,128)(2,1)S(1)}, u32[]{:S(2)}, u32[]{:S(2)}) collective-permute-start(bf16[128,128]{1,0:T(8,128)(2,1)S(1)} %pad_maximum_fusion.1.own_part_ref), channel_id=1, source_target_pairs={{0,1},{1,0},{2,3},{3,2},{4,5},{5,4},{6,7},{7,6},{8,9},{9,8},{10,11... | collective-permute-start | bytes 98312 | tf_op jit(solution)/shard_map/ppermute | solution.py:632
  13.6 0.0 collective-permute-done.7.refs_3_
  13.6 1.5 %shard_map.49 = (f32[14,64,256]{2,1,0:T(8,128)S(1)}, bf16[2,2,128,256]{3,2,1,0:T(8,128)(2,1)S(1)}) custom-call(bf16[2,512,256]{2,1,0:T(8,128)(2,1)S(1)} %get-tuple-element.40.weights, bf16[128,192]{1,0:T(8,128)(2,1)S(1)} %get-tuple-element.41.left_rows_ref, bf16[512,512]{1,0:T(8,128)(2,1)S(1)} %get-tuple-element.42.own_ref, ...), custom_call_target="tpu_custom_call" | custom-call | bytes 300000 | tf_op jit(solution)/shard_map/pallas_call | solution.py:708
  15.1 0.1 collective-permute-done.6.own_low_ref
  15.2 0.0 collective-permute-done.3.other_part_ref
  15.2 0.2 %collective-permute-start.8 = (bf16[64,640]{1,0:T(8,128)(2,1)S(1)}, bf16[64,640]{1,0:T(8,128)(2,1)S(1)}, u32[]{:S(2)}, u32[]{:S(2)}) collective-permute-start(bf16[64,640]{1,0:T(8,128)(2,1)S(1)} %collective-permute-done.6.own_low_ref), channel_id=1, source_target_pairs={{0,1},{1,0},{2,3},{3,2},{4,5},{5,4},{6,7},{7,6},{8,9},{9,8},{10,11... | collective-permute-start | bytes 245768 | tf_op jit(solution)/shard_map/ppermute | solution.py:632
  15.5 0.0 copy-start.1
  15.5 1.3 %shard_map.50 = (f32[2,2,4,32,128]{4,3,2,1,0:T(8,128)S(1)}, f32[2,8,16]{2,1,0:T(8,128)S(1)}) custom-call(bf16[64,256]{1,0:T(8,128)(2,1)S(1)} %get-tuple-element.35.forward_rows_ref, bf16[768,256]{1,0:T(8,128)(2,1)S(1)} %get-tuple-element.33.inverse_ref, bf16[64,256]{1,0:T(8,128)(2,1)S(1)} %get-tuple-element.34.inverse_rows_ref, ...), custom_call_target="tpu_custom_call" | custom-call | bytes 300000 | tf_op jit(solution)/shard_map/pallas_call | solution.py:730
  16.8 0.0 collective-permute-done.8.other_low_ref
  16.8 0.0 copy-done.1
  16.8 3.3 %shard_map.51 = f32[2,1,8,16]{3,2,1,0:T(8,128)} custom-call(bf16[768,256]{1,0:T(8,128)(2,1)S(1)} %get-tuple-element.33.inverse_ref, bf16[64,256]{1,0:T(8,128)(2,1)S(1)} %get-tuple-element.34.inverse_rows_ref, s32[16,16]{1,0:T(8,128)S(1)} %copy-done.1, f32[2,8,16]{2,1,0:T(8,128)S(1)} %get-tuple-element.54.base_ref, ...), custom_call_target="tpu_custom_call" | custom-call | bytes 300000 | tf_op jit(solution)/shard_map/pallas_call | solution.py:752
  (8 shorter events, 0.0 us)
Async XLA Ops:
  0.0 1.0 %copy-start = (bf16[1,512,512]{2,1,0:T(8,128)(2,1)S(1)}, bf16[1,512,512]{2,1,0:T(8,128)(2,1)}, u32[]{:S(2)}) copy-start(bf16[1,512,512]{2,1,0:T(8,128)(2,1)} %param.4) | copy-start | bytes 1572868
  1.4 5.4 %collective-permute-start = (bf16[288,128]{1,0:T(8,128)(2,1)S(1)}, bf16[288,128]{1,0:T(8,128)(2,1)S(1)}, u32[]{:S(2)}, u32[]{:S(2)}) collective-permute-start(bf16[288,128]{1,0:T(8,128)(2,1)S(1)} %get-tuple-element.39), channel_id=1, source_target_pairs={{0,4},{4,0},{8,12},{12,8},{1,5},{5,1},{9,13},{13,9},{2,6},{6,2},{1... | collective-permute-start | bytes 221192 | tf_op jit(solution)/shard_map/ppermute | solution.py:617
  4.5 5.8 %collective-permute-start.4 = (bf16[256,128]{1,0:T(8,128)(2,1)S(1)}, bf16[256,128]{1,0:T(8,128)(2,1)S(1)}, u32[]{:S(2)}, u32[]{:S(2)}) collective-permute-start(bf16[256,128]{1,0:T(8,128)(2,1)S(1)} %slice.22), channel_id=1, source_target_pairs={{8,4},{9,5},{10,6},{11,7},{24,20},{25,21},{26,22},{27,23}} | collective-permute-start | bytes 196616 | tf_op jit(solution)/shard_map/ppermute | solution.py:693
  5.1 6.8 %collective-permute-start.2 = (bf16[512,512]{1,0:T(8,128)(2,1)S(1)}, bf16[512,512]{1,0:T(8,128)(2,1)S(1)}, u32[]{:S(2)}, u32[]{:S(2)}) collective-permute-start(bf16[512,512]{1,0:T(8,128)(2,1)S(1)} %get-tuple-element.42.own_ref), channel_id=1, source_target_pairs={{0,1},{1,0},{2,3},{3,2},{4,5},{5,4},{6,7},{7,6},{8,9},{9,8},{10,11... | collective-permute-start | bytes 1572872 | tf_op jit(solution)/shard_map/ppermute | solution.py:632
  5.2 0.7 %copy-start.2 = (s32[2]{0:T(128)S(1)}, s32[2]{0:T(128)}, u32[]{:S(2)}) copy-start(s32[2]{0:T(128)} %param.5) | copy-start | bytes 28
  6.8 3.5 %collective-permute-start.5 = (bf16[256,128]{1,0:T(8,128)(2,1)S(1)}, bf16[256,128]{1,0:T(8,128)(2,1)S(1)}, u32[]{:S(2)}, u32[]{:S(2)}) collective-permute-start(bf16[256,128]{1,0:T(8,128)(2,1)S(1)} %slice.27.refs_0_), channel_id=1, source_target_pairs={{0,1},{1,0},{2,3},{3,2},{4,5},{5,4},{6,7},{7,6},{8,9},{9,8},{10,11... | collective-permute-start | bytes 196616 | tf_op jit(solution)/shard_map/ppermute | solution.py:632
  7.1 6.2 %collective-permute-start.1 = (bf16[64,128]{1,0:T(8,128)(2,1)S(1)}, bf16[64,128]{1,0:T(8,128)(2,1)S(1)}, u32[]{:S(2)}, u32[]{:S(2)}) collective-permute-start(bf16[64,128]{1,0:T(8,128)(2,1)S(1)} %pad_maximum_fusion.2), channel_id=1, source_target_pairs={{0,8},{4,12},{8,0},{12,4},{1,9},{5,13},{9,1},{13,5},{2,10},{6,14},... | collective-permute-start | bytes 49160 | tf_op jit(solution)/shard_map/ppermute | solution.py:617
  10.3 3.3 %collective-permute-start.7 = (bf16[256,128]{1,0:T(8,128)(2,1)S(1)}, bf16[256,128]{1,0:T(8,128)(2,1)S(1)}, u32[]{:S(2)}, u32[]{:S(2)}) collective-permute-start(bf16[256,128]{1,0:T(8,128)(2,1)S(1)} %collective-permute-done.4.refs_1_), channel_id=1, source_target_pairs={{0,1},{1,0},{2,3},{3,2},{4,5},{5,4},{6,7},{7,6},{8,9},{9,8},{10,11... | collective-permute-start | bytes 196616 | tf_op jit(solution)/shard_map/ppermute | solution.py:632
  10.3 4.9 %collective-permute-start.6 = (bf16[64,640]{1,0:T(8,128)(2,1)S(1)}, bf16[64,640]{1,0:T(8,128)(2,1)S(1)}, u32[]{:S(2)}, u32[]{:S(2)}) collective-permute-start(bf16[64,640]{1,0:T(8,128)(2,1)S(1)} %pad_maximum_fusion), channel_id=1, source_target_pairs={{0,2},{2,0},{1,3},{3,1},{4,6},{6,4},{5,7},{7,5},{8,10},{10,8},{9,1... | collective-permute-start | bytes 245768 | tf_op jit(solution)/shard_map/ppermute | solution.py:625
  13.3 1.9 %collective-permute-start.3 = (bf16[128,128]{1,0:T(8,128)(2,1)S(1)}, bf16[128,128]{1,0:T(8,128)(2,1)S(1)}, u32[]{:S(2)}, u32[]{:S(2)}) collective-permute-start(bf16[128,128]{1,0:T(8,128)(2,1)S(1)} %pad_maximum_fusion.1.own_part_ref), channel_id=1, source_target_pairs={{0,1},{1,0},{2,3},{3,2},{4,5},{5,4},{6,7},{7,6},{8,9},{9,8},{10,11... | collective-permute-start | bytes 98312 | tf_op jit(solution)/shard_map/ppermute | solution.py:632
  15.2 1.5 %collective-permute-start.8 = (bf16[64,640]{1,0:T(8,128)(2,1)S(1)}, bf16[64,640]{1,0:T(8,128)(2,1)S(1)}, u32[]{:S(2)}, u32[]{:S(2)}) collective-permute-start(bf16[64,640]{1,0:T(8,128)(2,1)S(1)} %collective-permute-done.6.own_low_ref), channel_id=1, source_target_pairs={{0,1},{1,0},{2,3},{3,2},{4,5},{5,4},{6,7},{7,6},{8,9},{9,8},{10,11... | collective-permute-start | bytes 245768 | tf_op jit(solution)/shard_map/ppermute | solution.py:632
  15.5 1.3 %copy-start.1 = (s32[16,16]{1,0:T(8,128)S(1)}, s32[16,16]{1,0:T(8,128)}, u32[]{:S(2)}) copy-start(s32[16,16]{1,0:T(8,128)} %mask_ref.1) | copy-start | bytes 3076

commit v10 on v8

--- a/solution.py
+++ b/solution.py
@@ -322,11 +322,10 @@
     return jnp.where(left, a, b), pltpu.roll(jnp.where(left, b, a), P_SIZE, axis=1)
 
 
-def forward_columns(image, stacked, weights, first_block=0):
-    blocks = image.shape[1] // STRIDE
+def forward_columns(strips, stacked, weights, first_block=0):
+    blocks = strips[0].shape[0] // STRIDE
     supers = stacked.shape[3] // (2 * LANES)
     places = [(s, g) for s in range(2) for g in range(supers)]
-    strips = [image[s, :, g * 2 * LANES : (2 * g + 3) * LANES] for s, g in places]
     for (s, g), (a, b) in zip(places, column_transform(strips, weights)):
         lane = g * 2 * LANES
         for t in range(2):
@@ -369,31 +368,29 @@
 
 
 def upper_kernel(group, weights, left_rows_ref, own_ref, other_ref, *refs):
-    rights, (out_ref, tail_ref, image, stacked) = refs[:-4], refs[-4:]
+    rights, (out_ref, tail_ref, stacked) = refs[:-3], refs[-3:]
     lane = group * 2 * LANES
     wide = 2 * LANES if rights else 3 * LANES
+    inside = 1.0 - is_last("gx").astype(f32)
+    strips = []
     for s, main in enumerate((own_ref, other_ref)):
-        image[s, :, :wide] = main[:, lane : lane + wide]
+        strip = main[:, lane : lane + wide]
         if rights:
-            image[s, :, wide:] = unpack(from_right(rights[2 * s : 2 * s + 2], slice(None)))
-    if rights:
-
-        @pl.when(is_last("gx"))
-        def _():
-            image[:, :, wide:] = jnp.zeros((2, image.shape[1], LANES), bf16)
-
-    forward_columns(image, stacked, weights)
+            halo = unpack(from_right(rights[2 * s : 2 * s + 2], slice(None)) * inside)
+            strip = jnp.concatenate([strip, halo], axis=1)
+        strips.append(strip)
+    forward_columns(strips, stacked, weights)
     tail_ref[...] = stacked[:, :, stacked.shape[2] - 2 * P_SIZE :]
     forward_rows(stacked, left_rows_ref[...], 0, out_ref)
 
 
-def lower_image(own_low_ref, other_low_ref, image):
+def lower_strips(own_low_ref, other_low_ref, supers):
     shape = own_low_ref.shape
     inside = 1.0 - is_last("gx").astype(f32)
     above = 1.0 - is_last("gy").astype(f32)
     keep = jnp.where(iota(shape, 1) < shape[1] - LANES, above, above * inside)
-    for s, low in enumerate((own_low_ref, other_low_ref)):
-        image[s] = (low[...].astype(f32) * keep).astype(bf16)
+    rows = [(low[...].astype(f32) * keep).astype(bf16) for low in (own_low_ref, other_low_ref)]
+    return [x[:, g * 2 * LANES : (2 * g + 3) * LANES] for x in rows for g in range(supers)]
 
 
 def inverse_columns(high, low, table_ref):
@@ -544,7 +541,7 @@
     other_low_ref,
     *refs,
 ):
-    out_ref, image, stacked, lower_ref, high_ref, low_ref = refs[-6:]
+    out_ref, stacked, lower_ref, high_ref, low_ref = refs[-5:]
     supers = turns.shape[1]
     tails, spectra = refs[:supers], refs[supers : 2 * supers]
     per_row = supers * GROUP
@@ -574,10 +571,10 @@
                 high_ref[at, lanes] = high
                 low_ref[at, lanes] = low
 
-    lower_image(own_low_ref, other_low_ref, image)
+    strips = lower_strips(own_low_ref, other_low_ref, supers)
     for g in range(supers):
         stacked[:, :, : 2 * P_SIZE, g * 2 * LANES : (g + 1) * 2 * LANES] = tails[g][...]
-    forward_columns(image, stacked, weights, P_SIZE // STRIDE)
+    forward_columns(strips, stacked, weights, P_SIZE // STRIDE)
     for i in range(upper_bands // 2):
         turn_band(i)
     forward_rows(stacked, left_rows_ref[...], upper_bands, lower_ref)
@@ -712,7 +709,6 @@
             in_specs=[VMEM] * (4 + len(operands)),
             out_specs=(VMEM,) * 2,
             scratch_shapes=[
-                pltpu.VMEM((2, rows, 3 * LANES), bf16),
                 pltpu.VMEM((2, 2, 2 * rows, 2 * LANES), bf16),
             ],
             compiler_params=params(32),
@@ -753,7 +749,6 @@
         in_specs=[VMEM] * (9 + 2 * supers),
         out_specs=VMEM,
         scratch_shapes=[
-            pltpu.VMEM((2, P_SIZE, width + LANES), bf16),
             pltpu.VMEM((2, 2, 4 * P_SIZE, wide), bf16),
             pltpu.VMEM((low_bands, P_SIZE, wide), f32),
             pltpu.VMEM((bands * P_SIZE, wide), bf16),

time: 20.2 us -> 20.1 us (level)
  no operation moved by 1% of the time
where the time goes in v10:
time: 20.1 us; the launch traced here: 19.9 us
  starting transfers between devices  9.26 us (46%)
  Pallas kernels  8.13 us (40%)
  local copies, waits for them, and re-layouts  1.07 us (5%)
  between operations  0.81 us (4%)
  waiting for transfers between devices  0.56 us (3%)
    ppermute x2, starting transfers between devices, exchanged(): lax.ppermute(value, axis, [(i, i ^ step) for i in range(lax.axis_size(axi...  6.31 us
    pallas_call x1, Pallas kernels, local(): pl.pallas_call(peak_kernel, out_shape=jax.ShapeDtypeStruct((2, 1, per_row...  3.29 us
    pallas_call x2, Pallas kernels, upper(): pl.pallas_call(functools.partial(upper_kernel, group), out_shape=(jax.Sha...  2.76 us
    ppermute x1, starting transfers between devices, from_next(): got.append(lax.ppermute(value, axis, pairs + [(j, i) for i, j in pairs]))  1.56 us
    pallas_call x1, Pallas kernels, local(): pl.pallas_call(turn_kernel, out_shape=(jax.ShapeDtypeStruct((2, supers, 4...  1.26 us
    unnamed x6, local copies, waits for them, and re-layouts  1.05 us
    ppermute x5, starting transfers between devices, swapped(): return lax.ppermute(value, 'gz', [(0, 1), (1, 0)])  0.74 us
    ppermute x1, starting transfers between devices, local(): lax.ppermute(packed[HALF:], 'gx', [(i + 1, i) for i in range(1, count - 1...  0.65 us
  transfers between devices with their start and end apart: 9, of which 2 were waited for; matrix products, arithmetic and copies ran while one was open for 1% of the time, Pallas kernels for 23%

profile of v10, /device:TPU:0, one launch (start us, length us, event | category | flops | bytes accessed | tf_op | source)
XLA Modules:
  0.0 19.9 jit_solution(1971653136112556672)
XLA Ops:
  0.0 0.0 copy-start
  0.0 1.0 %copy-done = bf16[1,512,512]{2,1,0:T(8,128)(2,1)S(1)} copy-done((bf16[1,512,512]{2,1,0:T(8,128)(2,1)S(1)}, bf16[1,512,512]{2,1,0:T(8,128)(2,1)}, u32[]{:S(2)}) %copy-start) | copy-done | bytes 524312
  1.0 0.3 %shard_map.47 = (bf16[512,512]{1,0:T(8,128)(2,1)S(1)}, bf16[64,512]{1,0:T(8,128)(2,1)S(1)}, bf16[288,128]{1,0:T(8,128)(2,1)S(1)}) custom-call(bf16[512,512]{1,0:T(8,128)(2,1)S(1)} %bitcast.2), custom_call_target="tpu_custom_call" | custom-call | bytes 15000000 | tf_op jit(solution)/shard_map/pallas_call | solution.py:654
  1.4 3.1 %collective-permute-start = (bf16[288,128]{1,0:T(8,128)(2,1)S(1)}, bf16[288,128]{1,0:T(8,128)(2,1)S(1)}, u32[]{:S(2)}, u32[]{:S(2)}) collective-permute-start(bf16[288,128]{1,0:T(8,128)(2,1)S(1)} %get-tuple-element.39), channel_id=1, source_target_pairs={{0,4},{4,0},{8,12},{12,8},{1,5},{5,1},{9,13},{13,9},{2,6},{6,2},{1... | collective-permute-start | bytes 221192 | tf_op jit(solution)/shard_map/ppermute | solution.py:612
  4.5 0.7 %collective-permute-start.4 = (bf16[256,128]{1,0:T(8,128)(2,1)S(1)}, bf16[256,128]{1,0:T(8,128)(2,1)S(1)}, u32[]{:S(2)}, u32[]{:S(2)}) collective-permute-start(bf16[256,128]{1,0:T(8,128)(2,1)S(1)} %slice.22), channel_id=1, source_target_pairs={{8,4},{9,5},{10,6},{11,7},{24,20},{25,21},{26,22},{27,23}} | collective-permute-start | bytes 196616 | tf_op jit(solution)/shard_map/ppermute | solution.py:688
  5.1 0.1 collective-permute-start.2
  5.2 0.0 copy-start.2
  5.9 0.0 copy-done.2
  5.9 0.1 pad_add_fusion.offsets_in
  6.0 0.5 %shard_map.46 = (bf16[2,512,256]{2,1,0:T(8,128)(2,1)S(1)}, bf16[2,512,128]{2,1,0:T(8,128)(2,1)S(1)}, bf16[128,192]{1,0:T(8,128)(2,1)S(1)}, s32[2,2,8,128]{3,2,1,...) custom-call(s32[3]{0:T(128)S(1)} %pad_add_fusion.offsets_in), custom_call_target="tpu_custom_call" | custom-call | bytes 300000 | tf_op jit(solution)/shard_map/pallas_call | solution.py:667
  6.5 0.3 %collective-permute-done = bf16[288,128]{1,0:T(8,128)(2,1)S(1)} collective-permute-done((bf16[288,128]{1,0:T(8,128)(2,1)S(1)}, bf16[288,128]{1,0:T(8,128)(2,1)S(1)}, u32[]{:S(2)}, u32[]{:S(2)}) %collective-permute-start) | collective-permute-done | bytes 73760 | tf_op jit(solution)/shard_map/ppermute | solution.py:612
  6.8 0.3 %collective-permute-start.5 = (bf16[256,128]{1,0:T(8,128)(2,1)S(1)}, bf16[256,128]{1,0:T(8,128)(2,1)S(1)}, u32[]{:S(2)}, u32[]{:S(2)}) collective-permute-start(bf16[256,128]{1,0:T(8,128)(2,1)S(1)} %slice.27.refs_0_), channel_id=1, source_target_pairs={{0,1},{1,0},{2,3},{3,2},{4,5},{5,4},{6,7},{7,6},{8,9},{9,8},{10,11... | collective-permute-start | bytes 196616 | tf_op jit(solution)/shard_map/ppermute | solution.py:627
  7.1 3.2 %collective-permute-start.1 = (bf16[64,128]{1,0:T(8,128)(2,1)S(1)}, bf16[64,128]{1,0:T(8,128)(2,1)S(1)}, u32[]{:S(2)}, u32[]{:S(2)}) collective-permute-start(bf16[64,128]{1,0:T(8,128)(2,1)S(1)} %pad_maximum_fusion.2), channel_id=1, source_target_pairs={{0,8},{4,12},{8,0},{12,4},{1,9},{5,13},{9,1},{13,5},{2,10},{6,14},... | collective-permute-start | bytes 49160 | tf_op jit(solution)/shard_map/ppermute | solution.py:612
  10.3 0.0 collective-permute-done.4.refs_1_
  10.3 0.0 collective-permute-done.5.refs_2_
  10.3 0.0 collective-permute-start.7
  10.3 1.6 %collective-permute-start.6 = (bf16[64,640]{1,0:T(8,128)(2,1)S(1)}, bf16[64,640]{1,0:T(8,128)(2,1)S(1)}, u32[]{:S(2)}, u32[]{:S(2)}) collective-permute-start(bf16[64,640]{1,0:T(8,128)(2,1)S(1)} %pad_maximum_fusion), channel_id=1, source_target_pairs={{0,2},{2,0},{1,3},{3,1},{4,6},{6,4},{5,7},{7,5},{8,10},{10,8},{9,1... | collective-permute-start | bytes 245768 | tf_op jit(solution)/shard_map/ppermute | solution.py:620
  11.9 0.0 collective-permute-done.2.other_ref
  11.9 1.4 %shard_map.48 = (f32[14,64,256]{2,1,0:T(8,128)S(1)}, bf16[2,2,128,256]{3,2,1,0:T(8,128)(2,1)S(1)}) custom-call(bf16[2,512,256]{2,1,0:T(8,128)(2,1)S(1)} %get-tuple-element.40.weights, bf16[128,192]{1,0:T(8,128)(2,1)S(1)} %get-tuple-element.41.left_rows_ref, bf16[512,512]{1,0:T(8,128)(2,1)S(1)} %get-tuple-element.42.own_ref, ...), custom_call_target="tpu_custom_call" | custom-call | bytes 300000 | tf_op jit(solution)/shard_map/pallas_call | solution.py:703
  13.3 0.0 collective-permute-done.1
  13.3 0.3 %collective-permute-start.3 = (bf16[128,128]{1,0:T(8,128)(2,1)S(1)}, bf16[128,128]{1,0:T(8,128)(2,1)S(1)}, u32[]{:S(2)}, u32[]{:S(2)}) collective-permute-start(bf16[128,128]{1,0:T(8,128)(2,1)S(1)} %pad_maximum_fusion.1.own_part_ref), channel_id=1, source_target_pairs={{0,1},{1,0},{2,3},{3,2},{4,5},{5,4},{6,7},{7,6},{8,9},{9,8},{10,11... | collective-permute-start | bytes 98312 | tf_op jit(solution)/shard_map/ppermute | solution.py:627
  13.6 0.0 collective-permute-done.7.refs_3_
  13.6 1.4 %shard_map.49 = (f32[14,64,256]{2,1,0:T(8,128)S(1)}, bf16[2,2,128,256]{3,2,1,0:T(8,128)(2,1)S(1)}) custom-call(bf16[2,512,256]{2,1,0:T(8,128)(2,1)S(1)} %get-tuple-element.40.weights, bf16[128,192]{1,0:T(8,128)(2,1)S(1)} %get-tuple-element.41.left_rows_ref, bf16[512,512]{1,0:T(8,128)(2,1)S(1)} %get-tuple-element.42.own_ref, ...), custom_call_target="tpu_custom_call" | custom-call | bytes 300000 | tf_op jit(solution)/shard_map/pallas_call | solution.py:703
  15.0 0.3 %collective-permute-done.6.own_low_ref = bf16[64,640]{1,0:T(8,128)(2,1)S(1)} collective-permute-done((bf16[64,640]{1,0:T(8,128)(2,1)S(1)}, bf16[64,640]{1,0:T(8,128)(2,1)S(1)}, u32[]{:S(2)}, u32[]{:S(2)}) %collective-permute-start.6) | collective-permute-done | bytes 81952 | tf_op jit(solution)/shard_map/ppermute | solution.py:620
  15.2 0.0 collective-permute-done.3.other_part_ref
  15.2 0.1 collective-permute-start.8
  15.3 0.0 copy-start.1
  15.4 1.3 %shard_map.50 = (f32[2,2,4,32,128]{4,3,2,1,0:T(8,128)S(1)}, f32[2,8,16]{2,1,0:T(8,128)S(1)}) custom-call(bf16[64,256]{1,0:T(8,128)(2,1)S(1)} %get-tuple-element.35.forward_rows_ref, bf16[768,256]{1,0:T(8,128)(2,1)S(1)} %get-tuple-element.33.inverse_ref, bf16[64,256]{1,0:T(8,128)(2,1)S(1)} %get-tuple-element.34.inverse_rows_ref, ...), custom_call_target="tpu_custom_call" | custom-call | bytes 300000 | tf_op jit(solution)/shard_map/pallas_call | solution.py:724
  16.6 0.0 collective-permute-done.8.other_low_ref
  16.6 0.0 copy-done.1
  16.6 3.3 %shard_map.51 = f32[2,1,8,16]{3,2,1,0:T(8,128)} custom-call(bf16[768,256]{1,0:T(8,128)(2,1)S(1)} %get-tuple-element.33.inverse_ref, bf16[64,256]{1,0:T(8,128)(2,1)S(1)} %get-tuple-element.34.inverse_rows_ref, s32[16,16]{1,0:T(8,128)S(1)} %copy-done.1, f32[2,8,16]{2,1,0:T(8,128)S(1)} %get-tuple-element.54.base_ref, ...), custom_call_target="tpu_custom_call" | custom-call | bytes 300000 | tf_op jit(solution)/shard_map/pallas_call | solution.py:746
  (8 shorter events, 0.0 us)
Async XLA Ops:
  0.0 1.0 %copy-start = (bf16[1,512,512]{2,1,0:T(8,128)(2,1)S(1)}, bf16[1,512,512]{2,1,0:T(8,128)(2,1)}, u32[]{:S(2)}) copy-start(bf16[1,512,512]{2,1,0:T(8,128)(2,1)} %param.4) | copy-start | bytes 1572868
  1.4 5.4 %collective-permute-start = (bf16[288,128]{1,0:T(8,128)(2,1)S(1)}, bf16[288,128]{1,0:T(8,128)(2,1)S(1)}, u32[]{:S(2)}, u32[]{:S(2)}) collective-permute-start(bf16[288,128]{1,0:T(8,128)(2,1)S(1)} %get-tuple-element.39), channel_id=1, source_target_pairs={{0,4},{4,0},{8,12},{12,8},{1,5},{5,1},{9,13},{13,9},{2,6},{6,2},{1... | collective-permute-start | bytes 221192 | tf_op jit(solution)/shard_map/ppermute | solution.py:612
  4.5 5.8 %collective-permute-start.4 = (bf16[256,128]{1,0:T(8,128)(2,1)S(1)}, bf16[256,128]{1,0:T(8,128)(2,1)S(1)}, u32[]{:S(2)}, u32[]{:S(2)}) collective-permute-start(bf16[256,128]{1,0:T(8,128)(2,1)S(1)} %slice.22), channel_id=1, source_target_pairs={{8,4},{9,5},{10,6},{11,7},{24,20},{25,21},{26,22},{27,23}} | collective-permute-start | bytes 196616 | tf_op jit(solution)/shard_map/ppermute | solution.py:688
  5.1 6.8 %collective-permute-start.2 = (bf16[512,512]{1,0:T(8,128)(2,1)S(1)}, bf16[512,512]{1,0:T(8,128)(2,1)S(1)}, u32[]{:S(2)}, u32[]{:S(2)}) collective-permute-start(bf16[512,512]{1,0:T(8,128)(2,1)S(1)} %get-tuple-element.42.own_ref), channel_id=1, source_target_pairs={{0,1},{1,0},{2,3},{3,2},{4,5},{5,4},{6,7},{7,6},{8,9},{9,8},{10,11... | collective-permute-start | bytes 1572872 | tf_op jit(solution)/shard_map/ppermute | solution.py:627
  5.2 0.7 %copy-start.2 = (s32[2]{0:T(128)S(1)}, s32[2]{0:T(128)}, u32[]{:S(2)}) copy-start(s32[2]{0:T(128)} %param.5) | copy-start | bytes 28
  6.8 3.5 %collective-permute-start.5 = (bf16[256,128]{1,0:T(8,128)(2,1)S(1)}, bf16[256,128]{1,0:T(8,128)(2,1)S(1)}, u32[]{:S(2)}, u32[]{:S(2)}) collective-permute-start(bf16[256,128]{1,0:T(8,128)(2,1)S(1)} %slice.27.refs_0_), channel_id=1, source_target_pairs={{0,1},{1,0},{2,3},{3,2},{4,5},{5,4},{6,7},{7,6},{8,9},{9,8},{10,11... | collective-permute-start | bytes 196616 | tf_op jit(solution)/shard_map/ppermute | solution.py:627
  7.1 6.2 %collective-permute-start.1 = (bf16[64,128]{1,0:T(8,128)(2,1)S(1)}, bf16[64,128]{1,0:T(8,128)(2,1)S(1)}, u32[]{:S(2)}, u32[]{:S(2)}) collective-permute-start(bf16[64,128]{1,0:T(8,128)(2,1)S(1)} %pad_maximum_fusion.2), channel_id=1, source_target_pairs={{0,8},{4,12},{8,0},{12,4},{1,9},{5,13},{9,1},{13,5},{2,10},{6,14},... | collective-permute-start | bytes 49160 | tf_op jit(solution)/shard_map/ppermute | solution.py:612
  10.3 3.3 %collective-permute-start.7 = (bf16[256,128]{1,0:T(8,128)(2,1)S(1)}, bf16[256,128]{1,0:T(8,128)(2,1)S(1)}, u32[]{:S(2)}, u32[]{:S(2)}) collective-permute-start(bf16[256,128]{1,0:T(8,128)(2,1)S(1)} %collective-permute-done.4.refs_1_), channel_id=1, source_target_pairs={{0,1},{1,0},{2,3},{3,2},{4,5},{5,4},{6,7},{7,6},{8,9},{9,8},{10,11... | collective-permute-start | bytes 196616 | tf_op jit(solution)/shard_map/ppermute | solution.py:627
  10.3 4.9 %collective-permute-start.6 = (bf16[64,640]{1,0:T(8,128)(2,1)S(1)}, bf16[64,640]{1,0:T(8,128)(2,1)S(1)}, u32[]{:S(2)}, u32[]{:S(2)}) collective-permute-start(bf16[64,640]{1,0:T(8,128)(2,1)S(1)} %pad_maximum_fusion), channel_id=1, source_target_pairs={{0,2},{2,0},{1,3},{3,1},{4,6},{6,4},{5,7},{7,5},{8,10},{10,8},{9,1... | collective-permute-start | bytes 245768 | tf_op jit(solution)/shard_map/ppermute | solution.py:620
  13.3 1.9 %collective-permute-start.3 = (bf16[128,128]{1,0:T(8,128)(2,1)S(1)}, bf16[128,128]{1,0:T(8,128)(2,1)S(1)}, u32[]{:S(2)}, u32[]{:S(2)}) collective-permute-start(bf16[128,128]{1,0:T(8,128)(2,1)S(1)} %pad_maximum_fusion.1.own_part_ref), channel_id=1, source_target_pairs={{0,1},{1,0},{2,3},{3,2},{4,5},{5,4},{6,7},{7,6},{8,9},{9,8},{10,11... | collective-permute-start | bytes 98312 | tf_op jit(solution)/shard_map/ppermute | solution.py:627
  15.2 1.4 %collective-permute-start.8 = (bf16[64,640]{1,0:T(8,128)(2,1)S(1)}, bf16[64,640]{1,0:T(8,128)(2,1)S(1)}, u32[]{:S(2)}, u32[]{:S(2)}) collective-permute-start(bf16[64,640]{1,0:T(8,128)(2,1)S(1)} %collective-permute-done.6.own_low_ref), channel_id=1, source_target_pairs={{0,1},{1,0},{2,3},{3,2},{4,5},{5,4},{6,7},{7,6},{8,9},{9,8},{10,11... | collective-permute-start | bytes 245768 | tf_op jit(solution)/shard_map/ppermute | solution.py:627
  15.3 1.3 %copy-start.1 = (s32[16,16]{1,0:T(8,128)S(1)}, s32[16,16]{1,0:T(8,128)}, u32[]{:S(2)}) copy-start(s32[16,16]{1,0:T(8,128)} %mask_ref.1) | copy-start | bytes 3076
